TPU v7x, 128 devices: a whole 4x4x4 slice. The times are simulated.
128 devices in a mesh: shot: 16 (over y, x), rcv: 8 (over z, core).
Axes of the slice: x: 4, y: 4, z: 4, core: 2. Of those that a mesh axis runs over, the one named last changes fastest.
Arguments:
- traces: bfloat16 [81920, 1024], P(('shot', 'rcv')), may hold values from -216 to 216
- src_index: int32 [81920], P(('shot', 'rcv')), may hold values from 0 to 2047, as said below
- rcv_index: int32 [81920], P(('shot', 'rcv')), may hold values from 0 to 2047, as said below
- off_index: int32 [81920], P(('shot', 'rcv')), may hold values from 0 to 127
- send_rows: int32 [128, 16, 80], P(('shot', 'rcv')), may hold values from 0 to 639, as said below
- send_counts: int32 [128, 16], P(('shot', 'rcv')), may hold values from 0 to 80, as said below
- recv_bins: int32 [128, 16, 80], P(('shot', 'rcv')), may hold values from 0 to 31
Outputs:
- source_terms: float32 [2048, 512], P('shot')
- receiver_terms: float32 [8, 256, 512], P('rcv', 'shot')
- offset_terms: float32 [128, 512], replicated
- cmp_terms: float32 [512, 512], P('shot')
Inputs may be any that keep to these rules, and one draw needn't show every extreme that they name: `send_counts`: each device's 16 counts add up to 640; in every draw every device of some rcv index has 80 toward one shot index. `send_rows`: for each device and shot index, the first send_counts entries are rows of that device's traces; over all shot indices they name each of its 640 rows exactly once; later entries are arbitrary rows. `src_index`: A trace's source lies in the block of 128 sources of its device's shot index. `rcv_index`: A trace's receiver lies in the block of 256 receivers of its device's rcv index.
All inputs are finite; a program needn't handle non-finite values.
Results may differ from a plain program's by a relative error of at most 0.0017.
Values sent between devices are 32-bit elements; how exact they have to be, the bound alone decides.
No kernel may reach another device: no remote copies, remote signals or barrier semaphores. Data moves between devices by JAX's collectives and lax.ppermute only.
A program may use at most 64 MiB of HBM per device.

v0:
```python
import jax
import jax.numpy as jnp
from jax import lax
from jax.sharding import PartitionSpec as P

SRC_DEV = 16
RCV_DEV = 16
CMP_DEV = 4
OFFSETS = 128
ITERS = 2


def fourier_basis(samples, freq_count):
    sample_ids = jnp.arange(samples, dtype=jnp.int32)[:, None]
    freq_ids = jnp.arange(freq_count, dtype=jnp.int32)[None, :]
    angle = (sample_ids * freq_ids % samples).astype(jnp.float32) * (2.0 * jnp.pi / samples)
    factor = 1.0 / jnp.sqrt(jnp.float32(samples))
    return jnp.concatenate([jnp.cos(angle) * factor, jnp.sin(angle) * factor], axis=1).astype(
        jnp.bfloat16
    )


def gather_rows(table, one_hot):
    return lax.dot_general(
        one_hot,
        table,
        (((0,), (0,)), ((), ())),
        precision=lax.Precision.HIGHEST,
        preferred_element_type=jnp.float32,
    )


def sum_rows(one_hot, values):
    return jnp.dot(
        one_hot, values, precision=lax.Precision.HIGHEST, preferred_element_type=jnp.float32
    )


def per_device(traces, src_index, rcv_index, off_index, send_rows, send_counts, recv_bins):
    n_shot = lax.axis_size("shot")
    n_rcv = lax.axis_size("rcv")
    shot_pos = lax.axis_index("shot")
    rcv_pos = lax.axis_index("rcv")
    tr_count, samples = traces.shape
    freq_count = samples // 2
    capacity = send_rows.shape[2]
    src_group = SRC_DEV * n_rcv
    rcv_group = RCV_DEV * n_shot
    cmp_group = CMP_DEV * n_rcv
    fourier = fourier_basis(samples, freq_count)
    spectra = jnp.dot(traces, fourier, preferred_element_type=jnp.float32)
    real_part = spectra[:, :freq_count]
    imag_part = spectra[:, freq_count:]
    log_spectra = jnp.log1p(real_part * real_part + imag_part * imag_part)
    src_local = src_index - shot_pos * src_group
    rcv_local = rcv_index - rcv_pos * rcv_group
    src_hot = (jnp.arange(src_group, dtype=jnp.int32)[:, None] == src_local[None, :]).astype(
        jnp.float32
    )
    rcv_hot = (jnp.arange(rcv_group, dtype=jnp.int32)[:, None] == rcv_local[None, :]).astype(
        jnp.float32
    )
    off_hot = (jnp.arange(OFFSETS, dtype=jnp.int32)[:, None] == off_index[None, :]).astype(
        jnp.float32
    )
    owner_ids = jnp.arange(n_shot, dtype=jnp.int32)[:, None]
    slot_ids = jnp.arange(capacity, dtype=jnp.int32)[None, :]
    slot_live = slot_ids < send_counts[0][:, None]
    target = jnp.where(slot_live, send_rows[0], tr_count).reshape(-1)
    slot_of_trace = (
        jnp.zeros((tr_count,), jnp.int32)
        .at[target]
        .set((owner_ids * capacity + slot_ids).reshape(-1), mode="drop")
    )
    bins_hot = (
        jnp.arange(cmp_group, dtype=jnp.int32)[:, None] == recv_bins[0].reshape(-1)[None, :]
    ).astype(jnp.float32)

    def adjoint_apply(values):
        src_part = sum_rows(src_hot, values)
        rcv_part = sum_rows(rcv_hot, values).reshape(n_shot, RCV_DEV, freq_count)
        off_part = sum_rows(off_hot, values)
        picked = jnp.take(values, send_rows[0].reshape(-1), axis=0).reshape(
            n_shot, capacity, freq_count
        )
        outgoing = jnp.where(slot_live[:, :, None], picked, 0.0)
        arrived = lax.all_to_all(
            jnp.concatenate([outgoing, rcv_part], axis=1),
            "shot",
            split_axis=0,
            concat_axis=0,
            tiled=True,
        )
        rcv_shard = jnp.sum(arrived[:, capacity:, :], axis=0)[None]
        cmp_part = sum_rows(
            bins_hot, arrived[:, :capacity, :].reshape(n_shot * capacity, freq_count)
        )
        src_full, cmp_full = lax.psum((src_part, cmp_part), "rcv")
        off_full, squares = lax.psum((off_part, jnp.sum(values * values)), ("shot", "rcv"))
        return ((src_full, rcv_shard, off_full, cmp_full), squares)

    def table_norm(tables):
        source_tab, receiver_tab, offset_tab, cmp_tab = tables
        own_source = lax.dynamic_slice_in_dim(source_tab, rcv_pos * SRC_DEV, SRC_DEV, 0)
        own_cmp = lax.dynamic_slice_in_dim(cmp_tab, rcv_pos * CMP_DEV, CMP_DEV, 0)
        partial_sum = (
            jnp.sum(own_source * own_source)
            + jnp.sum(receiver_tab * receiver_tab)
            + jnp.sum(own_cmp * own_cmp)
        )
        shared = lax.psum(partial_sum, ("shot", "rcv"))
        return jnp.sqrt(shared + jnp.sum(offset_tab * offset_tab))

    raw_tables, squares = adjoint_apply(log_spectra)
    beta_val = jnp.sqrt(squares)
    left_vec = log_spectra / beta_val
    right_raw = jax.tree.map(lambda member: member / beta_val, raw_tables)
    alpha_val = table_norm(right_raw)
    right_vec = jax.tree.map(lambda member: member / alpha_val, right_raw)
    search = right_vec
    solution = jax.tree.map(jnp.zeros_like, right_vec)
    phibar = beta_val
    rhobar = alpha_val
    for iteration in range(ITERS):
        forward_source_tab, forward_receiver_tab, forward_offset_tab, forward_cmp_tab = right_vec
        answers = gather_rows(forward_cmp_tab, bins_hot).reshape(n_shot, capacity, freq_count)
        rcv_copies = jnp.broadcast_to(forward_receiver_tab, (n_shot, RCV_DEV, freq_count))
        returned = lax.all_to_all(
            jnp.concatenate([answers, rcv_copies], axis=1),
            "shot",
            split_axis=0,
            concat_axis=0,
            tiled=True,
        )
        rcv_whole = returned[:, capacity:, :].reshape(rcv_group, freq_count)
        cmp_rows = returned[:, :capacity, :].reshape(n_shot * capacity, freq_count)
        cmp_pred = jnp.take(cmp_rows, slot_of_trace, axis=0)
        result = gather_rows(forward_source_tab, src_hot) + gather_rows(rcv_whole, rcv_hot)
        result = result + gather_rows(forward_offset_tab, off_hot)
        left_raw = result + cmp_pred - alpha_val * left_vec
        raw_tables, squares = adjoint_apply(left_raw)
        beta_val = jnp.sqrt(squares)
        left_vec = left_raw / beta_val
        right_raw = jax.tree.map(
            lambda member, former: member / beta_val - beta_val * former, raw_tables, right_vec
        )
        alpha_val = table_norm(right_raw)
        right_vec = jax.tree.map(lambda member: member / alpha_val, right_raw)
        rho_val = jnp.sqrt(rhobar * rhobar + beta_val * beta_val)
        cosine = rhobar / rho_val
        sine_val = beta_val / rho_val
        theta_val = sine_val * alpha_val
        rhobar = -cosine * alpha_val
        phi_val = cosine * phibar
        phibar = sine_val * phibar
        solution = jax.tree.map(
            lambda member, former: member + phi_val / rho_val * former, solution, search
        )
        search = jax.tree.map(
            lambda member, former: member - theta_val / rho_val * former, right_vec, search
        )
    source_tab, receiver_tab, offset_tab, cmp_tab = solution
    return (source_tab, receiver_tab, offset_tab, cmp_tab)


def solution(mesh):
    return jax.shard_map(
        per_device,
        mesh=mesh,
        in_specs=(
            P(("shot", "rcv"), None),
            P(("shot", "rcv")),
            P(("shot", "rcv")),
            P(("shot", "rcv")),
            P(("shot", "rcv"), None, None),
            P(("shot", "rcv"), None),
            P(("shot", "rcv"), None, None),
        ),
        out_specs=(P("shot", None), P("rcv", "shot", None), P(), P("shot", None)),
        check_vma=False,
    )
```

profile of v0, /device:TPU:0, one launch (start us, length us, event | category | flops | bytes accessed | tf_op | source)
XLA Modules:
  0.0 963.6 jit_solution(3433758967169323455)
XLA Ops:
  7.2 8.6 multiply_convert_fusion
  20.7 4.4 gather_fusion
  25.1 2.0 broadcast_select_fusion.1
  27.4 2.1 pad_maximum_fusion
  29.5 7.3 all-to-all-start
  38.6 45.8 %all-to-all-done = f32[16,96,512]{2,1,0:T(8,128)} async-done(((f32[16,96,512]{2,1,0:T(8,128)}), f32[16,96,512]{2,1,0:T(8,128)}, u32[]{:S(2)}, u32[]{:S(2)}) %all-to-all-start) | async-done | bytes 3145760 | tf_op jit(solution)/shard_map/all_to_all | solution.py:87
  89.8 65.3 %psum.78 = f32[]{:T(128)} all-reduce(f32[]{:T(128)} %get-tuple-element.12), channel_id=1, replica_groups=mesh['shot'=16,'rcv'=8] {'shot','rcv'}, use_global_device_ids=true, to_apply=%region_2.3 | all-reduce | flops 1 | bytes 8 | tf_op jit(solution)/shard_map/psum | solution.py:99
  162.2 133.5 %all-reduce.7.cloned.1.call-done = f32[128,512]{1,0:T(8,128)} async-done(((f32[128,512]{1,0:T(8,128)}), f32[128,512]{1,0:T(8,128)}) %all-reduce.7.cloned.1.call-update) | async-done | bytes 262160 | tf_op jit(solution)/shard_map/psum | solution.py:99
  297.3 63.1 %psum.80 = f32[]{:T(128)} all-reduce(f32[]{:T(128)S(6)} %add.146), channel_id=1, replica_groups=mesh['shot'=16,'rcv'=8] {'shot','rcv'}, use_global_device_ids=true, to_apply=%region_8.10 | all-reduce | flops 1 | bytes 8 | tf_op jit(solution)/shard_map/psum | solution.py:111
  361.8 2.1 fusion.39
  363.9 2.1 pad_maximum_fusion.1
  366.0 4.6 all-to-all-start.1
  371.0 5.2 scatter_custom_fusion
  378.2 40.8 %all-to-all-done.1 = f32[16,96,512]{2,1,0:T(8,128)} async-done(((f32[16,96,512]{2,1,0:T(8,128)}), f32[16,96,512]{2,1,0:T(8,128)}, u32[]{:S(2)}, u32[]{:S(2)}) %all-to-all-start.1) | async-done | bytes 3145760 | tf_op jit(solution)/shard_map/all_to_all | solution.py:128
  419.1 2.1 slice.53
  421.2 3.0 gather_fusion.1
  424.2 2.9 copy.15
  433.1 4.4 gather_fusion.2
  440.6 2.1 pad_maximum_fusion.2
  442.7 4.5 all-to-all-start.2
  447.2 98.5 %psum.82 = f32[]{:T(128)} all-reduce(f32[]{:T(128)} %get-tuple-element.14), channel_id=1, replica_groups=mesh['shot'=16,'rcv'=8] {'shot','rcv'}, use_global_device_ids=true, to_apply=%region_13.16 | all-reduce | flops 1 | bytes 8 | tf_op jit(solution)/shard_map/psum | solution.py:99
  555.1 54.6 %all-reduce.11.cloned.1.call-done = (f32[128,512]{1,0:T(8,128)}, f32[32,512]{1,0:T(8,128)}) async-done(((f32[128,512]{1,0:T(8,128)}, f32[32,512]{1,0:T(8,128)}), (f32[128,512]{1,0:T(8,128)}, f32[32,512]{1,0:T(8,128)})) %all-reduce.11.cloned.1.call-update) | async-done | bytes 327696 | tf_op jit(solution)/shard_map/psum | solution.py:98
  614.8 141.2 %all-reduce.9.cloned.1.call-done = f32[128,512]{1,0:T(8,128)} async-done(((f32[128,512]{1,0:T(8,128)}), f32[128,512]{1,0:T(8,128)}) %all-reduce.9.cloned.1.call-update) | async-done | bytes 262160 | tf_op jit(solution)/shard_map/psum | solution.py:99
  755.9 2.4 multiply_reduce_fusion.2
  758.3 62.9 %psum.85 = f32[]{:T(128)} all-reduce(f32[]{:T(128)S(6)} %add.157), channel_id=1, replica_groups=mesh['shot'=16,'rcv'=8] {'shot','rcv'}, use_global_device_ids=true, to_apply=%region_20.23 | all-reduce | flops 1 | bytes 8 | tf_op jit(solution)/shard_map/psum | solution.py:111
  823.9 2.1 pad_maximum_fusion.3
  826.0 4.5 all-to-all-start.3
  832.6 46.3 %all-to-all-done.3 = f32[16,96,512]{2,1,0:T(8,128)} async-done(((f32[16,96,512]{2,1,0:T(8,128)}), f32[16,96,512]{2,1,0:T(8,128)}, u32[]{:S(2)}, u32[]{:S(2)}) %all-to-all-start.3) | async-done | bytes 3145760 | tf_op jit(solution)/shard_map/all_to_all | solution.py:128
  878.9 2.1 slice.57
  881.1 3.0 gather_fusion.3
  884.1 2.9 copy.20
  890.8 62.5 %psum.87 = f32[]{:T(128)} all-reduce(f32[]{:T(128)} %fusion.20), channel_id=1, replica_groups=mesh['shot'=16,'rcv'=8] {'shot','rcv'}, use_global_device_ids=true, to_apply=%region_24.27 | all-reduce | flops 1 | bytes 8 | tf_op jit(solution)/shard_map/psum | solution.py:99
  (128 shorter events, 51.0 us)
Async XLA Ops:
  7.2 8.8 copy-start
  7.2 8.6 copy-start.19
  19.0 69.2 %copy-start.2 = (f32[640,512]{0,1:T(8,128)}, f32[640,512]{0,1:T(8,128)S(1)}, u32[]{:S(2)}) copy-start(f32[640,512]{0,1:T(8,128)S(1)} %get-tuple-element.13) | copy-start | bytes 3932164
  29.5 7.4 copy-start.22
  29.5 7.4 copy-start.24
  29.5 54.9 %all-to-all-start = ((f32[16,96,512]{2,1,0:T(8,128)}), f32[16,96,512]{2,1,0:T(8,128)}, u32[]{:S(2)}, u32[]{:S(2)}) async-start(f32[16,96,512]{2,1,0:T(8,128)} %pad_maximum_fusion), calls=%async_computation | async-start | bytes 6291456 | tf_op jit(solution)/shard_map/all_to_all | solution.py:87
  36.8 120.7 %all-reduce.13.cloned.1.call-start = ((), (), s32[]{:S(2)}) async-start(), calls=%async_computation.7 | async-start | bytes 655360 | tf_op jit(solution)/shard_map/psum | solution.py:98
  88.1 207.6 %all-reduce.7.cloned.1.call-start = ((), (), s32[]{:S(2)}) async-start(), calls=%async_computation.4 | async-start | bytes 524288 | tf_op jit(solution)/shard_map/psum | solution.py:99
  366.0 10.3 %copy-start.8 = (f32[128,512]{1,0:T(8,128)S(1)}, f32[128,512]{1,0:T(8,128)}, u32[]{:S(2)}) copy-start(f32[128,512]{1,0:T(8,128)} %get-tuple-element.8) | copy-start | bytes 786436
  366.0 53.0 %all-to-all-start.1 = ((f32[16,96,512]{2,1,0:T(8,128)}), f32[16,96,512]{2,1,0:T(8,128)}, u32[]{:S(2)}, u32[]{:S(2)}) async-start(f32[16,96,512]{2,1,0:T(8,128)} %pad_maximum_fusion.1), calls=%async_computation.1 | async-start | bytes 6291456 | tf_op jit(solution)/shard_map/all_to_all | solution.py:128
  376.3 44.9 %copy-start.17 = (s32[1024]{0:T(1024)}, s32[1024]{0:T(1024)S(1)}, u32[]{:S(2)}) copy-start(s32[1024]{0:T(1024)S(1)} %pad_clamp_fusion.1) | copy-start | bytes 12292
  376.3 53.0 %copy-start.25 = (pred[640]{0:T(1024)(128)(4,1)}, pred[640]{0:T(1024)(128)(4,1)S(1)}, u32[]{:S(2)}) copy-start(pred[640]{0:T(1024)(128)(4,1)S(1)} %compare_and_fusion.1) | copy-start | bytes 1924
  424.2 4.1 copy-start.7
  427.1 2.2 copy-start.3
  427.1 2.2 copy-start.9
  427.1 2.2 copy-start.12
  431.0 120.8 %copy-start.4 = (f32[640,512]{0,1:T(8,128)}, f32[640,512]{0,1:T(8,128)S(1)}, u32[]{:S(2)}) copy-start(f32[640,512]{0,1:T(8,128)S(1)} %get-tuple-element.15) | copy-start | bytes 3932164
  442.7 105.3 %all-to-all-start.2 = ((f32[16,96,512]{2,1,0:T(8,128)}), f32[16,96,512]{2,1,0:T(8,128)}, u32[]{:S(2)}, u32[]{:S(2)}) async-start(f32[16,96,512]{2,1,0:T(8,128)} %pad_maximum_fusion.2), calls=%async_computation.2 | async-start | bytes 6291456 | tf_op jit(solution)/shard_map/all_to_all | solution.py:87
  447.2 162.6 %all-reduce.11.cloned.1.call-start = ((), (), s32[]{:S(2)}) async-start(), calls=%async_computation.6 | async-start | bytes 655360 | tf_op jit(solution)/shard_map/psum | solution.py:98
  551.6 61.0 %copy-start.14 = (f32[32,512]{1,0:T(8,128)S(1)}, f32[32,512]{1,0:T(8,128)}, u32[]{:S(2)}) copy-start(f32[32,512]{1,0:T(8,128)} %get-tuple-element.9) | copy-start | bytes 196612
  551.7 204.2 %all-reduce.9.cloned.1.call-start = ((), (), s32[]{:S(2)}) async-start(), calls=%async_computation.5 | async-start | bytes 524288 | tf_op jit(solution)/shard_map/psum | solution.py:99
  613.5 212.6 %copy-start.15 = (f32[32,512]{1,0:T(8,128)}, f32[32,512]{1,0:T(8,128)S(1)}, u32[]{:S(2)}) copy-start(f32[32,512]{1,0:T(8,128)S(1)} %multiply_subtract_fusion.2) | copy-start | bytes 196612
  826.0 52.9 %all-to-all-start.3 = ((f32[16,96,512]{2,1,0:T(8,128)}), f32[16,96,512]{2,1,0:T(8,128)}, u32[]{:S(2)}, u32[]{:S(2)}) async-start(f32[16,96,512]{2,1,0:T(8,128)} %pad_maximum_fusion.3), calls=%async_computation.3 | async-start | bytes 6291456 | tf_op jit(solution)/shard_map/all_to_all | solution.py:128
  832.6 48.4 %copy-start.18 = (s32[1024]{0:T(1024)S(1)}, s32[1024]{0:T(1024)}, u32[]{:S(2)}) copy-start(s32[1024]{0:T(1024)} %copy-done.17) | copy-start | bytes 12292
  884.1 4.2 copy-start.6
  887.0 2.2 copy-start.5
  887.0 2.2 copy-start.11
  887.0 2.2 copy-start.13
  887.0 2.2 copy-start.21
  887.0 2.2 copy-start.26
  889.2 66.4 %copy-start.16 = (f32[32,512]{1,0:T(8,128)S(1)}, f32[32,512]{1,0:T(8,128)}, u32[]{:S(2)}) copy-start(f32[32,512]{1,0:T(8,128)} %copy-done.15) | copy-start | bytes 196612
  889.3 67.8 %copy-start.1 = (bf16[640,1024]{1,0:T(8,128)(2,1)S(1)}, bf16[640,1024]{1,0:T(8,128)(2,1)}, u32[]{:S(2)}) copy-start(bf16[640,1024]{1,0:T(8,128)(2,1)} %param.11) | copy-start | bytes 3932164
  (4 other events, 5.2 us)
Sparse Core Ops, SparseCore 0:
  88.2 60.4 all-reduce.12
  154.8 140.8 all-reduce.6
  551.8 57.8 all-reduce.10
  614.9 140.9 all-reduce.8
where the time goes:
time: 966 us; the launch traced here: 964 us
  waiting for transfers between devices  462 us (48%)
  blocking collectives  352 us (36%)
  other arithmetic  39.2 us (4%)
  local copies, waits for them, and re-layouts  39 us (4%)
  matrix products  26.3 us (3%)
  between operations  23.3 us (2%)
  starting transfers between devices  21 us (2%)
    psum x2, waiting for transfers between devices, adjoint_apply(): lax.psum((off_part, jnp.sum(values * values)), ('shot', 'rcv'))  275 us
    psum x3, blocking collectives, adjoint_apply(): lax.psum((off_part, jnp.sum(values * values)), ('shot', 'rcv'))  226 us
    psum x2, blocking collectives, table_norm(): shared = lax.psum(partial_sum, ('shot', 'rcv'))  126 us
    all_to_all x2, waiting for transfers between devices, per_device(): lax.all_to_all(jnp.concatenate([answers, rcv_copies], axis=1), 'shot', sp...  87.2 us
    psum x2, waiting for transfers between devices, adjoint_apply(): src_full, cmp_full = lax.psum((src_part, cmp_part), 'rcv')  54.6 us
    all_to_all x2, waiting for transfers between devices, adjoint_apply(): lax.all_to_all(jnp.concatenate([outgoing, rcv_part], axis=1), 'shot', spl...  45.8 us
  transfers between devices with their start and end apart: 8, of which 6 were waited for; matrix products, arithmetic and copies ran while one was open for 3% of the time, Pallas kernels for 0%

commit v1 on v0

v1 whole, which is shorter than its diff:
```python
import functools

import ml_dtypes
import numpy as np

import jax
import jax.numpy as jnp
from jax import lax
from jax.experimental import pallas as pl
from jax.experimental.pallas import tpu as pltpu
from jax.sharding import PartitionSpec as P

SAMPLES = 1024
FREQS = 512
TR_DEV = 640
N_SHOT = 16
N_RCV = 8
DEVICES = 128
CAP = 80
SRC_G = 128
RCV_G = 256
CMP_G = 32
SLICE = FREQS // N_SHOT
LANES = 128
OFF_TILE = 16
CMP_TILE = 17
LIVE_TILES = 21
LIVE_ROWS = LIVE_TILES * SLICE
SHARE = -(-LIVE_ROWS // (8 * N_RCV)) * 8
TAB_ROWS = N_RCV * SHARE
RCV_TILES = 2
ROWS = SRC_G + RCV_G + 128 + 512
SHARED = ROWS - SRC_G
SO = 2 * LANES
SOR = SO + RCV_G
OR = LANES + RCV_G
HALF = N_SHOT // 2
COUNT_STEPS = HALF // 2
CHUNKS = 4
CHUNK_ROWS = N_SHOT * SRC_G // CHUNKS
TRACE_TILES = TR_DEV // LANES
BINS_AT = TRACE_TILES * SLICE
INDEX_AT = BINS_AT + N_SHOT
INDEX_ROWS = 24
DATA_ROWS = INDEX_AT + INDEX_ROWS
STEPS = 2
OWN_ROWS = 2 * SLICE + SLICE // 2
PACK = LANES // CMP_G

VMEM = pltpu.VMEM
F32 = jnp.float32
BF16 = jnp.bfloat16


def fourier_rows():
    phase = np.arange(FREQS)[:, None] * np.arange(SAMPLES)[None, :] % SAMPLES
    angle = phase * (2.0 * np.pi / SAMPLES)
    waves = np.stack([np.cos(angle), np.sin(angle)]).reshape(2, STEPS, -1, SAMPLES)
    table = waves.transpose(1, 0, 2, 3).reshape(2 * FREQS, SAMPLES) / np.sqrt(SAMPLES)
    return table.astype(np.float32).astype(ml_dtypes.bfloat16)


def params(mib=48):
    return pltpu.CompilerParams(vmem_limit_bytes=mib * 2**20)


def cost(micros):
    return pl.CostEstimate(flops=int(micros * 1e9), bytes_accessed=int(micros * 3e6), transcendentals=0)


ANYWHERE = pl.BlockSpec(memory_space=pltpu.HBM)


def in_hbm(*arrays):
    return [pltpu.with_memory_space_constraint(array, pltpu.HBM) for array in arrays]


def nt_dot(left, right):
    return lax.dot_general(left, right, (((1,), (1,)), ((), ())), preferred_element_type=F32)


def split_rows(values):
    high = values.astype(BF16)
    low = (values - high.astype(F32)).astype(BF16)
    return jnp.concatenate([high, low], axis=0)


def at(tile):
    if isinstance(tile, int):
        return slice(tile * SLICE, (tile + 1) * SLICE)
    return pl.ds(pl.multiple_of(tile * SLICE, SLICE), SLICE)


def join_rows(both):
    half = both.shape[0] // 2
    return both[:half] + both[half:]


def flip(table):
    wide = jnp.concatenate(
        [table.astype(F32), jnp.zeros((N_SHOT, LANES - CAP), F32)], axis=1
    )
    return wide.T[:CAP].astype(jnp.int32)


def index_tiles(send_rows, send_counts, src, rcv, off):
    slots = lax.broadcasted_iota(jnp.int32, (CAP, N_SHOT), 0)
    targets = jnp.where(slots < send_counts[...], flip(send_rows[...]), -1)
    trace_ids = lax.broadcasted_iota(jnp.int32, (CAP, TR_DEV), 1)
    places = lax.broadcasted_iota(jnp.int32, (CAP, TR_DEV), 0)
    total = jnp.zeros((CAP, TR_DEV), jnp.int32)
    for owner in range(N_SHOT):
        hit = targets[:, owner : owner + 1] == trace_ids
        total = total + jnp.where(hit, places + owner * LANES, 0)
    slot_row = jnp.sum(total, axis=0, keepdims=True)
    rows = [src[...] & (SRC_G - 1), rcv[...] & (RCV_G - 1), off[...]]
    rows = [row.reshape(1, TR_DEV) for row in rows] + [slot_row]
    table = jnp.concatenate(rows, axis=0).astype(F32)
    tiles = [table[:, q * LANES : (q + 1) * LANES] for q in range(TRACE_TILES)]
    tiles.append(jnp.zeros((INDEX_ROWS - 4 * TRACE_TILES, LANES), F32))
    return jnp.concatenate(tiles, axis=0)


def spectra_kernel(traces, waves, *refs):
    given, out, own, basis, extra = refs[:6], refs[6], refs[7], refs[8], refs[9]
    small, sems, small_sems = refs[10:16], refs[16], refs[17]
    indices = [
        pltpu.make_async_copy(a, b, small_sems.at[k]) for k, (a, b) in enumerate(zip(given, small))
    ]
    for copy in indices:
        copy.start()
    pieces = []
    for k in range(TRACE_TILES):
        span = slice(k * LANES, (k + 1) * LANES)
        pieces.append((traces.at[span], own.at[span]))
    size = 2 * FREQS // STEPS // 2
    for k in range(2 * STEPS):
        span = slice(k * size, (k + 1) * size)
        pieces.append((waves.at[span], basis.at[span]))
    copies = [pltpu.make_async_copy(a, b, sems.at[k]) for k, (a, b) in enumerate(pieces)]
    for copy in copies:
        copy.start()
    for copy in indices:
        copy.wait()
    send_rows, send_counts, bins, src, rcv, off = small
    pad = jnp.zeros((N_SHOT, LANES - CAP), F32)
    extra[:N_SHOT] = jnp.concatenate([bins[...].astype(F32), pad], axis=1)
    extra[N_SHOT:] = index_tiles(send_rows, send_counts, src, rcv, off)
    for part in range(N_SHOT):
        out[part, BINS_AT:, :] = extra[...]
    for copy in copies[:TRACE_TILES]:
        copy.wait()
    half = FREQS // STEPS
    for step in range(STEPS):
        for copy in copies[TRACE_TILES + 2 * step : TRACE_TILES + 2 * step + 2]:
            copy.wait()
        parts = nt_dot(basis[2 * half * step : 2 * half * (step + 1)], own[...])
        logs = jnp.log1p(parts[:half] * parts[:half] + parts[half:] * parts[half:])
        for part in range(half // SLICE):
            for q in range(TRACE_TILES):
                out[step * (half // SLICE) + part, q * SLICE : (q + 1) * SLICE, :] = logs[
                    part * SLICE : (part + 1) * SLICE, q * LANES : (q + 1) * LANES
                ]


def log_spectra(traces, basis, *small):
    return pl.pallas_call(
        spectra_kernel,
        in_specs=[ANYWHERE] * (2 + len(small)),
        out_shape=jax.ShapeDtypeStruct((N_SHOT, DATA_ROWS, LANES), F32),
        scratch_shapes=[
            VMEM((TR_DEV, SAMPLES), BF16),
            VMEM((2 * FREQS, SAMPLES), BF16),
            VMEM((DATA_ROWS - BINS_AT, LANES), F32),
        ]
        + [VMEM(array.shape, jnp.int32) for array in small]
        + [
            pltpu.SemaphoreType.DMA((TRACE_TILES + 2 * STEPS,)),
            pltpu.SemaphoreType.DMA((len(small),)),
        ],
        compiler_params=params(24),
        cost_estimate=cost(5),
        name="spectra",
    )(*in_hbm(traces, basis, *small))


def fill_ids(ids):
    ids[...] = lax.broadcasted_iota(jnp.int32, ids.shape, 0).astype(F32).astype(BF16)


def fill_hot(tiles, ids, hot):
    one = jnp.ones((1, 1), BF16)
    zero = jnp.zeros((1, 1), BF16)
    values = tiles.astype(F32)
    for q in range(TRACE_TILES):
        span = slice(q * LANES, (q + 1) * LANES)
        first = 0
        for row, size, base in ((0, SRC_G, 0), (2, 128, 0), (1, RCV_G, 0), (3, 256, 0), (3, 256, 256)):
            wanted = (values[4 * q + row : 4 * q + row + 1] - base).astype(BF16)
            hot[first : first + size, span] = jnp.where(ids[:size] == wanted, one, zero)
            first += size


def resolve_bins(data, block):
    tiles = data[block, INDEX_AT:].astype(jnp.int32)
    rows = [data[owner, pl.ds(BINS_AT + block, 1)] for owner in range(N_SHOT)]
    table = jnp.concatenate(rows, axis=0)
    owners = lax.broadcasted_iota(jnp.int32, (N_SHOT, LANES), 0)
    resolved = []
    for q in range(TRACE_TILES):
        slot = tiles[4 * q + 3 : 4 * q + 4]
        place = jnp.broadcast_to(slot & (LANES - 1), (N_SHOT, LANES))
        found = jnp.take_along_axis(table, place, axis=1, mode="promise_in_bounds")
        found = jnp.where(owners == slot >> 7, found.astype(jnp.int32) + owners * CMP_G, 0)
        resolved += [tiles[4 * q : 4 * q + 3], jnp.sum(found, axis=0, keepdims=True)]
    resolved.append(jnp.zeros((INDEX_ROWS - 4 * TRACE_TILES, LANES), jnp.int32))
    return jnp.concatenate(resolved, axis=0)


def prepare_block(data, index, ids, hot, block):
    tiles = resolve_bins(data, block)
    index[block] = tiles
    one = jnp.ones((1, 1), BF16)
    zero = jnp.zeros((1, 1), BF16)
    for q in range(TRACE_TILES):
        for place, row in enumerate((0, 2, 1, 3)):
            lane = tiles[4 * q + row : 4 * q + row + 1] & (LANES - 1)
            hit = ids[:LANES] == lane.astype(F32).astype(BF16)
            span = slice(q * LANES, (q + 1) * LANES)
            hot[place * LANES : (place + 1) * LANES, span] = jnp.where(hit, one, zero)


def add_block(data, index, hot, tab, rcv, block):
    tiles = index[block]
    values = [data[block, q * SLICE : (q + 1) * SLICE] for q in range(TRACE_TILES)]

    def of_tile(row, tile):
        picked = [
            jnp.where(tiles[4 * q + row : 4 * q + row + 1] >> 7 == tile, values[q], 0.0)
            for q in range(TRACE_TILES)
        ]
        return split_rows(jnp.concatenate(picked, axis=1))

    plain = nt_dot(split_rows(jnp.concatenate(values, axis=1)), hot[: 2 * LANES])
    tab[at(block)] = join_rows(plain[:, :LANES])
    tab[at(OFF_TILE)] += join_rows(plain[:, LANES:])
    parts = jnp.concatenate([of_tile(1, tile) for tile in range(RCV_TILES)], axis=0)
    sums = nt_dot(parts, hot[2 * LANES : 3 * LANES])
    for tile in range(RCV_TILES):
        rcv[tile] += join_rows(sums[tile * 2 * SLICE : (tile + 1) * 2 * SLICE])
    cmp_tiles = LIVE_TILES - CMP_TILE
    parts = jnp.concatenate([of_tile(3, tile) for tile in range(cmp_tiles)], axis=0)
    sums = nt_dot(parts, hot[3 * LANES :])
    for tile in range(cmp_tiles):
        tab[at(CMP_TILE + tile)] += join_rows(sums[tile * 2 * SLICE : (tile + 1) * 2 * SLICE])


def adjoint_kernel(data, tab, rcv, index, hot_even, hot_odd, ids):
    tab[OFF_TILE * SLICE :] = jnp.zeros((TAB_ROWS - OFF_TILE * SLICE, LANES), F32)
    rcv[...] = jnp.zeros((RCV_TILES, SLICE, LANES), F32)
    fill_ids(ids)
    prepare_block(data, index, ids, hot_even, 0)

    @pl.loop(0, N_SHOT // 2)
    def _(pair):
        even = 2 * pair
        prepare_block(data, index, ids, hot_odd, even + 1)
        add_block(data, index, hot_even, tab, rcv, even)
        prepare_block(data, index, ids, hot_even, jnp.minimum(even + 2, N_SHOT - 1))
        add_block(data, index, hot_odd, tab, rcv, even + 1)


EXACT = 128


def kept_part(counts):
    return (counts.astype(jnp.int32) & (EXACT - 1)).astype(jnp.int8)


def left_over(counts):
    whole = counts.astype(jnp.int32)
    return (whole - (whole & (EXACT - 1))).astype(F32).astype(BF16)


def widen(counts):
    return counts.astype(F32).astype(BF16)


def peak(counts):
    top = jnp.max(counts, axis=0, keepdims=True)
    best = top[:, :LANES]
    for start in range(LANES, counts.shape[1], LANES):
        best = jnp.maximum(best, top[:, start : start + LANES])
    return best


def block_counts(hot):
    with_cmp = nt_dot(hot[:SOR], hot[SOR:])
    with_rcv = nt_dot(hot[:SO], hot[SO:SOR])
    with_off = nt_dot(hot[:SRC_G], hot[SRC_G:SO])
    rows = jnp.concatenate([with_off, with_rcv[:SRC_G], with_cmp[:SRC_G]], axis=1)
    return rows, with_cmp[SRC_G:], with_rcv[SRC_G:]


def count_kernel(
    index, wide, kept, to_cmp_kept, to_rcv_kept, most, diag, hot_even, hot_odd, ids, to_cmp, to_rcv, *, first
):
    step = pl.program_id(0)
    even = first + 2 * step

    @pl.when(step == 0)
    def _():
        to_cmp[...] = jnp.zeros_like(to_cmp)
        to_rcv[...] = jnp.zeros_like(to_rcv)
        diag[...] = jnp.zeros_like(diag)
        most[...] = jnp.zeros_like(most)
        fill_ids(ids)
        fill_hot(index[even], ids, hot_even)

    def add(hot, place):
        rows, cmp_counts, rcv_counts = block_counts(hot)
        to_cmp[...] += cmp_counts
        to_rcv[...] += rcv_counts
        diag[...] += jnp.sum(rows, axis=0, keepdims=True)
        part = rows.astype(jnp.int32) & (EXACT - 1)
        span = slice(place * SRC_G, (place + 1) * SRC_G)
        kept[span] = part.astype(jnp.int8)
        wide[span] = part.astype(F32).astype(BF16)
        most[...] = jnp.maximum(most[...], peak(rows))

    fill_hot(index[even + 1], ids, hot_odd)
    add(hot_even, 0)
    fill_hot(index[jnp.minimum(even + 2, N_SHOT - 1)], ids, hot_even)
    add(hot_odd, 1)

    @pl.when(step == COUNT_STEPS - 1)
    def _():
        to_cmp_kept[...] = kept_part(to_cmp[...])
        to_rcv_kept[...] = kept_part(to_rcv[...])
        most[...] = jnp.maximum(most[...], jnp.maximum(peak(to_cmp[...]), peak(to_rcv[...])))


def add_left_over(most_1, most_2, index, hot, ids, to_cmp, to_rcv, use_both, use_rows):
    top = jnp.maximum(jnp.max(most_1[...]), jnp.max(most_2[...]))

    @pl.when(top >= EXACT)
    def _():
        fill_ids(ids)
        for half in range(2):
            to_cmp[...] = jnp.zeros_like(to_cmp)
            to_rcv[...] = jnp.zeros_like(to_rcv)

            @pl.loop(half * HALF, (half + 1) * HALF)
            def _(block):
                fill_hot(index[block], ids, hot)
                rows, cmp_counts, rcv_counts = block_counts(hot)
                to_cmp[...] += cmp_counts
                to_rcv[...] += rcv_counts
                use_rows(block, left_over(rows))

            use_both(left_over(to_cmp[...]), left_over(to_rcv[...]))


def widen_kernel(kept_1, kept_2, cmp_1, cmp_2, rcv_1, rcv_2, wide, to_cmp, to_rcv, held, small_cmp, small_rcv, sems):
    pieces = []
    for chunk in range(CHUNKS):
        source = kept_1 if chunk < CHUNKS // 2 else kept_2
        start = chunk % (CHUNKS // 2) * CHUNK_ROWS
        pieces.append((source.at[start : start + CHUNK_ROWS], held.at[chunk]))
    pieces += [(cmp_1, small_cmp.at[0]), (cmp_2, small_cmp.at[1])]
    pieces += [(rcv_1, small_rcv.at[0]), (rcv_2, small_rcv.at[1])]
    copies = [pltpu.make_async_copy(a, b, sems.at[k]) for k, (a, b) in enumerate(pieces)]
    for copy in copies:
        copy.start()
    for chunk in range(CHUNKS):
        copies[chunk].wait()
        wide[chunk * CHUNK_ROWS : (chunk + 1) * CHUNK_ROWS] = widen(held[chunk])
    for copy in copies[CHUNKS:]:
        copy.wait()
    to_cmp[...] = (small_cmp[0].astype(F32) + small_cmp[1].astype(F32)).astype(BF16)
    to_rcv[...] = (small_rcv[0].astype(F32) + small_rcv[1].astype(F32)).astype(BF16)


def load_halves(tab, rcv, own, shared):
    for tile in range(N_SHOT):
        own[:, tile * LANES : (tile + 1) * LANES] = split_rows(tab[at(tile)])
    shared[: 2 * SLICE, :LANES] = split_rows(tab[at(OFF_TILE)])
    for tile in range(RCV_TILES):
        shared[: 2 * SLICE, (1 + tile) * LANES : (2 + tile) * LANES] = split_rows(rcv[tile])
    for tile in range(CMP_TILE, LIVE_TILES):
        start = (tile - CMP_TILE) * LANES + OR
        shared[: 2 * SLICE, start : start + LANES] = split_rows(tab[at(tile)])


def normal_kernel(
    tab_in, rcv_in, first, last, cmp_1, cmp_2, rcv_1, rcv_2, diag_1, diag_2, most_1, most_2, index,
    tab, rcv, own_count, own, shared, to_shared, to_own, hot, ids, exact_cmp, exact_rcv,
):
    top = 2 * SLICE
    half = HALF * SRC_G
    load_halves(tab_in, rcv_in, own, shared)
    lanes = lax.broadcasted_iota(jnp.int32, (16, SHARED), 1)
    shared[top:] = jnp.where(lanes < LANES, 1.0, 0.0).astype(BF16)
    sums = jnp.dot(own[:, :half], first[...], preferred_element_type=F32)
    to_shared[...] = sums + jnp.dot(own[:, half:], last[...], preferred_element_type=F32)
    to_own[:, :half] = nt_dot(shared[...], first[...])
    to_own[:, half:] = nt_dot(shared[...], last[...])

    def others(to_cmp, to_rcv):
        cmp_sums = jnp.dot(shared[:top, :OR], to_cmp, preferred_element_type=F32)
        to_shared[:, OR:] += cmp_sums
        to_shared[:, :OR] += nt_dot(shared[:top, OR:], to_cmp)
        rcv_sums = jnp.dot(shared[:top, :LANES], to_rcv, preferred_element_type=F32)
        to_shared[:, LANES:OR] += rcv_sums
        to_shared[:, :LANES] += nt_dot(shared[:top, LANES:OR], to_rcv)

    def use_rows(block, rows):
        span = pl.ds(pl.multiple_of(block * SRC_G, SRC_G), SRC_G)
        to_shared[...] += jnp.dot(own[:, span], rows, preferred_element_type=F32)
        to_own[:, span] += nt_dot(shared[...], rows)

    def both_of(one, other):
        return (one[...].astype(F32) + other[...].astype(F32)).astype(BF16)

    others(both_of(cmp_1, cmp_2), both_of(rcv_1, rcv_2))
    add_left_over(most_1, most_2, index, hot, ids, exact_cmp, exact_rcv, others, use_rows)
    diag = diag_1[...] + diag_2[...]
    for tile in range(N_SHOT):
        span = slice(tile * LANES, (tile + 1) * LANES)
        count = to_own[top : top + 1, span]
        own_count[tile : tile + 1] = count
        tab[at(tile)] = join_rows(to_own[:top, span]) + count * tab_in[at(tile)]
    tab[at(OFF_TILE)] = join_rows(to_shared[:, :LANES]) + diag[:, :LANES] * tab_in[at(OFF_TILE)]
    for tile in range(RCV_TILES):
        span = slice((1 + tile) * LANES, (2 + tile) * LANES)
        rcv[tile] = join_rows(to_shared[:, span]) + diag[:, span] * rcv_in[tile]
    for tile in range(CMP_TILE, LIVE_TILES):
        start = (tile - CMP_TILE) * LANES + OR
        span = slice(start, start + LANES)
        tab[at(tile)] = join_rows(to_shared[:, span]) + diag[:, span] * tab_in[at(tile)]
    tab[LIVE_ROWS:] = jnp.zeros((TAB_ROWS - LIVE_ROWS, LANES), F32)


def all_sum(values):
    return jnp.sum(values, axis=tuple(range(values.ndim)), keepdims=True).reshape(1, 1)


def fold(values):
    total = values[:, :LANES]
    for start in range(LANES, values.shape[1], LANES):
        total = total + values[:, start : start + LANES]
    return total


def norm_kernel(
    tab_b, rcv_b, tab_y, rcv_y, wide, cmp_counts, rcv_counts, diag_1, diag_2, most_1, most_2, index, own_count,
    out, tab_z, rcv_z, own, shared, to_shared, hot, ids, exact_cmp, exact_rcv,
):
    shared_b = tab_b[:LIVE_ROWS]
    shared_y = tab_y[:LIVE_ROWS]
    shift = all_sum(shared_b * shared_y) / all_sum(shared_b * shared_b)
    shared_z = shared_y - shift * shared_b
    own_b = rcv_b[...]
    own_z = rcv_y[...] - shift * own_b
    tab_z[...] = shared_z
    rcv_z[...] = own_z
    load_halves(tab_z, rcv_z, own, shared)
    to_shared[...] = jnp.dot(own[...], wide[...], preferred_element_type=F32)

    def whole(tabs, own):
        return all_sum(tabs) * (1.0 / N_RCV) + all_sum(own)

    def others(to_cmp, to_rcv):
        cmp_sums = jnp.dot(shared[:, :OR], to_cmp, preferred_element_type=F32)
        to_shared[:, OR:] += cmp_sums
        rcv_sums = jnp.dot(shared[:, :LANES], to_rcv, preferred_element_type=F32)
        to_shared[:, LANES:OR] += rcv_sums

    def use_rows(block, rows):
        span = pl.ds(pl.multiple_of(block * SRC_G, SRC_G), SRC_G)
        to_shared[...] += jnp.dot(own[:, span], rows, preferred_element_type=F32)

    others(cmp_counts[...], rcv_counts[...])
    add_left_over(most_1, most_2, index, hot, ids, exact_cmp, exact_rcv, others, use_rows)
    tiles = [tab_z[at(OFF_TILE)]] + [rcv_z[tile] for tile in range(RCV_TILES)]
    tiles += [tab_z[at(tile)] for tile in range(CMP_TILE, LIVE_TILES)]
    rest = jnp.concatenate(tiles, axis=1)
    diag = diag_1[...] + diag_2[...]
    total = fold(2.0 * rest * join_rows(to_shared[...]) + diag * rest * rest)
    for tile in range(N_SHOT):
        total = total + own_count[tile : tile + 1] * tab_z[at(tile)] * tab_z[at(tile)]
    sums = (
        whole(shared_b * shared_b, own_b * own_b),
        whole(shared_b * shared_z, own_b * own_z),
        whole(shared_z * shared_z, own_z * own_z),
        all_sum(total),
        shift,
    )
    lanes = lax.broadcasted_iota(jnp.int32, (1, LANES), 1)
    row = jnp.zeros((1, LANES), F32)
    for lane, value in enumerate(sums):
        row = jnp.where(lanes == lane, value, row)
    out[...] = row


def whole_spec(*shape):
    return pl.BlockSpec(shape, lambda c: (0,) * len(shape))


TAB = (TAB_ROWS, LANES)
RCV = (RCV_TILES, SLICE, LANES)
INDEX = (N_SHOT, INDEX_ROWS, LANES)
INDEX_SPEC = pl.BlockSpec((1, INDEX_ROWS, LANES), lambda c: (c, 0, 0))


def table_shapes():
    return [jax.ShapeDtypeStruct(TAB, F32), jax.ShapeDtypeStruct(RCV, F32)]


def hot_scratch():
    return [VMEM((ROWS, TR_DEV), BF16), VMEM((256, LANES), BF16)]


def adjoint_apply(data):
    return pl.pallas_call(
        adjoint_kernel,
        out_shape=table_shapes() + [jax.ShapeDtypeStruct(INDEX, jnp.int32)],
        scratch_shapes=[VMEM((4 * LANES, TR_DEV), BF16)] * 2 + [VMEM((256, LANES), BF16)],
        compiler_params=params(24),
        cost_estimate=cost(8),
        name="adjoint_apply",
    )(data)


COUNTS = (HALF * SRC_G, SHARED)
TO_CMP = (OR, SHARED - OR)
TO_RCV = (LANES, RCV_G)
IN_VMEM = pl.BlockSpec(memory_space=VMEM)


def count_call(index, first):
    rows = pl.BlockSpec((2 * SRC_G, SHARED), lambda c: (c, 0))
    small = [whole_spec(*TO_CMP), whole_spec(*TO_RCV), whole_spec(1, LANES), whole_spec(1, SHARED)]
    return pl.pallas_call(
        functools.partial(count_kernel, first=first),
        grid=(COUNT_STEPS,),
        in_specs=[whole_spec(*INDEX)],
        out_specs=[rows, rows] + small,
        out_shape=[
            jax.ShapeDtypeStruct(COUNTS, BF16),
            pltpu.HBM(COUNTS, jnp.int8),
            jax.ShapeDtypeStruct(TO_CMP, jnp.int8),
            jax.ShapeDtypeStruct(TO_RCV, jnp.int8),
            jax.ShapeDtypeStruct((1, LANES), F32),
            jax.ShapeDtypeStruct((1, SHARED), F32),
        ],
        scratch_shapes=[VMEM((ROWS, TR_DEV), BF16)] * 2
        + [VMEM((256, LANES), BF16), VMEM(TO_CMP, F32), VMEM(TO_RCV, F32)],
        compiler_params=params(24),
        cost_estimate=cost(6),
        name="count_pairs",
    )(index)


def exact_scratch():
    return hot_scratch() + [VMEM(TO_CMP, F32), VMEM(TO_RCV, F32)]


def normal_apply(tab, rcv, index, counts_1, counts_2):
    wide_1, _, cmp_1, rcv_1, most_1, diag_1 = counts_1
    wide_2, _, cmp_2, rcv_2, most_2, diag_2 = counts_2
    return pl.pallas_call(
        normal_kernel,
        out_shape=table_shapes() + [jax.ShapeDtypeStruct((N_SHOT, LANES), F32)],
        scratch_shapes=[
            VMEM((2 * SLICE, N_SHOT * SRC_G), BF16),
            VMEM((2 * SLICE + 16, SHARED), BF16),
            VMEM((2 * SLICE, SHARED), F32),
            VMEM((2 * SLICE + 16, N_SHOT * SRC_G), F32),
        ]
        + exact_scratch(),
        compiler_params=params(20),
        cost_estimate=cost(3),
        name="normal_apply",
    )(tab, rcv, wide_1, wide_2, cmp_1, cmp_2, rcv_1, rcv_2, diag_1, diag_2, most_1, most_2, index)


def widen_counts(kept_1, kept_2):
    operands = [array for pair in zip(kept_1, kept_2) for array in pair]
    return pl.pallas_call(
        widen_kernel,
        in_specs=[ANYWHERE] * 6,
        out_shape=[
            jax.ShapeDtypeStruct((N_SHOT * SRC_G, SHARED), BF16),
            jax.ShapeDtypeStruct(TO_CMP, BF16),
            jax.ShapeDtypeStruct(TO_RCV, BF16),
        ],
        scratch_shapes=[
            VMEM((CHUNKS, CHUNK_ROWS, SHARED), jnp.int8),
            VMEM((2,) + TO_CMP, jnp.int8),
            VMEM((2,) + TO_RCV, jnp.int8),
            pltpu.SemaphoreType.DMA((CHUNKS + 4,)),
        ],
        compiler_params=params(20),
        cost_estimate=cost(3),
        name="widen_counts",
    )(*in_hbm(*operands))


def norm_sums(tab_b, rcv_b, tab_y, rcv_y, own_count, index, wide, counts_1, counts_2):
    most_1, diag_1 = counts_1[4:]
    most_2, diag_2 = counts_2[4:]
    return pl.pallas_call(
        norm_kernel,
        out_shape=jax.ShapeDtypeStruct((1, LANES), F32),
        scratch_shapes=[
            VMEM((LIVE_ROWS, LANES), F32),
            VMEM(RCV, F32),
            VMEM((2 * SLICE, N_SHOT * SRC_G), BF16),
            VMEM((2 * SLICE, SHARED), BF16),
            VMEM((2 * SLICE, SHARED), F32),
        ]
        + exact_scratch(),
        compiler_params=params(20),
        cost_estimate=cost(2),
        name="norm_sums",
    )(tab_b, rcv_b, tab_y, rcv_y, *wide, diag_1, diag_2, most_1, most_2, index, own_count)


def spread_kernel(parts, out):
    total = parts[0]
    for source in range(1, N_RCV):
        total = total + parts[source]
    for dest in range(N_RCV):
        out[dest] = total


def exchange(array, axis):
    return lax.all_to_all(array, axis, split_axis=0, concat_axis=0, tiled=True)


def spread_shares(arrived):
    shape = (N_RCV, SHARE, LANES)
    spread = pl.pallas_call(
        spread_kernel,
        out_shape=jax.ShapeDtypeStruct(shape, F32),
        compiler_params=params(24),
        cost_estimate=cost(1),
        name="sum_shares",
    )(arrived.reshape(shape))
    return spread.reshape(TAB)


def pack_kernel(tab, rcv, *refs, first):
    out, rows, sems = refs[-3:]
    lanes = lax.broadcasted_iota(jnp.int32, (SLICE, LANES), 1)
    half = SLICE // 2
    copies = []
    for dest in range(N_SHOT):
        rows[dest, :SLICE] = tab[at(dest)]
        rows[dest, SLICE : 2 * SLICE] = tab[at(OFF_TILE)]
        cmp_first = dest * CMP_G
        rcv_first = dest * (RCV_G // N_SHOT)
        bins = tab[at(CMP_TILE + cmp_first // LANES)]
        cmp_part = pltpu.roll(bins, (-cmp_first) % LANES, 1)
        rcv_part = pltpu.roll(rcv[rcv_first // LANES], (CMP_G - rcv_first) % LANES, 1)
        both = jnp.where(lanes < CMP_G, cmp_part, rcv_part)
        moved = pltpu.roll(both[half:], LANES // 2, 1)
        rows[dest, 2 * SLICE :] = jnp.where(lanes[:half] < LANES // 2, both[:half], moved)
        if dest % PACK == PACK - 1:
            group = dest // PACK
            span = slice(group * PACK, (group + 1) * PACK)
            place = out.at[span, first : first + OWN_ROWS]
            copies.append(pltpu.make_async_copy(rows.at[span], place, sems.at[group]))
            copies[-1].start()
    for copy in copies:
        copy.wait()


def pack_owned(tab, rcv, former=None):
    given = [] if former is None else in_hbm(former)
    return pl.pallas_call(
        functools.partial(pack_kernel, first=OWN_ROWS * len(given)),
        in_specs=[pl.BlockSpec(memory_space=VMEM)] * 2 + [ANYWHERE] * len(given),
        out_specs=ANYWHERE,
        out_shape=pltpu.HBM((N_SHOT, 2 * OWN_ROWS, LANES), F32),
        scratch_shapes=[
            VMEM((N_SHOT, OWN_ROWS, LANES), F32),
            pltpu.SemaphoreType.DMA((N_SHOT // PACK,)),
        ],
        input_output_aliases={2: 0} if given else {},
        compiler_params=params(24),
        cost_estimate=cost(1),
        name="pack_owned",
    )(tab, rcv, *given)


def swapped(value, axis, size, bit):
    return lax.ppermute(value, axis, [(s, s ^ bit) for s in range(size)])


def gather_sums(sums):
    for bit in (1, 2, 6):
        sums = sums + swapped(sums, "rcv", N_RCV, bit)
    here = jnp.arange(N_SHOT, dtype=jnp.int32)[:, None] == lax.axis_index("shot")
    rows = jnp.where(here, sums, 0.0)
    for bit in (1, 3, 4, 12):
        rows = rows + swapped(rows, "shot", N_SHOT, bit)
    return rows


def finish_kernel(sums, owned, source, receiver, offset, cmp):
    rows = sums[...]
    norm_b, cross, norm_z, norm_az, shift = (rows[:, lane : lane + 1] for lane in range(5))
    shift = shift * (1.0 / N_RCV)

    def total(values):
        return jnp.sum(values, axis=0, keepdims=True)

    total_b = total(norm_b)
    first = total(cross + shift * norm_b) / total_b
    off = shift - first
    zz = total(norm_z + 2.0 * off * cross + off * off * norm_b)
    zaz = total(
        norm_az
        + 2.0 * off * (norm_z + shift * cross)
        + off * off * (cross + shift * norm_b)
    )
    second = zaz / zz
    det = first * second - zz / total_b
    scale_b = (first + second) / det
    scale_y = 1.0 / det

    def combine(sender, start, stop):
        part_y = owned[sender, OWN_ROWS + start : OWN_ROWS + stop]
        return scale_b * owned[sender, start:stop] - scale_y * part_y

    def spread_halves(tile):
        return jnp.concatenate([tile, pltpu.roll(tile, LANES // 2, 1)], axis=0)

    per_tile = LANES // SLICE
    for group in range(N_SHOT // per_tile):
        span = slice(group * LANES, (group + 1) * LANES)
        senders = range(group * per_tile, (group + 1) * per_tile)
        source[:, span] = jnp.concatenate([combine(i, 0, SLICE) for i in senders], axis=0).T
        offset[:, span] = jnp.concatenate(
            [combine(i, SLICE, 2 * SLICE) for i in senders], axis=0
        ).T
        rest = jnp.concatenate(
            [spread_halves(combine(i, 2 * SLICE, OWN_ROWS)) for i in senders], axis=0
        ).T
        cmp[:, span] = rest[:CMP_G]
        receiver[0, :, span] = rest[CMP_G : CMP_G + RCV_G // N_SHOT]


def finish(sums, owned):
    return pl.pallas_call(
        finish_kernel,
        out_shape=[
            jax.ShapeDtypeStruct((SRC_G, FREQS), F32),
            jax.ShapeDtypeStruct((1, RCV_G // N_SHOT, FREQS), F32),
            jax.ShapeDtypeStruct((128, FREQS), F32),
            jax.ShapeDtypeStruct((CMP_G, FREQS), F32),
        ],
        compiler_params=params(),
        name="finish",
    )(sums, owned)


def per_device(basis, traces, src_index, rcv_index, off_index, send_rows, send_counts, recv_bins):
    data = log_spectra(
        traces, basis, send_rows[0], send_counts, recv_bins[0], src_index, rcv_index, off_index
    )
    data = exchange(data, "shot")

    tab_b, rcv_b, index = adjoint_apply(data)
    arrived = exchange(tab_b, "rcv")
    counts_1 = count_call(index, 0)
    arrived, index, counts_1 = lax.optimization_barrier((arrived, index, counts_1))
    spread = spread_shares(arrived)
    spread, index = lax.optimization_barrier((spread, index))
    tab_b = exchange(spread, "rcv")
    counts = (counts_1, count_call(index, HALF))

    tab_y, rcv_y, own_count = normal_apply(tab_b, rcv_b, index, *counts)
    arrived = exchange(tab_y, "rcv")
    packed = pack_owned(tab_b, rcv_b)
    arrived, packed = lax.optimization_barrier((arrived, packed))
    spread = spread_shares(arrived)
    kept = [counts_half[1:4] for counts_half in counts]
    spread, kept = lax.optimization_barrier((spread, kept))
    tab_y = exchange(spread, "rcv")
    wide = widen_counts(*kept)
    tab_y, wide = lax.optimization_barrier((tab_y, wide))
    packed = pack_owned(tab_y, rcv_y, packed)
    tab_y, packed = lax.optimization_barrier((tab_y, packed))
    owned = exchange(packed, "shot")
    sums = norm_sums(tab_b, rcv_b, tab_y, rcv_y, own_count, index, wide, *counts)
    return tuple(finish(gather_sums(sums), owned))


def solution(mesh):
    basis = fourier_rows()
    mapped = jax.shard_map(
        per_device,
        mesh=mesh,
        in_specs=(
            P(),
            P(("shot", "rcv"), None),
            P(("shot", "rcv")),
            P(("shot", "rcv")),
            P(("shot", "rcv")),
            P(("shot", "rcv"), None, None),
            P(("shot", "rcv"), None),
            P(("shot", "rcv"), None, None),
        ),
        out_specs=(P("shot", None), P("rcv", "shot", None), P(), P("shot", None)),
        check_vma=False,
    )

    def run(*args):
        return mapped(jnp.asarray(basis), *args)

    return run
```

time: 966 us -> 142 us (0.15)
  waiting for transfers between devices: 462 us -> 27.3 us
  blocking collectives: 352 us -> 30.4 us
  other arithmetic: 39.2 us -> 0.24 us
  Pallas kernels: 0 us -> 38.9 us
  local copies, waits for them, and re-layouts: 39 us -> 9.52 us
  matrix products: 26.3 us -> 0 us
  between operations: 23.3 us -> 0.76 us
  starting transfers between devices: 21 us -> 33.7 us
    psum x5 -> x0, blocking collectives: 352 us -> none  [the longest x3 226 us: adjoint_apply(): lax.psum((off_part, jnp.sum(values * values)), ('shot', 'rcv'))]
    psum x4 -> x0, waiting for transfers between devices: 329 us -> none  [the longest x2 275 us: adjoint_apply(): lax.psum((off_part, jnp.sum(values * values)), ('shot', 'rcv'))]
    all_to_all x4 -> x5, waiting for transfers between devices: 133 us -> 12.4 us  [exchange(): return lax.all_to_all(array, axis, split_axis=0, concat_axis=0, tiled=True)]
    pallas_call x0 -> x12, Pallas kernels: none -> 38.9 us  [the longest x2 14.9 us: count_call(): pl.pallas_call(functools.partial(count_kernel, first=first), grid=(COUNT_...]
    all_to_all x0 -> x1, blocking collectives: none -> 30.4 us  [exchange(): return lax.all_to_all(array, axis, split_axis=0, concat_axis=0, tiled=True)]
    dot_general x17 -> x0, matrix products: 26.3 us -> none  [the longest x8 12.3 us: sum_rows(): jnp.dot(one_hot, values, precision=lax.Precision.HIGHEST, preferred_eleme...]
    gather x6 -> x0, local copies, waits for them, and re-layouts: 20.7 us -> none  [the longest x4 11.9 us: per_device(): cmp_pred = jnp.take(cmp_rows, slot_of_trace, axis=0)]
    ppermute x0 -> x7, waiting for transfers between devices: none -> 14.9 us  [swapped(): return lax.ppermute(value, axis, [(s, s ^ bit) for s in range(size)])]
  transfers between devices with their start and end apart: 8 -> 12, of which waited for: 6 -> 9; matrix products, arithmetic and copies ran while one was open for 3% -> 0% of each run, Pallas kernels for 0% -> 14%
where the time goes in v1:
time: 142 us; the launch traced here: 141 us
  Pallas kernels  38.9 us (27%)
  starting transfers between devices  33.7 us (24%)
  blocking collectives  30.4 us (21%)
  waiting for transfers between devices  27.3 us (19%)
  local copies, waits for them, and re-layouts  9.52 us (7%)
    all_to_all x1, blocking collectives, exchange(): return lax.all_to_all(array, axis, split_axis=0, concat_axis=0, tiled=True)  30.4 us
    all_to_all x5, starting transfers between devices, exchange(): return lax.all_to_all(array, axis, split_axis=0, concat_axis=0, tiled=True)  22 us
    ppermute x7, waiting for transfers between devices, swapped(): return lax.ppermute(value, axis, [(s, s ^ bit) for s in range(size)])  14.9 us
    pallas_call x2, Pallas kernels, count_call(): pl.pallas_call(functools.partial(count_kernel, first=first), grid=(COUNT_...  14.9 us
    all_to_all x5, waiting for transfers between devices, exchange(): return lax.all_to_all(array, axis, split_axis=0, concat_axis=0, tiled=True)  12.4 us
    ppermute x7, starting transfers between devices, swapped(): return lax.ppermute(value, axis, [(s, s ^ bit) for s in range(size)])  11.6 us
    unnamed x20, local copies, waits for them, and re-layouts  9.52 us
    pallas_call x1, Pallas kernels, adjoint_apply(): pl.pallas_call(adjoint_kernel, out_shape=table_shapes() + [jax.ShapeDtype...  7.46 us
  transfers between devices with their start and end apart: 12, of which 9 were waited for; matrix products, arithmetic and copies ran while one was open for 0% of the time, Pallas kernels for 14%

profile of v1, /device:TPU:0, one launch (start us, length us, event | category | flops | bytes accessed | tf_op | source)
XLA Modules:
  0.0 140.8 jit_solution(12570745836121978331)
XLA Ops:
  0.6 5.0 %spectra.1 = f32[16,200,128]{2,1,0:T(8,128)S(1)} custom-call(bf16[640,1024]{1,0:T(8,128)(2,1)} %traces.1, bf16[1024,1024]{1,0:T(8,128)(2,1)} %constant.10.clone.waves, s32[16,80]{1,0:T(8,128)} %bitcast.21, s32[1,16]{1,0:T(1,128)} %refs_1_.1, s32[16,80]{1,0:T(8,128)} %bitcast.22, s32[640]{0:T(1024)} %refs_3_.1, s32[640]{0:T(1024)} %refs_4_.1, s32[640]{0:T(1024)} %refs_5_.1), custom_call_target="tpu_custom_call" | custom-call | flops 5000000000 | bytes 15000000 | tf_op jit(solution)/shard_map/spectra/pallas_call | solution.py:167
  5.7 30.4 %all_to_all.57.data = f32[16,200,128]{2,1,0:T(8,128)S(1)} all-to-all(f32[16,200,128]{2,1,0:T(8,128)S(1)} %spectra.1), channel_id=1, replica_groups=mesh['shot'=16,'rcv'=8] {'shot'}, dimensions={0} | all-to-all | bytes 3276800 | tf_op jit(solution)/shard_map/all_to_all | solution.py:639
  36.1 7.5 %adjoint_apply.1 = (f32[704,128]{1,0:T(8,128)}, f32[2,32,128]{2,1,0:T(8,128)S(1)}, s32[16,24,128]{2,1,0:T(8,128)S(1)}) custom-call(f32[16,200,128]{2,1,0:T(8,128)S(1)} %all_to_all.57.data), custom_call_target="tpu_custom_call" | custom-call | flops 8000000000 | bytes 24000000 | tf_op jit(solution)/shard_map/adjoint_apply/pallas_call | solution.py:525
  43.5 5.3 %all-to-all-start.1 = ((f32[8,88,128]{2,1,0:T(8,128)}), f32[8,88,128]{2,1,0:T(8,128)S(1)}, u32[]{:S(2)}, u32[]{:S(2)}) async-start(f32[8,88,128]{2,1,0:T(8,128)} %bitcast.2), calls=%async_computation.1 | async-start | bytes 720896 | tf_op jit(solution)/shard_map/all_to_all | solution.py:639
  48.9 7.4 %count_pairs.2 = (bf16[1024,896]{1,0:T(8,128)(2,1)S(1)}, s8[1024,896]{1,0:T(32,128)(4,1)}, s8[384,512]{1,0:T(32,128)(4,1)S(1)}, s8[128,256]{1,0:T(32,128)(4,1)S(...) custom-call(s32[16,24,128]{2,1,0:T(8,128)S(1)} %get-tuple-element.63.index), custom_call_target="tpu_custom_call" | custom-call | flops 6000000000 | bytes 18000000 | tf_op jit(solution)/shard_map/count_pairs/pallas_call | solution.py:544
  56.3 1.2 copy-done.2
  58.4 4.8 %all-to-all-start.2 = ((f32[8,88,128]{2,1,0:T(8,128)}), f32[8,88,128]{2,1,0:T(8,128)S(1)}, u32[]{:S(2)}, u32[]{:S(2)}) async-start(f32[8,88,128]{2,1,0:T(8,128)} %bitcast.6), calls=%async_computation.2 | async-start | bytes 720896 | tf_op jit(solution)/shard_map/all_to_all | solution.py:639
  63.2 7.4 %count_pairs.3 = (bf16[1024,896]{1,0:T(8,128)(2,1)S(1)}, s8[1024,896]{1,0:T(32,128)(4,1)}, s8[384,512]{1,0:T(32,128)(4,1)S(1)}, s8[128,256]{1,0:T(32,128)(4,1)S(...) custom-call(s32[16,24,128]{2,1,0:T(8,128)S(1)} %get-tuple-element.63.index), custom_call_target="tpu_custom_call" | custom-call | flops 6000000000 | bytes 18000000 | tf_op jit(solution)/shard_map/count_pairs/pallas_call | solution.py:544
  70.6 1.3 copy-done.4
  71.9 1.6 %copy-done.3 = bf16[1024,896]{1,0:T(8,128)(2,1)S(1)} copy-done((bf16[1024,896]{1,0:T(8,128)(2,1)S(1)}, bf16[1024,896]{1,0:T(8,128)(2,1)}, u32[]{:S(2)}) %copy-start.3) | copy-done | bytes 1835032
  73.5 1.5 %copy-done.5 = bf16[1024,896]{1,0:T(8,128)(2,1)S(1)} copy-done((bf16[1024,896]{1,0:T(8,128)(2,1)S(1)}, bf16[1024,896]{1,0:T(8,128)(2,1)}, u32[]{:S(2)}) %copy-start.5) | copy-done | bytes 1835032
  75.0 3.0 %normal_apply.1 = (f32[704,128]{1,0:T(8,128)}, f32[2,32,128]{2,1,0:T(8,128)S(1)}, f32[16,128]{1,0:T(8,128)S(1)}) custom-call(f32[704,128]{1,0:T(8,128)S(1)} %bitcast.16, f32[2,32,128]{2,1,0:T(8,128)S(1)} %get-tuple-element.61.rcv_in.rcv.rcv_b, bf16[1024,896]{1,0:T(8,128)(2,1)S(1)} %copy-done.3, bf16[1024,896]{1,0:T(8,128)(2,1)S(1)} %copy-done.5, ...), custom_call_target="tpu_custom_call" | custom-call | flops 3000000000 | bytes 9000000 | tf_op jit(solution)/shard_map/normal_apply/pallas_call | solution.py:572
  78.0 4.8 %all-to-all-start.3 = ((f32[8,88,128]{2,1,0:T(8,128)}), f32[8,88,128]{2,1,0:T(8,128)S(1)}, u32[]{:S(2)}, u32[]{:S(2)}) async-start(f32[8,88,128]{2,1,0:T(8,128)} %bitcast.8), calls=%async_computation.3 | async-start | bytes 720896 | tf_op jit(solution)/shard_map/all_to_all | solution.py:639
  83.9 7.5 %all-to-all-done.3 = f32[8,88,128]{2,1,0:T(8,128)S(1)} async-done(((f32[8,88,128]{2,1,0:T(8,128)}), f32[8,88,128]{2,1,0:T(8,128)S(1)}, u32[]{:S(2)}, u32[]{:S(2)}) %all-to-all-start.3) | async-done | bytes 360480 | tf_op jit(solution)/shard_map/all_to_all | solution.py:639
  92.1 3.4 %all-to-all-start.4 = ((f32[8,88,128]{2,1,0:T(8,128)}), f32[8,88,128]{2,1,0:T(8,128)S(1)}, u32[]{:S(2)}, u32[]{:S(2)}) async-start(f32[8,88,128]{2,1,0:T(8,128)} %bitcast.12), calls=%async_computation.4 | async-start | bytes 720896 | tf_op jit(solution)/shard_map/all_to_all | solution.py:639
  95.6 1.8 %widen_counts.1 = (bf16[2048,896]{1,0:T(8,128)(2,1)S(1)}, bf16[384,512]{1,0:T(8,128)(2,1)S(1)}, bf16[128,256]{1,0:T(8,128)(2,1)S(1)}) custom-call(s8[1024,896]{1,0:T(32,128)(4,1)} %get-tuple-element.78.kept_1, s8[1024,896]{1,0:T(32,128)(4,1)} %get-tuple-element.79.kept_2, s8[384,512]{1,0:T(32,128)(4,1)} %copy-done.6, s8[384,512]{1,0:T(32,128)(4,1)} %copy-done.7, ...), custom_call_target="tpu_custom_call" | custom-call | flops 3000000000 | bytes 9000000 | tf_op jit(solution)/shard_map/widen_counts/pallas_call | solution.py:590
  97.4 1.9 %copy-done = bf16[2048,896]{1,0:T(8,128)(2,1)} copy-done((bf16[2048,896]{1,0:T(8,128)(2,1)}, bf16[2048,896]{1,0:T(8,128)(2,1)S(1)}, u32[]{:S(2)}) %copy-start) | copy-done | bytes 3670040
  99.3 4.8 %all-to-all-done.4 = f32[8,88,128]{2,1,0:T(8,128)S(1)} async-done(((f32[8,88,128]{2,1,0:T(8,128)}), f32[8,88,128]{2,1,0:T(8,128)S(1)}, u32[]{:S(2)}, u32[]{:S(2)}) %all-to-all-start.4) | async-done | bytes 360480 | tf_op jit(solution)/shard_map/all_to_all | solution.py:639
  105.2 3.7 %all-to-all-start.5 = ((f32[16,160,128]{2,1,0:T(8,128)}), f32[16,160,128]{2,1,0:T(8,128)S(1)}, u32[]{:S(2)}, u32[]{:S(2)}) async-start(f32[16,160,128]{2,1,0:T(8,128)} %pack_owned.3), calls=%async_computation.5 | async-start | bytes 2621440 | tf_op jit(solution)/shard_map/all_to_all | solution.py:639
  108.9 2.0 %copy-done.1 = bf16[2048,896]{1,0:T(8,128)(2,1)S(1)} copy-done((bf16[2048,896]{1,0:T(8,128)(2,1)S(1)}, bf16[2048,896]{1,0:T(8,128)(2,1)}, u32[]{:S(2)}) %copy-start.1) | copy-done | bytes 3670040
  111.0 1.3 norm_sums.1
  114.1 3.0 %collective-permute-done.1 = f32[1,128]{1,0:T(1,128)S(1)} collective-permute-done((f32[1,128]{1,0:T(1,128)S(1)}, f32[1,128]{1,0:T(1,128)S(1)}, u32[]{:S(2)}, u32[]{:S(2)}) %collective-permute-start.1) | collective-permute-done | bytes 544 | tf_op jit(solution)/shard_map/ppermute | solution.py:699
  118.2 3.6 %collective-permute-done.2 = f32[1,128]{1,0:T(1,128)S(1)} collective-permute-done((f32[1,128]{1,0:T(1,128)S(1)}, f32[1,128]{1,0:T(1,128)S(1)}, u32[]{:S(2)}, u32[]{:S(2)}) %collective-permute-start.2) | collective-permute-done | bytes 544 | tf_op jit(solution)/shard_map/ppermute | solution.py:699
  121.9 1.8 %collective-permute-start.3 = (f32[16,128]{1,0:T(8,128)S(1)}, f32[16,128]{1,0:T(8,128)S(1)}, u32[]{:S(2)}, u32[]{:S(2)}) collective-permute-start(f32[16,128]{1,0:T(8,128)S(1)} %broadcast_select_fusion), channel_id=1, source_target_pairs={{0,8},{8,0},{16,24},{24,16},{32,40},{40,32},{48,56},{56,48},{64,72... | collective-permute-start | bytes 24584 | tf_op jit(solution)/shard_map/ppermute | solution.py:699
  123.7 1.8 %collective-permute-done.3 = f32[16,128]{1,0:T(8,128)S(1)} collective-permute-done((f32[16,128]{1,0:T(8,128)S(1)}, f32[16,128]{1,0:T(8,128)S(1)}, u32[]{:S(2)}, u32[]{:S(2)}) %collective-permute-start.3) | collective-permute-done | bytes 8224 | tf_op jit(solution)/shard_map/ppermute | solution.py:699
  125.6 3.0 %collective-permute-start.4 = (f32[16,128]{1,0:T(8,128)S(1)}, f32[16,128]{1,0:T(8,128)S(1)}, u32[]{:S(2)}, u32[]{:S(2)}) collective-permute-start(f32[16,128]{1,0:T(8,128)S(1)} %fusion), channel_id=1, source_target_pairs={{0,24},{8,16},{16,8},{24,0},{32,56},{40,48},{48,40},{56,32},{64,88... | collective-permute-start | bytes 24584 | tf_op jit(solution)/shard_map/ppermute | solution.py:699
  128.7 1.8 %collective-permute-done.4 = f32[16,128]{1,0:T(8,128)S(1)} collective-permute-done((f32[16,128]{1,0:T(8,128)S(1)}, f32[16,128]{1,0:T(8,128)S(1)}, u32[]{:S(2)}, u32[]{:S(2)}) %collective-permute-start.4) | collective-permute-done | bytes 8224 | tf_op jit(solution)/shard_map/ppermute | solution.py:699
  130.6 1.8 %collective-permute-start.5 = (f32[16,128]{1,0:T(8,128)S(1)}, f32[16,128]{1,0:T(8,128)S(1)}, u32[]{:S(2)}, u32[]{:S(2)}) collective-permute-start(f32[16,128]{1,0:T(8,128)S(1)} %fusion.1), channel_id=1, source_target_pairs={{0,32},{8,40},{16,48},{24,56},{32,0},{40,8},{48,16},{56,24},{64,96... | collective-permute-start | bytes 24584 | tf_op jit(solution)/shard_map/ppermute | solution.py:699
  132.4 1.8 %collective-permute-done.5 = f32[16,128]{1,0:T(8,128)S(1)} collective-permute-done((f32[16,128]{1,0:T(8,128)S(1)}, f32[16,128]{1,0:T(8,128)S(1)}, u32[]{:S(2)}, u32[]{:S(2)}) %collective-permute-start.5) | collective-permute-done | bytes 8224 | tf_op jit(solution)/shard_map/ppermute | solution.py:699
  134.2 3.1 %collective-permute-start.6 = (f32[16,128]{1,0:T(8,128)S(1)}, f32[16,128]{1,0:T(8,128)S(1)}, u32[]{:S(2)}, u32[]{:S(2)}) collective-permute-start(f32[16,128]{1,0:T(8,128)S(1)} %add.26), channel_id=1, source_target_pairs={{0,96},{8,104},{16,112},{24,120},{32,64},{40,72},{48,80},{56,88},{... | collective-permute-start | bytes 24584 | tf_op jit(solution)/shard_map/ppermute | solution.py:699
  137.3 1.8 %collective-permute-done.6 = f32[16,128]{1,0:T(8,128)S(1)} collective-permute-done((f32[16,128]{1,0:T(8,128)S(1)}, f32[16,128]{1,0:T(8,128)S(1)}, u32[]{:S(2)}, u32[]{:S(2)}) %collective-permute-start.6) | collective-permute-done | bytes 8224 | tf_op jit(solution)/shard_map/ppermute | solution.py:699
  139.1 1.7 %finish.1 = (f32[128,512]{1,0:T(8,128)}, f32[1,16,512]{2,1,0:T(8,128)}, f32[128,512]{1,0:T(8,128)}, f32[32,512]{1,0:T(8,128)}) custom-call(f32[16,128]{1,0:T(8,128)S(1)} %add.27.sums, f32[16,160,128]{2,1,0:T(8,128)S(1)} %all-to-all-done.5.owned), custom_call_target="tpu_custom_call" | custom-call | tf_op jit(solution)/shard_map/finish/pallas_call | solution.py:757
  (34 shorter events, 6.9 us)
Async XLA Ops:
  43.5 14.0 %all-to-all-start.1 = ((f32[8,88,128]{2,1,0:T(8,128)}), f32[8,88,128]{2,1,0:T(8,128)S(1)}, u32[]{:S(2)}, u32[]{:S(2)}) async-start(f32[8,88,128]{2,1,0:T(8,128)} %bitcast.2), calls=%async_computation.1 | async-start | bytes 720896 | tf_op jit(solution)/shard_map/all_to_all | solution.py:639
  56.3 1.3 copy-start.2
  57.5 14.3 %copy-start.6 = (s8[384,512]{1,0:T(32,128)(4,1)}, s8[384,512]{1,0:T(32,128)(4,1)S(1)}, u32[]{:S(2)}) copy-start(s8[384,512]{1,0:T(32,128)(4,1)S(1)} %get-tuple-element.80.cmp_1) | copy-start | bytes 589828
  57.6 14.4 %copy-start.8 = (s8[128,256]{1,0:T(32,128)(4,1)}, s8[128,256]{1,0:T(32,128)(4,1)S(1)}, u32[]{:S(2)}) copy-start(s8[128,256]{1,0:T(32,128)(4,1)S(1)} %get-tuple-element.82.rcv_1) | copy-start | bytes 98308
  58.4 13.5 %all-to-all-start.2 = ((f32[8,88,128]{2,1,0:T(8,128)}), f32[8,88,128]{2,1,0:T(8,128)S(1)}, u32[]{:S(2)}, u32[]{:S(2)}) async-start(f32[8,88,128]{2,1,0:T(8,128)} %bitcast.6), calls=%async_computation.2 | async-start | bytes 720896 | tf_op jit(solution)/shard_map/all_to_all | solution.py:639
  70.6 1.3 copy-start.4
  71.9 6.1 %copy-start.7 = (s8[384,512]{1,0:T(32,128)(4,1)}, s8[384,512]{1,0:T(32,128)(4,1)S(1)}, u32[]{:S(2)}) copy-start(s8[384,512]{1,0:T(32,128)(4,1)S(1)} %get-tuple-element.81.cmp_2) | copy-start | bytes 589828
  71.9 6.1 %copy-start.9 = (s8[128,256]{1,0:T(32,128)(4,1)}, s8[128,256]{1,0:T(32,128)(4,1)S(1)}, u32[]{:S(2)}) copy-start(s8[128,256]{1,0:T(32,128)(4,1)S(1)} %get-tuple-element.83.rcv_2) | copy-start | bytes 98308
  71.9 1.6 %copy-start.3 = (bf16[1024,896]{1,0:T(8,128)(2,1)S(1)}, bf16[1024,896]{1,0:T(8,128)(2,1)}, u32[]{:S(2)}) copy-start(bf16[1024,896]{1,0:T(8,128)(2,1)} %copy-done.2) | copy-start | bytes 5505028
  73.5 1.5 %copy-start.5 = (bf16[1024,896]{1,0:T(8,128)(2,1)S(1)}, bf16[1024,896]{1,0:T(8,128)(2,1)}, u32[]{:S(2)}) copy-start(bf16[1024,896]{1,0:T(8,128)(2,1)} %copy-done.4) | copy-start | bytes 5505028
  78.0 13.4 %all-to-all-start.3 = ((f32[8,88,128]{2,1,0:T(8,128)}), f32[8,88,128]{2,1,0:T(8,128)S(1)}, u32[]{:S(2)}, u32[]{:S(2)}) async-start(f32[8,88,128]{2,1,0:T(8,128)} %bitcast.8), calls=%async_computation.3 | async-start | bytes 720896 | tf_op jit(solution)/shard_map/all_to_all | solution.py:639
  92.1 12.0 %all-to-all-start.4 = ((f32[8,88,128]{2,1,0:T(8,128)}), f32[8,88,128]{2,1,0:T(8,128)S(1)}, u32[]{:S(2)}, u32[]{:S(2)}) async-start(f32[8,88,128]{2,1,0:T(8,128)} %bitcast.12), calls=%async_computation.4 | async-start | bytes 720896 | tf_op jit(solution)/shard_map/all_to_all | solution.py:639
  97.4 1.9 %copy-start = (bf16[2048,896]{1,0:T(8,128)(2,1)}, bf16[2048,896]{1,0:T(8,128)(2,1)S(1)}, u32[]{:S(2)}) copy-start(bf16[2048,896]{1,0:T(8,128)(2,1)S(1)} %get-tuple-element.91.wide) | copy-start | bytes 11010052
  105.2 33.9 %all-to-all-start.5 = ((f32[16,160,128]{2,1,0:T(8,128)}), f32[16,160,128]{2,1,0:T(8,128)S(1)}, u32[]{:S(2)}, u32[]{:S(2)}) async-start(f32[16,160,128]{2,1,0:T(8,128)} %pack_owned.3), calls=%async_computation.5 | async-start | bytes 2621440 | tf_op jit(solution)/shard_map/all_to_all | solution.py:639
  108.9 2.0 %copy-start.1 = (bf16[2048,896]{1,0:T(8,128)(2,1)S(1)}, bf16[2048,896]{1,0:T(8,128)(2,1)}, u32[]{:S(2)}) copy-start(bf16[2048,896]{1,0:T(8,128)(2,1)} %copy-done) | copy-start | bytes 11010052
  112.3 1.2 collective-permute-start
  113.5 3.5 %collective-permute-start.1 = (f32[1,128]{1,0:T(1,128)S(1)}, f32[1,128]{1,0:T(1,128)S(1)}, u32[]{:S(2)}, u32[]{:S(2)}) collective-permute-start(f32[1,128]{1,0:T(1,128)S(1)} %add.21), channel_id=1, source_target_pairs={{0,2},{1,3},{2,0},{3,1},{4,6},{5,7},{6,4},{7,5},{8,10},{9,11},{10,... | collective-permute-start | bytes 1544 | tf_op jit(solution)/shard_map/ppermute | solution.py:699
  117.0 4.8 %collective-permute-start.2 = (f32[1,128]{1,0:T(1,128)S(1)}, f32[1,128]{1,0:T(1,128)S(1)}, u32[]{:S(2)}, u32[]{:S(2)}) collective-permute-start(f32[1,128]{1,0:T(1,128)S(1)} %add.22), channel_id=1, source_target_pairs={{0,6},{1,7},{2,4},{3,5},{4,2},{5,3},{6,0},{7,1},{8,14},{9,15},{10,... | collective-permute-start | bytes 1544 | tf_op jit(solution)/shard_map/ppermute | solution.py:699
  121.9 3.7 %collective-permute-start.3 = (f32[16,128]{1,0:T(8,128)S(1)}, f32[16,128]{1,0:T(8,128)S(1)}, u32[]{:S(2)}, u32[]{:S(2)}) collective-permute-start(f32[16,128]{1,0:T(8,128)S(1)} %broadcast_select_fusion), channel_id=1, source_target_pairs={{0,8},{8,0},{16,24},{24,16},{32,40},{40,32},{48,56},{56,48},{64,72... | collective-permute-start | bytes 24584 | tf_op jit(solution)/shard_map/ppermute | solution.py:699
  125.6 4.9 %collective-permute-start.4 = (f32[16,128]{1,0:T(8,128)S(1)}, f32[16,128]{1,0:T(8,128)S(1)}, u32[]{:S(2)}, u32[]{:S(2)}) collective-permute-start(f32[16,128]{1,0:T(8,128)S(1)} %fusion), channel_id=1, source_target_pairs={{0,24},{8,16},{16,8},{24,0},{32,56},{40,48},{48,40},{56,32},{64,88... | collective-permute-start | bytes 24584 | tf_op jit(solution)/shard_map/ppermute | solution.py:699
  130.6 3.7 %collective-permute-start.5 = (f32[16,128]{1,0:T(8,128)S(1)}, f32[16,128]{1,0:T(8,128)S(1)}, u32[]{:S(2)}, u32[]{:S(2)}) collective-permute-start(f32[16,128]{1,0:T(8,128)S(1)} %fusion.1), channel_id=1, source_target_pairs={{0,32},{8,40},{16,48},{24,56},{32,0},{40,8},{48,16},{56,24},{64,96... | collective-permute-start | bytes 24584 | tf_op jit(solution)/shard_map/ppermute | solution.py:699
  134.2 4.9 %collective-permute-start.6 = (f32[16,128]{1,0:T(8,128)S(1)}, f32[16,128]{1,0:T(8,128)S(1)}, u32[]{:S(2)}, u32[]{:S(2)}) collective-permute-start(f32[16,128]{1,0:T(8,128)S(1)} %add.26), channel_id=1, source_target_pairs={{0,96},{8,104},{16,112},{24,120},{32,64},{40,72},{48,80},{56,88},{... | collective-permute-start | bytes 24584 | tf_op jit(solution)/shard_map/ppermute | solution.py:699

commit v2 on v1

--- a/solution.py
+++ b/solution.py
@@ -44,12 +44,14 @@
 INDEX_ROWS = 24
 DATA_ROWS = INDEX_AT + INDEX_ROWS
 STEPS = 2
+TRACE_PIECES = 10
+BASIS_PIECES = 16
 OWN_ROWS = 2 * SLICE + SLICE // 2
-PACK = LANES // CMP_G
 
 VMEM = pltpu.VMEM
 F32 = jnp.float32
 BF16 = jnp.bfloat16
+FP8 = jnp.float8_e4m3fn
 
 
 def fourier_rows():
@@ -130,14 +132,16 @@
     for copy in indices:
         copy.start()
     pieces = []
-    for k in range(TRACE_TILES):
-        span = slice(k * LANES, (k + 1) * LANES)
+    for k in range(TRACE_PIECES):
+        size = TR_DEV // TRACE_PIECES
+        span = slice(k * size, (k + 1) * size)
         pieces.append((traces.at[span], own.at[span]))
-    size = 2 * FREQS // STEPS // 2
-    for k in range(2 * STEPS):
+    for k in range(BASIS_PIECES):
+        size = 2 * FREQS // BASIS_PIECES
         span = slice(k * size, (k + 1) * size)
         pieces.append((waves.at[span], basis.at[span]))
     copies = [pltpu.make_async_copy(a, b, sems.at[k]) for k, (a, b) in enumerate(pieces)]
+    early = TRACE_PIECES + BASIS_PIECES // STEPS
     for copy in copies:
         copy.start()
     for copy in indices:
@@ -148,12 +152,13 @@
     extra[N_SHOT:] = index_tiles(send_rows, send_counts, src, rcv, off)
     for part in range(N_SHOT):
         out[part, BINS_AT:, :] = extra[...]
-    for copy in copies[:TRACE_TILES]:
+    for copy in copies[:early]:
         copy.wait()
     half = FREQS // STEPS
     for step in range(STEPS):
-        for copy in copies[TRACE_TILES + 2 * step : TRACE_TILES + 2 * step + 2]:
-            copy.wait()
+        if step == 1:
+            for copy in copies[early:]:
+                copy.wait()
         parts = nt_dot(basis[2 * half * step : 2 * half * (step + 1)], own[...])
         logs = jnp.log1p(parts[:half] * parts[:half] + parts[half:] * parts[half:])
         for part in range(half // SLICE):
@@ -175,7 +180,7 @@
         ]
         + [VMEM(array.shape, jnp.int32) for array in small]
         + [
-            pltpu.SemaphoreType.DMA((TRACE_TILES + 2 * STEPS,)),
+            pltpu.SemaphoreType.DMA((TRACE_PIECES + BASIS_PIECES,)),
             pltpu.SemaphoreType.DMA((len(small),)),
         ],
         compiler_params=params(24),
@@ -197,7 +202,8 @@
         first = 0
         for row, size, base in ((0, SRC_G, 0), (2, 128, 0), (1, RCV_G, 0), (3, 256, 0), (3, 256, 256)):
             wanted = (values[4 * q + row : 4 * q + row + 1] - base).astype(BF16)
-            hot[first : first + size, span] = jnp.where(ids[:size] == wanted, one, zero)
+            hits = jnp.where(ids[:size] == wanted, one, zero)
+            hot[first : first + size, span] = hits.astype(hot.dtype)
             first += size
 
 
@@ -274,16 +280,12 @@
 
 
 def kept_part(counts):
-    return (counts.astype(jnp.int32) & (EXACT - 1)).astype(jnp.int8)
+    return (counts.astype(jnp.int32) & (EXACT - 1)).astype(F32).astype(BF16)
 
 
 def left_over(counts):
     whole = counts.astype(jnp.int32)
     return (whole - (whole & (EXACT - 1))).astype(F32).astype(BF16)
-
-
-def widen(counts):
-    return counts.astype(F32).astype(BF16)
 
 
 def peak(counts):
@@ -303,7 +305,7 @@
 
 
 def count_kernel(
-    index, wide, kept, to_cmp_kept, to_rcv_kept, most, diag, hot_even, hot_odd, ids, to_cmp, to_rcv, *, first
+    index, kept, to_cmp_kept, to_rcv_kept, most, diag, hot_even, hot_odd, ids, to_cmp, to_rcv, *, first
 ):
     step = pl.program_id(0)
     even = first + 2 * step
@@ -322,10 +324,7 @@
         to_cmp[...] += cmp_counts
         to_rcv[...] += rcv_counts
         diag[...] += jnp.sum(rows, axis=0, keepdims=True)
-        part = rows.astype(jnp.int32) & (EXACT - 1)
-        span = slice(place * SRC_G, (place + 1) * SRC_G)
-        kept[span] = part.astype(jnp.int8)
-        wide[span] = part.astype(F32).astype(BF16)
+        kept[place * SRC_G : (place + 1) * SRC_G] = kept_part(rows)
         most[...] = jnp.maximum(most[...], peak(rows))
 
     fill_hot(index[even + 1], ids, hot_odd)
@@ -361,24 +360,31 @@
             use_both(left_over(to_cmp[...]), left_over(to_rcv[...]))
 
 
-def widen_kernel(kept_1, kept_2, cmp_1, cmp_2, rcv_1, rcv_2, wide, to_cmp, to_rcv, held, small_cmp, small_rcv, sems):
+def fetch_counts(refs, held, held_cmp, held_rcv, sems):
+    first, last, cmp_1, cmp_2, rcv_1, rcv_2 = refs
     pieces = []
-    for chunk in range(CHUNKS):
-        source = kept_1 if chunk < CHUNKS // 2 else kept_2
-        start = chunk % (CHUNKS // 2) * CHUNK_ROWS
-        pieces.append((source.at[start : start + CHUNK_ROWS], held.at[chunk]))
-    pieces += [(cmp_1, small_cmp.at[0]), (cmp_2, small_cmp.at[1])]
-    pieces += [(rcv_1, small_rcv.at[0]), (rcv_2, small_rcv.at[1])]
+    for block in range(N_SHOT):
+        source = first if block < HALF else last
+        start = block % HALF * SRC_G
+        place = block * SRC_G
+        pieces.append((source.at[start : start + SRC_G], held.at[place : place + SRC_G]))
+    pieces += [(cmp_1, held_cmp.at[0]), (cmp_2, held_cmp.at[1])]
+    pieces += [(rcv_1, held_rcv.at[0]), (rcv_2, held_rcv.at[1])]
     copies = [pltpu.make_async_copy(a, b, sems.at[k]) for k, (a, b) in enumerate(pieces)]
     for copy in copies:
         copy.start()
-    for chunk in range(CHUNKS):
-        copies[chunk].wait()
-        wide[chunk * CHUNK_ROWS : (chunk + 1) * CHUNK_ROWS] = widen(held[chunk])
-    for copy in copies[CHUNKS:]:
+    return copies
+
+
+def wait_chunk(copies, chunk):
+    blocks = N_SHOT // CHUNKS
+    for copy in copies[chunk * blocks : (chunk + 1) * blocks]:
         copy.wait()
-    to_cmp[...] = (small_cmp[0].astype(F32) + small_cmp[1].astype(F32)).astype(BF16)
-    to_rcv[...] = (small_rcv[0].astype(F32) + small_rcv[1].astype(F32)).astype(BF16)
+    return slice(chunk * CHUNK_ROWS, (chunk + 1) * CHUNK_ROWS)
+
+
+def sum_halves(held):
+    return (held[0].astype(F32) + held[1].astype(F32)).astype(BF16)
 
 
 def load_halves(tab, rcv, own, shared):
@@ -393,18 +399,21 @@
 
 
 def normal_kernel(
-    tab_in, rcv_in, first, last, cmp_1, cmp_2, rcv_1, rcv_2, diag_1, diag_2, most_1, most_2, index,
-    tab, rcv, own_count, own, shared, to_shared, to_own, hot, ids, exact_cmp, exact_rcv,
+    first, last, cmp_1, cmp_2, rcv_1, rcv_2, tab_in, rcv_in, diag_1, diag_2, most_1, most_2, index,
+    tab, rcv, own_count, own, shared, to_shared, to_own,
+    held, held_cmp, held_rcv, sems, hot, ids, exact_cmp, exact_rcv,
 ):
+    counts = (first, last, cmp_1, cmp_2, rcv_1, rcv_2)
+    copies = fetch_counts(counts, held, held_cmp, held_rcv, sems)
     top = 2 * SLICE
-    half = HALF * SRC_G
     load_halves(tab_in, rcv_in, own, shared)
     lanes = lax.broadcasted_iota(jnp.int32, (16, SHARED), 1)
     shared[top:] = jnp.where(lanes < LANES, 1.0, 0.0).astype(BF16)
-    sums = jnp.dot(own[:, :half], first[...], preferred_element_type=F32)
-    to_shared[...] = sums + jnp.dot(own[:, half:], last[...], preferred_element_type=F32)
-    to_own[:, :half] = nt_dot(shared[...], first[...])
-    to_own[:, half:] = nt_dot(shared[...], last[...])
+    for chunk in range(CHUNKS):
+        span = wait_chunk(copies, chunk)
+        sums = jnp.dot(own[:, span], held[span], preferred_element_type=F32)
+        to_shared[...] = sums if chunk == 0 else to_shared[...] + sums
+        to_own[:, span] = nt_dot(shared[...], held[span])
 
     def others(to_cmp, to_rcv):
         cmp_sums = jnp.dot(shared[:top, :OR], to_cmp, preferred_element_type=F32)
@@ -419,10 +428,9 @@
         to_shared[...] += jnp.dot(own[:, span], rows, preferred_element_type=F32)
         to_own[:, span] += nt_dot(shared[...], rows)
 
-    def both_of(one, other):
-        return (one[...].astype(F32) + other[...].astype(F32)).astype(BF16)
-
-    others(both_of(cmp_1, cmp_2), both_of(rcv_1, rcv_2))
+    for copy in copies[N_SHOT:]:
+        copy.wait()
+    others(sum_halves(held_cmp), sum_halves(held_rcv))
     add_left_over(most_1, most_2, index, hot, ids, exact_cmp, exact_rcv, others, use_rows)
     diag = diag_1[...] + diag_2[...]
     for tile in range(N_SHOT):
@@ -453,9 +461,13 @@
 
 
 def norm_kernel(
-    tab_b, rcv_b, tab_y, rcv_y, wide, cmp_counts, rcv_counts, diag_1, diag_2, most_1, most_2, index, own_count,
-    out, tab_z, rcv_z, own, shared, to_shared, hot, ids, exact_cmp, exact_rcv,
+    first, last, cmp_1, cmp_2, rcv_1, rcv_2,
+    tab_b, rcv_b, tab_y, rcv_y, diag_1, diag_2, most_1, most_2, index, own_count,
+    out, tab_z, rcv_z, own, shared, to_shared,
+    held, held_cmp, held_rcv, sems, hot, ids, exact_cmp, exact_rcv,
 ):
+    counts = (first, last, cmp_1, cmp_2, rcv_1, rcv_2)
+    copies = fetch_counts(counts, held, held_cmp, held_rcv, sems)
     shared_b = tab_b[:LIVE_ROWS]
     shared_y = tab_y[:LIVE_ROWS]
     shift = all_sum(shared_b * shared_y) / all_sum(shared_b * shared_b)
@@ -465,7 +477,10 @@
     tab_z[...] = shared_z
     rcv_z[...] = own_z
     load_halves(tab_z, rcv_z, own, shared)
-    to_shared[...] = jnp.dot(own[...], wide[...], preferred_element_type=F32)
+    for chunk in range(CHUNKS):
+        span = wait_chunk(copies, chunk)
+        sums = jnp.dot(own[:, span], held[span], preferred_element_type=F32)
+        to_shared[...] = sums if chunk == 0 else to_shared[...] + sums
 
     def whole(tabs, own):
         return all_sum(tabs) * (1.0 / N_RCV) + all_sum(own)
@@ -480,7 +495,9 @@
         span = pl.ds(pl.multiple_of(block * SRC_G, SRC_G), SRC_G)
         to_shared[...] += jnp.dot(own[:, span], rows, preferred_element_type=F32)
 
-    others(cmp_counts[...], rcv_counts[...])
+    for copy in copies[N_SHOT:]:
+        copy.wait()
+    others(sum_halves(held_cmp), sum_halves(held_rcv))
     add_left_over(most_1, most_2, index, hot, ids, exact_cmp, exact_rcv, others, use_rows)
     tiles = [tab_z[at(OFF_TILE)]] + [rcv_z[tile] for tile in range(RCV_TILES)]
     tiles += [tab_z[at(tile)] for tile in range(CMP_TILE, LIVE_TILES)]
@@ -518,7 +535,7 @@
 
 
 def hot_scratch():
-    return [VMEM((ROWS, TR_DEV), BF16), VMEM((256, LANES), BF16)]
+    return [VMEM((ROWS, TR_DEV), FP8), VMEM((256, LANES), BF16)]
 
 
 def adjoint_apply(data):
@@ -545,16 +562,15 @@
         functools.partial(count_kernel, first=first),
         grid=(COUNT_STEPS,),
         in_specs=[whole_spec(*INDEX)],
-        out_specs=[rows, rows] + small,
+        out_specs=[rows] + small,
         out_shape=[
-            jax.ShapeDtypeStruct(COUNTS, BF16),
-            pltpu.HBM(COUNTS, jnp.int8),
-            jax.ShapeDtypeStruct(TO_CMP, jnp.int8),
-            jax.ShapeDtypeStruct(TO_RCV, jnp.int8),
+            pltpu.HBM(COUNTS, BF16),
+            pltpu.HBM(TO_CMP, BF16),
+            pltpu.HBM(TO_RCV, BF16),
             jax.ShapeDtypeStruct((1, LANES), F32),
             jax.ShapeDtypeStruct((1, SHARED), F32),
         ],
-        scratch_shapes=[VMEM((ROWS, TR_DEV), BF16)] * 2
+        scratch_shapes=[VMEM((ROWS, TR_DEV), FP8)] * 2
         + [VMEM((256, LANES), BF16), VMEM(TO_CMP, F32), VMEM(TO_RCV, F32)],
         compiler_params=params(24),
         cost_estimate=cost(6),
@@ -562,15 +578,30 @@
     )(index)
 
 
-def exact_scratch():
-    return hot_scratch() + [VMEM(TO_CMP, F32), VMEM(TO_RCV, F32)]
-
-
-def normal_apply(tab, rcv, index, counts_1, counts_2):
-    wide_1, _, cmp_1, rcv_1, most_1, diag_1 = counts_1
-    wide_2, _, cmp_2, rcv_2, most_2, diag_2 = counts_2
+def count_scratch():
+    return (
+        [
+            VMEM((N_SHOT * SRC_G, SHARED), BF16),
+            VMEM((2,) + TO_CMP, BF16),
+            VMEM((2,) + TO_RCV, BF16),
+            pltpu.SemaphoreType.DMA((N_SHOT + 4,)),
+        ]
+        + hot_scratch()
+        + [VMEM(TO_CMP, F32), VMEM(TO_RCV, F32)]
+    )
+
+
+def count_operands(counts):
+    big = in_hbm(*[array for pair in zip(counts[0][:3], counts[1][:3]) for array in pair])
+    (most_1, diag_1), (most_2, diag_2) = counts[0][3:], counts[1][3:]
+    return big, [diag_1, diag_2, most_1, most_2]
+
+
+def normal_apply(tab, rcv, index, counts):
+    big, small = count_operands(counts)
     return pl.pallas_call(
         normal_kernel,
+        in_specs=[ANYWHERE] * 6 + [IN_VMEM] * 7,
         out_shape=table_shapes() + [jax.ShapeDtypeStruct((N_SHOT, LANES), F32)],
         scratch_shapes=[
             VMEM((2 * SLICE, N_SHOT * SRC_G), BF16),
@@ -578,40 +609,18 @@
             VMEM((2 * SLICE, SHARED), F32),
             VMEM((2 * SLICE + 16, N_SHOT * SRC_G), F32),
         ]
-        + exact_scratch(),
-        compiler_params=params(20),
+        + count_scratch(),
+        compiler_params=params(24),
         cost_estimate=cost(3),
         name="normal_apply",
-    )(tab, rcv, wide_1, wide_2, cmp_1, cmp_2, rcv_1, rcv_2, diag_1, diag_2, most_1, most_2, index)
-
-
-def widen_counts(kept_1, kept_2):
-    operands = [array for pair in zip(kept_1, kept_2) for array in pair]
-    return pl.pallas_call(
-        widen_kernel,
-        in_specs=[ANYWHERE] * 6,
-        out_shape=[
-            jax.ShapeDtypeStruct((N_SHOT * SRC_G, SHARED), BF16),
-            jax.ShapeDtypeStruct(TO_CMP, BF16),
-            jax.ShapeDtypeStruct(TO_RCV, BF16),
-        ],
-        scratch_shapes=[
-            VMEM((CHUNKS, CHUNK_ROWS, SHARED), jnp.int8),
-            VMEM((2,) + TO_CMP, jnp.int8),
-            VMEM((2,) + TO_RCV, jnp.int8),
-            pltpu.SemaphoreType.DMA((CHUNKS + 4,)),
-        ],
-        compiler_params=params(20),
-        cost_estimate=cost(3),
-        name="widen_counts",
-    )(*in_hbm(*operands))
-
-
-def norm_sums(tab_b, rcv_b, tab_y, rcv_y, own_count, index, wide, counts_1, counts_2):
-    most_1, diag_1 = counts_1[4:]
-    most_2, diag_2 = counts_2[4:]
+    )(*big, tab, rcv, *small, index)
+
+
+def norm_sums(tab_b, rcv_b, tab_y, rcv_y, own_count, index, counts):
+    big, small = count_operands(counts)
     return pl.pallas_call(
         norm_kernel,
+        in_specs=[ANYWHERE] * 6 + [IN_VMEM] * 10,
         out_shape=jax.ShapeDtypeStruct((1, LANES), F32),
         scratch_shapes=[
             VMEM((LIVE_ROWS, LANES), F32),
@@ -620,11 +629,11 @@
             VMEM((2 * SLICE, SHARED), BF16),
             VMEM((2 * SLICE, SHARED), F32),
         ]
-        + exact_scratch(),
-        compiler_params=params(20),
+        + count_scratch(),
+        compiler_params=params(24),
         cost_estimate=cost(2),
         name="norm_sums",
-    )(tab_b, rcv_b, tab_y, rcv_y, *wide, diag_1, diag_2, most_1, most_2, index, own_count)
+    )(*big, tab_b, rcv_b, tab_y, rcv_y, *small, index, own_count)
 
 
 def spread_kernel(parts, out):
@@ -667,12 +676,9 @@
         both = jnp.where(lanes < CMP_G, cmp_part, rcv_part)
         moved = pltpu.roll(both[half:], LANES // 2, 1)
         rows[dest, 2 * SLICE :] = jnp.where(lanes[:half] < LANES // 2, both[:half], moved)
-        if dest % PACK == PACK - 1:
-            group = dest // PACK
-            span = slice(group * PACK, (group + 1) * PACK)
-            place = out.at[span, first : first + OWN_ROWS]
-            copies.append(pltpu.make_async_copy(rows.at[span], place, sems.at[group]))
-            copies[-1].start()
+        place = out.at[dest, first : first + OWN_ROWS]
+        copies.append(pltpu.make_async_copy(rows.at[dest], place, sems.at[dest]))
+        copies[-1].start()
     for copy in copies:
         copy.wait()
 
@@ -686,7 +692,7 @@
         out_shape=pltpu.HBM((N_SHOT, 2 * OWN_ROWS, LANES), F32),
         scratch_shapes=[
             VMEM((N_SHOT, OWN_ROWS, LANES), F32),
-            pltpu.SemaphoreType.DMA((N_SHOT // PACK,)),
+            pltpu.SemaphoreType.DMA((N_SHOT,)),
         ],
         input_output_aliases={2: 0} if given else {},
         compiler_params=params(24),
@@ -709,7 +715,7 @@
     return rows
 
 
-def finish_kernel(sums, owned, source, receiver, offset, cmp):
+def finish_kernel(sums, owned, source, receiver, offset, cmp, done_so, done_rest, sems):
     rows = sums[...]
     norm_b, cross, norm_z, norm_az, shift = (rows[:, lane : lane + 1] for lane in range(5))
     shift = shift * (1.0 / N_RCV)
@@ -739,30 +745,47 @@
         return jnp.concatenate([tile, pltpu.roll(tile, LANES // 2, 1)], axis=0)
 
     per_tile = LANES // SLICE
+    rcv_rows = RCV_G // N_SHOT
+    copies = []
+
+    def write(block, target):
+        copies.append(pltpu.make_async_copy(block, target, sems.at[len(copies)]))
+        copies[-1].start()
+
     for group in range(N_SHOT // per_tile):
         span = slice(group * LANES, (group + 1) * LANES)
         senders = range(group * per_tile, (group + 1) * per_tile)
-        source[:, span] = jnp.concatenate([combine(i, 0, SLICE) for i in senders], axis=0).T
-        offset[:, span] = jnp.concatenate(
-            [combine(i, SLICE, 2 * SLICE) for i in senders], axis=0
-        ).T
-        rest = jnp.concatenate(
-            [spread_halves(combine(i, 2 * SLICE, OWN_ROWS)) for i in senders], axis=0
-        ).T
-        cmp[:, span] = rest[:CMP_G]
-        receiver[0, :, span] = rest[CMP_G : CMP_G + RCV_G // N_SHOT]
+        for place, target in enumerate((source, offset)):
+            start = place * SLICE
+            table = [combine(i, start, start + SLICE) for i in senders]
+            done_so[place, group] = jnp.concatenate(table, axis=0).T
+            write(done_so.at[place, group], target.at[:, span])
+        rest = [spread_halves(combine(i, 2 * SLICE, OWN_ROWS)) for i in senders]
+        done_rest[group] = jnp.concatenate(rest, axis=0).T
+        write(done_rest.at[group, :CMP_G], cmp.at[:, span])
+        write(done_rest.at[group, CMP_G : CMP_G + rcv_rows], receiver.at[0, :, span])
+    for copy in copies:
+        copy.wait()
 
 
 def finish(sums, owned):
+    groups = FREQS // LANES
     return pl.pallas_call(
         finish_kernel,
+        in_specs=[IN_VMEM] * 2,
+        out_specs=[ANYWHERE] * 4,
         out_shape=[
             jax.ShapeDtypeStruct((SRC_G, FREQS), F32),
             jax.ShapeDtypeStruct((1, RCV_G // N_SHOT, FREQS), F32),
             jax.ShapeDtypeStruct((128, FREQS), F32),
             jax.ShapeDtypeStruct((CMP_G, FREQS), F32),
         ],
-        compiler_params=params(),
+        scratch_shapes=[
+            VMEM((2, groups, LANES, LANES), F32),
+            VMEM((groups, LANES, LANES), F32),
+            pltpu.SemaphoreType.DMA((4 * groups,)),
+        ],
+        compiler_params=params(24),
         name="finish",
     )(sums, owned)
 
@@ -782,20 +805,15 @@
     tab_b = exchange(spread, "rcv")
     counts = (counts_1, count_call(index, HALF))
 
-    tab_y, rcv_y, own_count = normal_apply(tab_b, rcv_b, index, *counts)
+    tab_y, rcv_y, own_count = normal_apply(tab_b, rcv_b, index, counts)
     arrived = exchange(tab_y, "rcv")
     packed = pack_owned(tab_b, rcv_b)
     arrived, packed = lax.optimization_barrier((arrived, packed))
-    spread = spread_shares(arrived)
-    kept = [counts_half[1:4] for counts_half in counts]
-    spread, kept = lax.optimization_barrier((spread, kept))
-    tab_y = exchange(spread, "rcv")
-    wide = widen_counts(*kept)
-    tab_y, wide = lax.optimization_barrier((tab_y, wide))
+    tab_y = exchange(spread_shares(arrived), "rcv")
     packed = pack_owned(tab_y, rcv_y, packed)
     tab_y, packed = lax.optimization_barrier((tab_y, packed))
     owned = exchange(packed, "shot")
-    sums = norm_sums(tab_b, rcv_b, tab_y, rcv_y, own_count, index, wide, *counts)
+    sums = norm_sums(tab_b, rcv_b, tab_y, rcv_y, own_count, index, counts)
     return tuple(finish(gather_sums(sums), owned))
 
 

time: 142 us -> 136 us (0.958)
  blocking collectives: 30.4 us -> 41.4 us
  local copies, waits for them, and re-layouts: 9.52 us -> 0 us
  starting transfers between devices: 33.7 us -> 27.7 us
  Pallas kernels: 38.9 us -> 36.5 us
    all_to_all x1 -> x2, blocking collectives: 30.4 us -> 41.4 us  [exchange(): return lax.all_to_all(array, axis, split_axis=0, concat_axis=0, tiled=True)]
    unnamed x20 -> x0, local copies, waits for them, and re-layouts: 9.52 us -> none
    all_to_all x5 -> x4, starting transfers between devices: 22 us -> 16.1 us  [exchange(): return lax.all_to_all(array, axis, split_axis=0, concat_axis=0, tiled=True)]
    pallas_call x2, Pallas kernels: 14.9 us -> 10.7 us  [count_call(): pl.pallas_call(functools.partial(count_kernel, first=first), grid=(COUNT_...]
    pallas_call x4 -> x3, Pallas kernels: 7.82 us -> 9.91 us  [the longest x1 4.89 us: normal_apply(): pl.pallas_call(normal_kernel, in_specs=[ANYWHERE] * 6 + [IN_VMEM] * 7, ou...]
    all_to_all x5 -> x4, waiting for transfers between devices: 12.4 us -> 13.8 us  [exchange(): return lax.all_to_all(array, axis, split_axis=0, concat_axis=0, tiled=True)]
  transfers between devices with their start and end apart: 12 -> 11, of which waited for: 9 -> 10; matrix products, arithmetic and copies ran while one was open for 0% -> 0% of each run, Pallas kernels for 14% -> 11%
where the time goes in v2:
time: 136 us; the launch traced here: 135 us
  blocking collectives  41.4 us (30%)
  Pallas kernels  36.5 us (27%)
  waiting for transfers between devices  28.7 us (21%)
  starting transfers between devices  27.7 us (20%)
    all_to_all x2, blocking collectives, exchange(): return lax.all_to_all(array, axis, split_axis=0, concat_axis=0, tiled=True)  41.4 us
    all_to_all x4, starting transfers between devices, exchange(): return lax.all_to_all(array, axis, split_axis=0, concat_axis=0, tiled=True)  16.1 us
    ppermute x7, waiting for transfers between devices, swapped(): return lax.ppermute(value, axis, [(s, s ^ bit) for s in range(size)])  14.9 us
    all_to_all x4, waiting for transfers between devices, exchange(): return lax.all_to_all(array, axis, split_axis=0, concat_axis=0, tiled=True)  13.8 us
    ppermute x7, starting transfers between devices, swapped(): return lax.ppermute(value, axis, [(s, s ^ bit) for s in range(size)])  11.6 us
    pallas_call x2, Pallas kernels, count_call(): pl.pallas_call(functools.partial(count_kernel, first=first), grid=(COUNT_...  10.7 us
    pallas_call x1, Pallas kernels, adjoint_apply(): pl.pallas_call(adjoint_kernel, out_shape=table_shapes() + [jax.ShapeDtype...  7.47 us
    pallas_call x1, Pallas kernels, log_spectra(): pl.pallas_call(spectra_kernel, in_specs=[ANYWHERE] * (2 + len(small)), ou...  5.37 us
  transfers between devices with their start and end apart: 11, of which 10 were waited for; matrix products, arithmetic and copies ran while one was open for 0% of the time, Pallas kernels for 11%

profile of v2, /device:TPU:0, one launch (start us, length us, event | category | flops | bytes accessed | tf_op | source)
XLA Modules:
  0.0 135.5 jit_solution(8674703905323830535)
XLA Ops:
  0.6 5.4 %spectra.1 = f32[16,200,128]{2,1,0:T(8,128)S(1)} custom-call(bf16[640,1024]{1,0:T(8,128)(2,1)} %traces.1, bf16[1024,1024]{1,0:T(8,128)(2,1)} %constant.10.clone.waves, s32[16,80]{1,0:T(8,128)} %bitcast.19, s32[1,16]{1,0:T(1,128)} %refs_1_.1, s32[16,80]{1,0:T(8,128)} %bitcast.20, s32[640]{0:T(1024)} %refs_3_.1, s32[640]{0:T(1024)} %refs_4_.1, s32[640]{0:T(1024)} %refs_5_.1), custom_call_target="tpu_custom_call" | custom-call | flops 5000000000 | bytes 15000000 | tf_op jit(solution)/shard_map/spectra/pallas_call | solution.py:172
  6.0 30.4 %all_to_all.53.data = f32[16,200,128]{2,1,0:T(8,128)S(1)} all-to-all(f32[16,200,128]{2,1,0:T(8,128)S(1)} %spectra.1), channel_id=1, replica_groups=mesh['shot'=16,'rcv'=8] {'shot'}, dimensions={0} | all-to-all | bytes 3276800 | tf_op jit(solution)/shard_map/all_to_all | solution.py:648
  36.4 7.5 %adjoint_apply.1 = (f32[704,128]{1,0:T(8,128)}, f32[2,32,128]{2,1,0:T(8,128)S(1)}, s32[16,24,128]{2,1,0:T(8,128)S(1)}) custom-call(f32[16,200,128]{2,1,0:T(8,128)S(1)} %all_to_all.53.data), custom_call_target="tpu_custom_call" | custom-call | flops 8000000000 | bytes 24000000 | tf_op jit(solution)/shard_map/adjoint_apply/pallas_call | solution.py:542
  43.9 5.3 %all-to-all-start.1 = ((f32[8,88,128]{2,1,0:T(8,128)}), f32[8,88,128]{2,1,0:T(8,128)S(1)}, u32[]{:S(2)}, u32[]{:S(2)}) async-start(f32[8,88,128]{2,1,0:T(8,128)} %bitcast.2), calls=%async_computation.1 | async-start | bytes 720896 | tf_op jit(solution)/shard_map/all_to_all | solution.py:648
  49.2 5.3 %count_pairs.2 = (bf16[1024,896]{1,0:T(8,128)(2,1)}, bf16[384,512]{1,0:T(8,128)(2,1)}, bf16[128,256]{1,0:T(8,128)(2,1)}, f32[1,128]{1,0:T(1,128)S(1)}, f32[1,896]{1,0:T(1,128)S(1)}) custom-call(s32[16,24,128]{2,1,0:T(8,128)S(1)} %get-tuple-element.43.index), custom_call_target="tpu_custom_call" | custom-call | flops 6000000000 | bytes 18000000 | tf_op jit(solution)/shard_map/count_pairs/pallas_call | solution.py:561
  54.5 3.3 %all-to-all-done.1 = f32[8,88,128]{2,1,0:T(8,128)S(1)} async-done(((f32[8,88,128]{2,1,0:T(8,128)}), f32[8,88,128]{2,1,0:T(8,128)S(1)}, u32[]{:S(2)}, u32[]{:S(2)}) %all-to-all-start.1) | async-done | bytes 360480 | tf_op jit(solution)/shard_map/all_to_all | solution.py:648
  57.8 0.8 sum_shares.2
  58.6 3.4 %all-to-all-start.2 = ((f32[8,88,128]{2,1,0:T(8,128)}), f32[8,88,128]{2,1,0:T(8,128)S(1)}, u32[]{:S(2)}, u32[]{:S(2)}) async-start(f32[8,88,128]{2,1,0:T(8,128)} %bitcast.6), calls=%async_computation.2 | async-start | bytes 720896 | tf_op jit(solution)/shard_map/all_to_all | solution.py:648
  62.0 5.4 %count_pairs.3 = (bf16[1024,896]{1,0:T(8,128)(2,1)}, bf16[384,512]{1,0:T(8,128)(2,1)}, bf16[128,256]{1,0:T(8,128)(2,1)}, f32[1,128]{1,0:T(1,128)S(1)}, f32[1,896]{1,0:T(1,128)S(1)}) custom-call(s32[16,24,128]{2,1,0:T(8,128)S(1)} %get-tuple-element.43.index), custom_call_target="tpu_custom_call" | custom-call | flops 6000000000 | bytes 18000000 | tf_op jit(solution)/shard_map/count_pairs/pallas_call | solution.py:561
  67.4 3.1 %all-to-all-done.2 = f32[8,88,128]{2,1,0:T(8,128)S(1)} async-done(((f32[8,88,128]{2,1,0:T(8,128)}), f32[8,88,128]{2,1,0:T(8,128)S(1)}, u32[]{:S(2)}, u32[]{:S(2)}) %all-to-all-start.2) | async-done | bytes 360480 | tf_op jit(solution)/shard_map/all_to_all | solution.py:648
  70.5 4.9 %normal_apply.1 = (f32[704,128]{1,0:T(8,128)}, f32[2,32,128]{2,1,0:T(8,128)S(1)}, f32[16,128]{1,0:T(8,128)S(1)}) custom-call(bf16[1024,896]{1,0:T(8,128)(2,1)} %get-tuple-element.40.first, bf16[1024,896]{1,0:T(8,128)(2,1)} %get-tuple-element.44.last, bf16[384,512]{1,0:T(8,128)(2,1)} %get-tuple-element.45.cmp_1, bf16[384,512]{1,0:T(8,128)(2,1)} %get-tuple-element.46.cmp_2, ...), custom_call_target="tpu_custom_call" | custom-call | flops 3000000000 | bytes 9000000 | tf_op jit(solution)/shard_map/normal_apply/pallas_call | solution.py:602
  75.4 3.5 %all-to-all-start.3 = ((f32[8,88,128]{2,1,0:T(8,128)}), f32[8,88,128]{2,1,0:T(8,128)S(1)}, u32[]{:S(2)}, u32[]{:S(2)}) async-start(f32[8,88,128]{2,1,0:T(8,128)} %bitcast.8), calls=%async_computation.3 | async-start | bytes 720896 | tf_op jit(solution)/shard_map/all_to_all | solution.py:648
  78.9 1.1 pack_owned.2.refs_0_
  80.0 7.4 %all-to-all-done.3 = f32[8,88,128]{2,1,0:T(8,128)S(1)} async-done(((f32[8,88,128]{2,1,0:T(8,128)}), f32[8,88,128]{2,1,0:T(8,128)S(1)}, u32[]{:S(2)}, u32[]{:S(2)}) %all-to-all-start.3) | async-done | bytes 360480 | tf_op jit(solution)/shard_map/all_to_all | solution.py:648
  87.4 11.0 %all_to_all.54 = f32[8,88,128]{2,1,0:T(8,128)S(1)} all-to-all(f32[8,88,128]{2,1,0:T(8,128)S(1)} %sum_shares.3), channel_id=1, replica_groups=mesh['shot'=16,'rcv'=8] {'rcv'}, dimensions={0} | all-to-all | bytes 720896 | tf_op jit(solution)/shard_map/all_to_all | solution.py:648
  98.4 1.1 pack_owned.3
  99.6 3.9 %all-to-all-start.5 = ((f32[16,160,128]{2,1,0:T(8,128)}), f32[16,160,128]{2,1,0:T(8,128)S(1)}, u32[]{:S(2)}, u32[]{:S(2)}) async-start(f32[16,160,128]{2,1,0:T(8,128)} %pack_owned.3), calls=%async_computation.5 | async-start | bytes 2621440 | tf_op jit(solution)/shard_map/all_to_all | solution.py:648
  103.5 3.3 %norm_sums.1 = f32[1,128]{1,0:T(1,128)S(1)} custom-call(bf16[1024,896]{1,0:T(8,128)(2,1)} %get-tuple-element.40.first, bf16[1024,896]{1,0:T(8,128)(2,1)} %get-tuple-element.44.last, bf16[384,512]{1,0:T(8,128)(2,1)} %get-tuple-element.45.cmp_1, bf16[384,512]{1,0:T(8,128)(2,1)} %get-tuple-element.46.cmp_2, bf16[128,256]{1,0:T(8,128)(2,1)} %get-tuple-element.47.rcv_1, ...), custom_call_target="tpu_custom_call" | custom-call | flops 2000000000 | bytes 6000000 | tf_op jit(solution)/shard_map/norm_sums/pallas_call | solution.py:621
  106.9 1.1 collective-permute-done
  108.0 0.6 collective-permute-start.1
  108.6 3.0 %collective-permute-done.1 = f32[1,128]{1,0:T(1,128)S(1)} collective-permute-done((f32[1,128]{1,0:T(1,128)S(1)}, f32[1,128]{1,0:T(1,128)S(1)}, u32[]{:S(2)}, u32[]{:S(2)}) %collective-permute-start.1) | collective-permute-done | bytes 544 | tf_op jit(solution)/shard_map/ppermute | solution.py:705
  111.5 1.2 collective-permute-start.2
  112.7 3.6 %collective-permute-done.2 = f32[1,128]{1,0:T(1,128)S(1)} collective-permute-done((f32[1,128]{1,0:T(1,128)S(1)}, f32[1,128]{1,0:T(1,128)S(1)}, u32[]{:S(2)}, u32[]{:S(2)}) %collective-permute-start.2) | collective-permute-done | bytes 544 | tf_op jit(solution)/shard_map/ppermute | solution.py:705
  116.4 1.8 %collective-permute-start.3 = (f32[16,128]{1,0:T(8,128)S(1)}, f32[16,128]{1,0:T(8,128)S(1)}, u32[]{:S(2)}, u32[]{:S(2)}) collective-permute-start(f32[16,128]{1,0:T(8,128)S(1)} %broadcast_select_fusion), channel_id=1, source_target_pairs={{0,8},{8,0},{16,24},{24,16},{32,40},{40,32},{48,56},{56,48},{64,72... | collective-permute-start | bytes 24584 | tf_op jit(solution)/shard_map/ppermute | solution.py:705
  118.2 1.9 %collective-permute-done.3 = f32[16,128]{1,0:T(8,128)S(1)} collective-permute-done((f32[16,128]{1,0:T(8,128)S(1)}, f32[16,128]{1,0:T(8,128)S(1)}, u32[]{:S(2)}, u32[]{:S(2)}) %collective-permute-start.3) | collective-permute-done | bytes 8224 | tf_op jit(solution)/shard_map/ppermute | solution.py:705
  120.1 3.0 %collective-permute-start.4 = (f32[16,128]{1,0:T(8,128)S(1)}, f32[16,128]{1,0:T(8,128)S(1)}, u32[]{:S(2)}, u32[]{:S(2)}) collective-permute-start(f32[16,128]{1,0:T(8,128)S(1)} %fusion), channel_id=1, source_target_pairs={{0,24},{8,16},{16,8},{24,0},{32,56},{40,48},{48,40},{56,32},{64,88... | collective-permute-start | bytes 24584 | tf_op jit(solution)/shard_map/ppermute | solution.py:705
  123.1 1.8 %collective-permute-done.4 = f32[16,128]{1,0:T(8,128)S(1)} collective-permute-done((f32[16,128]{1,0:T(8,128)S(1)}, f32[16,128]{1,0:T(8,128)S(1)}, u32[]{:S(2)}, u32[]{:S(2)}) %collective-permute-start.4) | collective-permute-done | bytes 8224 | tf_op jit(solution)/shard_map/ppermute | solution.py:705
  125.1 1.8 %collective-permute-start.5 = (f32[16,128]{1,0:T(8,128)S(1)}, f32[16,128]{1,0:T(8,128)S(1)}, u32[]{:S(2)}, u32[]{:S(2)}) collective-permute-start(f32[16,128]{1,0:T(8,128)S(1)} %fusion.1), channel_id=1, source_target_pairs={{0,32},{8,40},{16,48},{24,56},{32,0},{40,8},{48,16},{56,24},{64,96... | collective-permute-start | bytes 24584 | tf_op jit(solution)/shard_map/ppermute | solution.py:705
  126.9 1.8 %collective-permute-done.5 = f32[16,128]{1,0:T(8,128)S(1)} collective-permute-done((f32[16,128]{1,0:T(8,128)S(1)}, f32[16,128]{1,0:T(8,128)S(1)}, u32[]{:S(2)}, u32[]{:S(2)}) %collective-permute-start.5) | collective-permute-done | bytes 8224 | tf_op jit(solution)/shard_map/ppermute | solution.py:705
  128.7 3.1 %collective-permute-start.6 = (f32[16,128]{1,0:T(8,128)S(1)}, f32[16,128]{1,0:T(8,128)S(1)}, u32[]{:S(2)}, u32[]{:S(2)}) collective-permute-start(f32[16,128]{1,0:T(8,128)S(1)} %add.26), channel_id=1, source_target_pairs={{0,96},{8,104},{16,112},{24,120},{32,64},{40,72},{48,80},{56,88},{... | collective-permute-start | bytes 24584 | tf_op jit(solution)/shard_map/ppermute | solution.py:705
  131.8 1.8 %collective-permute-done.6 = f32[16,128]{1,0:T(8,128)S(1)} collective-permute-done((f32[16,128]{1,0:T(8,128)S(1)}, f32[16,128]{1,0:T(8,128)S(1)}, u32[]{:S(2)}, u32[]{:S(2)}) %collective-permute-start.6) | collective-permute-done | bytes 8224 | tf_op jit(solution)/shard_map/ppermute | solution.py:705
  133.6 1.7 %finish.1 = (f32[128,512]{1,0:T(8,128)}, f32[1,16,512]{2,1,0:T(8,128)}, f32[128,512]{1,0:T(8,128)}, f32[32,512]{1,0:T(8,128)}) custom-call(f32[16,128]{1,0:T(8,128)S(1)} %add.27.sums, f32[16,160,128]{2,1,0:T(8,128)S(1)} %all-to-all-done.5.owned), custom_call_target="tpu_custom_call" | custom-call | tf_op jit(solution)/shard_map/finish/pallas_call | solution.py:773
  (12 shorter events, 0.4 us)
Async XLA Ops:
  43.9 13.9 %all-to-all-start.1 = ((f32[8,88,128]{2,1,0:T(8,128)}), f32[8,88,128]{2,1,0:T(8,128)S(1)}, u32[]{:S(2)}, u32[]{:S(2)}) async-start(f32[8,88,128]{2,1,0:T(8,128)} %bitcast.2), calls=%async_computation.1 | async-start | bytes 720896 | tf_op jit(solution)/shard_map/all_to_all | solution.py:648
  58.6 12.0 %all-to-all-start.2 = ((f32[8,88,128]{2,1,0:T(8,128)}), f32[8,88,128]{2,1,0:T(8,128)S(1)}, u32[]{:S(2)}, u32[]{:S(2)}) async-start(f32[8,88,128]{2,1,0:T(8,128)} %bitcast.6), calls=%async_computation.2 | async-start | bytes 720896 | tf_op jit(solution)/shard_map/all_to_all | solution.py:648
  75.4 12.0 %all-to-all-start.3 = ((f32[8,88,128]{2,1,0:T(8,128)}), f32[8,88,128]{2,1,0:T(8,128)S(1)}, u32[]{:S(2)}, u32[]{:S(2)}) async-start(f32[8,88,128]{2,1,0:T(8,128)} %bitcast.8), calls=%async_computation.3 | async-start | bytes 720896 | tf_op jit(solution)/shard_map/all_to_all | solution.py:648
  99.6 34.0 %all-to-all-start.5 = ((f32[16,160,128]{2,1,0:T(8,128)}), f32[16,160,128]{2,1,0:T(8,128)S(1)}, u32[]{:S(2)}, u32[]{:S(2)}) async-start(f32[16,160,128]{2,1,0:T(8,128)} %pack_owned.3), calls=%async_computation.5 | async-start | bytes 2621440 | tf_op jit(solution)/shard_map/all_to_all | solution.py:648
  106.8 1.2 collective-permute-start
  108.0 3.5 %collective-permute-start.1 = (f32[1,128]{1,0:T(1,128)S(1)}, f32[1,128]{1,0:T(1,128)S(1)}, u32[]{:S(2)}, u32[]{:S(2)}) collective-permute-start(f32[1,128]{1,0:T(1,128)S(1)} %add.21), channel_id=1, source_target_pairs={{0,2},{1,3},{2,0},{3,1},{4,6},{5,7},{6,4},{7,5},{8,10},{9,11},{10,... | collective-permute-start | bytes 1544 | tf_op jit(solution)/shard_map/ppermute | solution.py:705
  111.5 4.8 %collective-permute-start.2 = (f32[1,128]{1,0:T(1,128)S(1)}, f32[1,128]{1,0:T(1,128)S(1)}, u32[]{:S(2)}, u32[]{:S(2)}) collective-permute-start(f32[1,128]{1,0:T(1,128)S(1)} %add.22), channel_id=1, source_target_pairs={{0,6},{1,7},{2,4},{3,5},{4,2},{5,3},{6,0},{7,1},{8,14},{9,15},{10,... | collective-permute-start | bytes 1544 | tf_op jit(solution)/shard_map/ppermute | solution.py:705
  116.4 3.7 %collective-permute-start.3 = (f32[16,128]{1,0:T(8,128)S(1)}, f32[16,128]{1,0:T(8,128)S(1)}, u32[]{:S(2)}, u32[]{:S(2)}) collective-permute-start(f32[16,128]{1,0:T(8,128)S(1)} %broadcast_select_fusion), channel_id=1, source_target_pairs={{0,8},{8,0},{16,24},{24,16},{32,40},{40,32},{48,56},{56,48},{64,72... | collective-permute-start | bytes 24584 | tf_op jit(solution)/shard_map/ppermute | solution.py:705
  120.1 4.9 %collective-permute-start.4 = (f32[16,128]{1,0:T(8,128)S(1)}, f32[16,128]{1,0:T(8,128)S(1)}, u32[]{:S(2)}, u32[]{:S(2)}) collective-permute-start(f32[16,128]{1,0:T(8,128)S(1)} %fusion), channel_id=1, source_target_pairs={{0,24},{8,16},{16,8},{24,0},{32,56},{40,48},{48,40},{56,32},{64,88... | collective-permute-start | bytes 24584 | tf_op jit(solution)/shard_map/ppermute | solution.py:705
  125.1 3.7 %collective-permute-start.5 = (f32[16,128]{1,0:T(8,128)S(1)}, f32[16,128]{1,0:T(8,128)S(1)}, u32[]{:S(2)}, u32[]{:S(2)}) collective-permute-start(f32[16,128]{1,0:T(8,128)S(1)} %fusion.1), channel_id=1, source_target_pairs={{0,32},{8,40},{16,48},{24,56},{32,0},{40,8},{48,16},{56,24},{64,96... | collective-permute-start | bytes 24584 | tf_op jit(solution)/shard_map/ppermute | solution.py:705
  128.7 4.9 %collective-permute-start.6 = (f32[16,128]{1,0:T(8,128)S(1)}, f32[16,128]{1,0:T(8,128)S(1)}, u32[]{:S(2)}, u32[]{:S(2)}) collective-permute-start(f32[16,128]{1,0:T(8,128)S(1)} %add.26), channel_id=1, source_target_pairs={{0,96},{8,104},{16,112},{24,120},{32,64},{40,72},{48,80},{56,88},{... | collective-permute-start | bytes 24584 | tf_op jit(solution)/shard_map/ppermute | solution.py:705

commit v3 on v2

--- a/solution.py
+++ b/solution.py
@@ -44,9 +44,8 @@
 INDEX_ROWS = 24
 DATA_ROWS = INDEX_AT + INDEX_ROWS
 STEPS = 2
-TRACE_PIECES = 10
-BASIS_PIECES = 16
 OWN_ROWS = 2 * SLICE + SLICE // 2
+PACK = LANES // CMP_G
 
 VMEM = pltpu.VMEM
 F32 = jnp.float32
@@ -132,17 +131,16 @@
     for copy in indices:
         copy.start()
     pieces = []
-    for k in range(TRACE_PIECES):
-        size = TR_DEV // TRACE_PIECES
-        span = slice(k * size, (k + 1) * size)
+    for k in range(TRACE_TILES):
+        span = slice(k * LANES, (k + 1) * LANES)
         pieces.append((traces.at[span], own.at[span]))
-    for k in range(BASIS_PIECES):
-        size = 2 * FREQS // BASIS_PIECES
+    size = 2 * FREQS // STEPS // 2
+    for k in range(2 * STEPS):
         span = slice(k * size, (k + 1) * size)
         pieces.append((waves.at[span], basis.at[span]))
     copies = [pltpu.make_async_copy(a, b, sems.at[k]) for k, (a, b) in enumerate(pieces)]
-    early = TRACE_PIECES + BASIS_PIECES // STEPS
-    for copy in copies:
+    early = TRACE_TILES + 2
+    for copy in copies[:early]:
         copy.start()
     for copy in indices:
         copy.wait()
@@ -154,6 +152,8 @@
         out[part, BINS_AT:, :] = extra[...]
     for copy in copies[:early]:
         copy.wait()
+    for copy in copies[early:]:
+        copy.start()
     half = FREQS // STEPS
     for step in range(STEPS):
         if step == 1:
@@ -180,7 +180,7 @@
         ]
         + [VMEM(array.shape, jnp.int32) for array in small]
         + [
-            pltpu.SemaphoreType.DMA((TRACE_PIECES + BASIS_PIECES,)),
+            pltpu.SemaphoreType.DMA((TRACE_TILES + 2 * STEPS,)),
             pltpu.SemaphoreType.DMA((len(small),)),
         ],
         compiler_params=params(24),
@@ -240,22 +240,23 @@
     tiles = index[block]
     values = [data[block, q * SLICE : (q + 1) * SLICE] for q in range(TRACE_TILES)]
 
-    def of_tile(row, tile):
-        picked = [
-            jnp.where(tiles[4 * q + row : 4 * q + row + 1] >> 7 == tile, values[q], 0.0)
-            for q in range(TRACE_TILES)
-        ]
-        return split_rows(jnp.concatenate(picked, axis=1))
-
-    plain = nt_dot(split_rows(jnp.concatenate(values, axis=1)), hot[: 2 * LANES])
+    both = split_rows(jnp.concatenate(values, axis=1))
+    zero = jnp.zeros((1, 1), BF16)
+
+    def of_tiles(row, count):
+        place = [tiles[4 * q + row : 4 * q + row + 1] >> 7 for q in range(TRACE_TILES)]
+        place = jnp.concatenate(place, axis=1).astype(F32).astype(BF16)
+        return jnp.concatenate([jnp.where(place == tile, both, zero) for tile in range(count)], axis=0)
+
+    plain = nt_dot(both, hot[: 2 * LANES])
     tab[at(block)] = join_rows(plain[:, :LANES])
     tab[at(OFF_TILE)] += join_rows(plain[:, LANES:])
-    parts = jnp.concatenate([of_tile(1, tile) for tile in range(RCV_TILES)], axis=0)
+    parts = of_tiles(1, RCV_TILES)
     sums = nt_dot(parts, hot[2 * LANES : 3 * LANES])
     for tile in range(RCV_TILES):
         rcv[tile] += join_rows(sums[tile * 2 * SLICE : (tile + 1) * 2 * SLICE])
     cmp_tiles = LIVE_TILES - CMP_TILE
-    parts = jnp.concatenate([of_tile(3, tile) for tile in range(cmp_tiles)], axis=0)
+    parts = of_tiles(3, cmp_tiles)
     sums = nt_dot(parts, hot[3 * LANES :])
     for tile in range(cmp_tiles):
         tab[at(CMP_TILE + tile)] += join_rows(sums[tile * 2 * SLICE : (tile + 1) * 2 * SLICE])
@@ -305,8 +306,9 @@
 
 
 def count_kernel(
-    index, kept, to_cmp_kept, to_rcv_kept, most, diag, hot_even, hot_odd, ids, to_cmp, to_rcv, *, first
+    index, kept, to_cmp_kept, to_rcv_kept, most, diag, *refs, first
 ):
+    *handed, hot_even, hot_odd, ids, to_cmp, to_rcv = refs
     step = pl.program_id(0)
     even = first + 2 * step
 
@@ -324,7 +326,9 @@
         to_cmp[...] += cmp_counts
         to_rcv[...] += rcv_counts
         diag[...] += jnp.sum(rows, axis=0, keepdims=True)
-        kept[place * SRC_G : (place + 1) * SRC_G] = kept_part(rows)
+        part = kept_part(rows)
+        for out in [kept] + handed:
+            out[place * SRC_G : (place + 1) * SRC_G] = part
         most[...] = jnp.maximum(most[...], peak(rows))
 
     fill_hot(index[even + 1], ids, hot_odd)
@@ -334,8 +338,8 @@
 
     @pl.when(step == COUNT_STEPS - 1)
     def _():
-        to_cmp_kept[...] = kept_part(to_cmp[...])
-        to_rcv_kept[...] = kept_part(to_rcv[...])
+        to_cmp_kept[...] = (to_cmp[...].astype(jnp.int32) & (EXACT - 1)).astype(jnp.int8)
+        to_rcv_kept[...] = (to_rcv[...].astype(jnp.int32) & (EXACT - 1)).astype(jnp.int8)
         most[...] = jnp.maximum(most[...], jnp.maximum(peak(to_cmp[...]), peak(to_rcv[...])))
 
 
@@ -361,26 +365,19 @@
 
 
 def fetch_counts(refs, held, held_cmp, held_rcv, sems):
-    first, last, cmp_1, cmp_2, rcv_1, rcv_2 = refs
+    *halves, cmp_1, cmp_2, rcv_1, rcv_2 = refs
     pieces = []
-    for block in range(N_SHOT):
-        source = first if block < HALF else last
-        start = block % HALF * SRC_G
-        place = block * SRC_G
-        pieces.append((source.at[start : start + SRC_G], held.at[place : place + SRC_G]))
+    for half, source in enumerate(halves):
+        for chunk in range(CHUNKS // 2):
+            start = chunk * CHUNK_ROWS
+            place = held.at[half * (CHUNKS // 2) + chunk]
+            pieces.append((source.at[start : start + CHUNK_ROWS], place))
     pieces += [(cmp_1, held_cmp.at[0]), (cmp_2, held_cmp.at[1])]
     pieces += [(rcv_1, held_rcv.at[0]), (rcv_2, held_rcv.at[1])]
     copies = [pltpu.make_async_copy(a, b, sems.at[k]) for k, (a, b) in enumerate(pieces)]
     for copy in copies:
         copy.start()
     return copies
-
-
-def wait_chunk(copies, chunk):
-    blocks = N_SHOT // CHUNKS
-    for copy in copies[chunk * blocks : (chunk + 1) * blocks]:
-        copy.wait()
-    return slice(chunk * CHUNK_ROWS, (chunk + 1) * CHUNK_ROWS)
 
 
 def sum_halves(held):
@@ -399,21 +396,24 @@
 
 
 def normal_kernel(
-    first, last, cmp_1, cmp_2, rcv_1, rcv_2, tab_in, rcv_in, diag_1, diag_2, most_1, most_2, index,
+    first, cmp_1, cmp_2, rcv_1, rcv_2, tab_in, rcv_in, last, diag_1, diag_2, most_1, most_2, index,
     tab, rcv, own_count, own, shared, to_shared, to_own,
     held, held_cmp, held_rcv, sems, hot, ids, exact_cmp, exact_rcv,
 ):
-    counts = (first, last, cmp_1, cmp_2, rcv_1, rcv_2)
+    counts = (first, cmp_1, cmp_2, rcv_1, rcv_2)
     copies = fetch_counts(counts, held, held_cmp, held_rcv, sems)
     top = 2 * SLICE
+    half = HALF * SRC_G
     load_halves(tab_in, rcv_in, own, shared)
     lanes = lax.broadcasted_iota(jnp.int32, (16, SHARED), 1)
     shared[top:] = jnp.where(lanes < LANES, 1.0, 0.0).astype(BF16)
-    for chunk in range(CHUNKS):
-        span = wait_chunk(copies, chunk)
-        sums = jnp.dot(own[:, span], held[span], preferred_element_type=F32)
-        to_shared[...] = sums if chunk == 0 else to_shared[...] + sums
-        to_own[:, span] = nt_dot(shared[...], held[span])
+    to_shared[...] = jnp.dot(own[:, half:], last[...], preferred_element_type=F32)
+    to_own[:, half:] = nt_dot(shared[...], last[...])
+    for chunk in range(CHUNKS // 2):
+        copies[chunk].wait()
+        span = slice(chunk * CHUNK_ROWS, (chunk + 1) * CHUNK_ROWS)
+        to_shared[...] += jnp.dot(own[:, span], held[chunk], preferred_element_type=F32)
+        to_own[:, span] = nt_dot(shared[...], held[chunk])
 
     def others(to_cmp, to_rcv):
         cmp_sums = jnp.dot(shared[:top, :OR], to_cmp, preferred_element_type=F32)
@@ -428,7 +428,7 @@
         to_shared[...] += jnp.dot(own[:, span], rows, preferred_element_type=F32)
         to_own[:, span] += nt_dot(shared[...], rows)
 
-    for copy in copies[N_SHOT:]:
+    for copy in copies[-4:]:
         copy.wait()
     others(sum_halves(held_cmp), sum_halves(held_rcv))
     add_left_over(most_1, most_2, index, hot, ids, exact_cmp, exact_rcv, others, use_rows)
@@ -478,8 +478,9 @@
     rcv_z[...] = own_z
     load_halves(tab_z, rcv_z, own, shared)
     for chunk in range(CHUNKS):
-        span = wait_chunk(copies, chunk)
-        sums = jnp.dot(own[:, span], held[span], preferred_element_type=F32)
+        copies[chunk].wait()
+        span = slice(chunk * CHUNK_ROWS, (chunk + 1) * CHUNK_ROWS)
+        sums = jnp.dot(own[:, span], held[chunk], preferred_element_type=F32)
         to_shared[...] = sums if chunk == 0 else to_shared[...] + sums
 
     def whole(tabs, own):
@@ -495,7 +496,7 @@
         span = pl.ds(pl.multiple_of(block * SRC_G, SRC_G), SRC_G)
         to_shared[...] += jnp.dot(own[:, span], rows, preferred_element_type=F32)
 
-    for copy in copies[N_SHOT:]:
+    for copy in copies[-4:]:
         copy.wait()
     others(sum_halves(held_cmp), sum_halves(held_rcv))
     add_left_over(most_1, most_2, index, hot, ids, exact_cmp, exact_rcv, others, use_rows)
@@ -558,18 +559,20 @@
 def count_call(index, first):
     rows = pl.BlockSpec((2 * SRC_G, SHARED), lambda c: (c, 0))
     small = [whole_spec(*TO_CMP), whole_spec(*TO_RCV), whole_spec(1, LANES), whole_spec(1, SHARED)]
+    handed = [] if first == 0 else [jax.ShapeDtypeStruct(COUNTS, BF16)]
     return pl.pallas_call(
         functools.partial(count_kernel, first=first),
         grid=(COUNT_STEPS,),
         in_specs=[whole_spec(*INDEX)],
-        out_specs=[rows] + small,
+        out_specs=[rows] + small + [rows] * len(handed),
         out_shape=[
             pltpu.HBM(COUNTS, BF16),
-            pltpu.HBM(TO_CMP, BF16),
-            pltpu.HBM(TO_RCV, BF16),
+            pltpu.HBM(TO_CMP, jnp.int8),
+            pltpu.HBM(TO_RCV, jnp.int8),
             jax.ShapeDtypeStruct((1, LANES), F32),
             jax.ShapeDtypeStruct((1, SHARED), F32),
-        ],
+        ]
+        + handed,
         scratch_shapes=[VMEM((ROWS, TR_DEV), FP8)] * 2
         + [VMEM((256, LANES), BF16), VMEM(TO_CMP, F32), VMEM(TO_RCV, F32)],
         compiler_params=params(24),
@@ -578,13 +581,13 @@
     )(index)
 
 
-def count_scratch():
+def count_scratch(chunks):
     return (
         [
-            VMEM((N_SHOT * SRC_G, SHARED), BF16),
-            VMEM((2,) + TO_CMP, BF16),
-            VMEM((2,) + TO_RCV, BF16),
-            pltpu.SemaphoreType.DMA((N_SHOT + 4,)),
+            VMEM((chunks, CHUNK_ROWS, SHARED), BF16),
+            VMEM((2,) + TO_CMP, jnp.int8),
+            VMEM((2,) + TO_RCV, jnp.int8),
+            pltpu.SemaphoreType.DMA((chunks + 4,)),
         ]
         + hot_scratch()
         + [VMEM(TO_CMP, F32), VMEM(TO_RCV, F32)]
@@ -593,15 +596,16 @@
 
 def count_operands(counts):
     big = in_hbm(*[array for pair in zip(counts[0][:3], counts[1][:3]) for array in pair])
-    (most_1, diag_1), (most_2, diag_2) = counts[0][3:], counts[1][3:]
+    (most_1, diag_1), (most_2, diag_2) = counts[0][3:5], counts[1][3:5]
     return big, [diag_1, diag_2, most_1, most_2]
 
 
 def normal_apply(tab, rcv, index, counts):
-    big, small = count_operands(counts)
+    (first, _, *rest), small = count_operands(counts)
+    last = counts[1][5]
     return pl.pallas_call(
         normal_kernel,
-        in_specs=[ANYWHERE] * 6 + [IN_VMEM] * 7,
+        in_specs=[ANYWHERE] * 5 + [IN_VMEM] * 8,
         out_shape=table_shapes() + [jax.ShapeDtypeStruct((N_SHOT, LANES), F32)],
         scratch_shapes=[
             VMEM((2 * SLICE, N_SHOT * SRC_G), BF16),
@@ -609,11 +613,11 @@
             VMEM((2 * SLICE, SHARED), F32),
             VMEM((2 * SLICE + 16, N_SHOT * SRC_G), F32),
         ]
-        + count_scratch(),
+        + count_scratch(CHUNKS // 2),
         compiler_params=params(24),
         cost_estimate=cost(3),
         name="normal_apply",
-    )(*big, tab, rcv, *small, index)
+    )(first, *rest, tab, rcv, last, *small, index)
 
 
 def norm_sums(tab_b, rcv_b, tab_y, rcv_y, own_count, index, counts):
@@ -629,7 +633,7 @@
             VMEM((2 * SLICE, SHARED), BF16),
             VMEM((2 * SLICE, SHARED), F32),
         ]
-        + count_scratch(),
+        + count_scratch(CHUNKS),
         compiler_params=params(24),
         cost_estimate=cost(2),
         name="norm_sums",
@@ -676,9 +680,12 @@
         both = jnp.where(lanes < CMP_G, cmp_part, rcv_part)
         moved = pltpu.roll(both[half:], LANES // 2, 1)
         rows[dest, 2 * SLICE :] = jnp.where(lanes[:half] < LANES // 2, both[:half], moved)
-        place = out.at[dest, first : first + OWN_ROWS]
-        copies.append(pltpu.make_async_copy(rows.at[dest], place, sems.at[dest]))
-        copies[-1].start()
+        if dest % PACK == PACK - 1:
+            group = dest // PACK
+            span = slice(group * PACK, (group + 1) * PACK)
+            place = out.at[span, first : first + OWN_ROWS]
+            copies.append(pltpu.make_async_copy(rows.at[span], place, sems.at[group]))
+            copies[-1].start()
     for copy in copies:
         copy.wait()
 
@@ -692,7 +699,7 @@
         out_shape=pltpu.HBM((N_SHOT, 2 * OWN_ROWS, LANES), F32),
         scratch_shapes=[
             VMEM((N_SHOT, OWN_ROWS, LANES), F32),
-            pltpu.SemaphoreType.DMA((N_SHOT,)),
+            pltpu.SemaphoreType.DMA((N_SHOT // PACK,)),
         ],
         input_output_aliases={2: 0} if given else {},
         compiler_params=params(24),
@@ -715,7 +722,7 @@
     return rows
 
 
-def finish_kernel(sums, owned, source, receiver, offset, cmp, done_so, done_rest, sems):
+def finish_kernel(sums, owned, source, receiver, offset, cmp):
     rows = sums[...]
     norm_b, cross, norm_z, norm_az, shift = (rows[:, lane : lane + 1] for lane in range(5))
     shift = shift * (1.0 / N_RCV)
@@ -745,47 +752,30 @@
         return jnp.concatenate([tile, pltpu.roll(tile, LANES // 2, 1)], axis=0)
 
     per_tile = LANES // SLICE
-    rcv_rows = RCV_G // N_SHOT
-    copies = []
-
-    def write(block, target):
-        copies.append(pltpu.make_async_copy(block, target, sems.at[len(copies)]))
-        copies[-1].start()
-
     for group in range(N_SHOT // per_tile):
         span = slice(group * LANES, (group + 1) * LANES)
         senders = range(group * per_tile, (group + 1) * per_tile)
-        for place, target in enumerate((source, offset)):
-            start = place * SLICE
-            table = [combine(i, start, start + SLICE) for i in senders]
-            done_so[place, group] = jnp.concatenate(table, axis=0).T
-            write(done_so.at[place, group], target.at[:, span])
-        rest = [spread_halves(combine(i, 2 * SLICE, OWN_ROWS)) for i in senders]
-        done_rest[group] = jnp.concatenate(rest, axis=0).T
-        write(done_rest.at[group, :CMP_G], cmp.at[:, span])
-        write(done_rest.at[group, CMP_G : CMP_G + rcv_rows], receiver.at[0, :, span])
-    for copy in copies:
-        copy.wait()
+        source[:, span] = jnp.concatenate([combine(i, 0, SLICE) for i in senders], axis=0).T
+        offset[:, span] = jnp.concatenate(
+            [combine(i, SLICE, 2 * SLICE) for i in senders], axis=0
+        ).T
+        rest = jnp.concatenate(
+            [spread_halves(combine(i, 2 * SLICE, OWN_ROWS)) for i in senders], axis=0
+        ).T
+        cmp[:, span] = rest[:CMP_G]
+        receiver[0, :, span] = rest[CMP_G : CMP_G + RCV_G // N_SHOT]
 
 
 def finish(sums, owned):
-    groups = FREQS // LANES
     return pl.pallas_call(
         finish_kernel,
-        in_specs=[IN_VMEM] * 2,
-        out_specs=[ANYWHERE] * 4,
         out_shape=[
             jax.ShapeDtypeStruct((SRC_G, FREQS), F32),
             jax.ShapeDtypeStruct((1, RCV_G // N_SHOT, FREQS), F32),
             jax.ShapeDtypeStruct((128, FREQS), F32),
             jax.ShapeDtypeStruct((CMP_G, FREQS), F32),
         ],
-        scratch_shapes=[
-            VMEM((2, groups, LANES, LANES), F32),
-            VMEM((groups, LANES, LANES), F32),
-            pltpu.SemaphoreType.DMA((4 * groups,)),
-        ],
-        compiler_params=params(24),
+        compiler_params=params(),
         name="finish",
     )(sums, owned)
 

time: 136 us -> 136 us (level)
  local copies, waits for them, and re-layouts: 0 us -> 2.76 us
  Pallas kernels: 36.5 us -> 34.2 us
    unnamed x0 -> x4, local copies, waits for them, and re-layouts: none -> 2.76 us
where the time goes in v3:
time: 136 us; the launch traced here: 135 us
  blocking collectives  41.4 us (30%)
  Pallas kernels  34.2 us (25%)
  waiting for transfers between devices  28.8 us (21%)
  starting transfers between devices  26.7 us (20%)
  local copies, waits for them, and re-layouts  2.76 us (2%)
    all_to_all x2, blocking collectives, exchange(): return lax.all_to_all(array, axis, split_axis=0, concat_axis=0, tiled=True)  41.4 us
    all_to_all x4, starting transfers between devices, exchange(): return lax.all_to_all(array, axis, split_axis=0, concat_axis=0, tiled=True)  16.1 us
    ppermute x7, waiting for transfers between devices, swapped(): return lax.ppermute(value, axis, [(s, s ^ bit) for s in range(size)])  16 us
    all_to_all x4, waiting for transfers between devices, exchange(): return lax.all_to_all(array, axis, split_axis=0, concat_axis=0, tiled=True)  12.8 us
    ppermute x7, starting transfers between devices, swapped(): return lax.ppermute(value, axis, [(s, s ^ bit) for s in range(size)])  10.6 us
    pallas_call x2, Pallas kernels, count_call(): pl.pallas_call(functools.partial(count_kernel, first=first), grid=(COUNT_...  10.5 us
    pallas_call x1, Pallas kernels, adjoint_apply(): pl.pallas_call(adjoint_kernel, out_shape=table_shapes() + [jax.ShapeDtype...  7.44 us
    pallas_call x1, Pallas kernels, log_spectra(): pl.pallas_call(spectra_kernel, in_specs=[ANYWHERE] * (2 + len(small)), ou...  4.72 us
  transfers between devices with their start and end apart: 11, of which 10 were waited for; matrix products, arithmetic and copies ran while one was open for 0% of the time, Pallas kernels for 11%

profile of v3, /device:TPU:0, one launch (start us, length us, event | category | flops | bytes accessed | tf_op | source)
XLA Modules:
  0.0 134.9 jit_solution(3920800016360953490)
XLA Ops:
  0.6 4.7 %spectra.1 = f32[16,200,128]{2,1,0:T(8,128)S(1)} custom-call(bf16[640,1024]{1,0:T(8,128)(2,1)} %traces.1, bf16[1024,1024]{1,0:T(8,128)(2,1)} %constant.10.clone.waves, s32[16,80]{1,0:T(8,128)} %bitcast.19, s32[1,16]{1,0:T(1,128)} %refs_1_.1, s32[16,80]{1,0:T(8,128)} %bitcast.20, s32[640]{0:T(1024)} %refs_3_.1, s32[640]{0:T(1024)} %refs_4_.1, s32[640]{0:T(1024)} %refs_5_.1), custom_call_target="tpu_custom_call" | custom-call | flops 5000000000 | bytes 15000000 | tf_op jit(solution)/shard_map/spectra/pallas_call | solution.py:172
  5.4 30.4 %all_to_all.53.data = f32[16,200,128]{2,1,0:T(8,128)S(1)} all-to-all(f32[16,200,128]{2,1,0:T(8,128)S(1)} %spectra.1), channel_id=1, replica_groups=mesh['shot'=16,'rcv'=8] {'shot'}, dimensions={0} | all-to-all | bytes 3276800 | tf_op jit(solution)/shard_map/all_to_all | solution.py:652
  35.8 7.4 %adjoint_apply.1 = (f32[704,128]{1,0:T(8,128)}, f32[2,32,128]{2,1,0:T(8,128)S(1)}, s32[16,24,128]{2,1,0:T(8,128)S(1)}) custom-call(f32[16,200,128]{2,1,0:T(8,128)S(1)} %all_to_all.53.data), custom_call_target="tpu_custom_call" | custom-call | flops 8000000000 | bytes 24000000 | tf_op jit(solution)/shard_map/adjoint_apply/pallas_call | solution.py:543
  43.2 5.3 %all-to-all-start.1 = ((f32[8,88,128]{2,1,0:T(8,128)}), f32[8,88,128]{2,1,0:T(8,128)S(1)}, u32[]{:S(2)}, u32[]{:S(2)}) async-start(f32[8,88,128]{2,1,0:T(8,128)} %bitcast.2), calls=%async_computation.1 | async-start | bytes 720896 | tf_op jit(solution)/shard_map/all_to_all | solution.py:652
  48.5 5.2 %count_pairs.2 = (bf16[1024,896]{1,0:T(8,128)(2,1)}, s8[384,512]{1,0:T(32,128)(4,1)}, s8[128,256]{1,0:T(32,128)(4,1)}, f32[1,128]{1,0:T(1,128)S(1)}, f32[1,896]{1,0:T(1,128)S(1)}) custom-call(s32[16,24,128]{2,1,0:T(8,128)S(1)} %get-tuple-element.44.index), custom_call_target="tpu_custom_call" | custom-call | flops 6000000000 | bytes 18000000 | tf_op jit(solution)/shard_map/count_pairs/pallas_call | solution.py:563
  53.8 3.4 %all-to-all-done.1 = f32[8,88,128]{2,1,0:T(8,128)S(1)} async-done(((f32[8,88,128]{2,1,0:T(8,128)}), f32[8,88,128]{2,1,0:T(8,128)S(1)}, u32[]{:S(2)}, u32[]{:S(2)}) %all-to-all-start.1) | async-done | bytes 360480 | tf_op jit(solution)/shard_map/all_to_all | solution.py:652
  57.9 3.4 %all-to-all-start.2 = ((f32[8,88,128]{2,1,0:T(8,128)}), f32[8,88,128]{2,1,0:T(8,128)S(1)}, u32[]{:S(2)}, u32[]{:S(2)}) async-start(f32[8,88,128]{2,1,0:T(8,128)} %bitcast.6), calls=%async_computation.2 | async-start | bytes 720896 | tf_op jit(solution)/shard_map/all_to_all | solution.py:652
  61.4 5.2 %count_pairs.3 = (bf16[1024,896]{1,0:T(8,128)(2,1)}, s8[384,512]{1,0:T(32,128)(4,1)}, s8[128,256]{1,0:T(32,128)(4,1)}, f32[1,128]{1,0:T(1,128)S(1)}, f32[1,896]{...) custom-call(s32[16,24,128]{2,1,0:T(8,128)S(1)} %get-tuple-element.44.index), custom_call_target="tpu_custom_call" | custom-call | flops 6000000000 | bytes 18000000 | tf_op jit(solution)/shard_map/count_pairs/pallas_call | solution.py:563
  66.6 1.3 copy-done
  67.9 2.0 %all-to-all-done.2 = f32[8,88,128]{2,1,0:T(8,128)S(1)} async-done(((f32[8,88,128]{2,1,0:T(8,128)}), f32[8,88,128]{2,1,0:T(8,128)S(1)}, u32[]{:S(2)}, u32[]{:S(2)}) %all-to-all-start.2) | async-done | bytes 360480 | tf_op jit(solution)/shard_map/all_to_all | solution.py:652
  69.9 1.5 %copy-done.1 = bf16[1024,896]{1,0:T(8,128)(2,1)S(1)} copy-done((bf16[1024,896]{1,0:T(8,128)(2,1)S(1)}, bf16[1024,896]{1,0:T(8,128)(2,1)}, u32[]{:S(2)}) %copy-start.1) | copy-done | bytes 1835032
  71.4 4.0 %normal_apply.1 = (f32[704,128]{1,0:T(8,128)}, f32[2,32,128]{2,1,0:T(8,128)S(1)}, f32[16,128]{1,0:T(8,128)S(1)}) custom-call(bf16[1024,896]{1,0:T(8,128)(2,1)} %get-tuple-element.41.first, s8[384,512]{1,0:T(32,128)(4,1)} %get-tuple-element.46.cmp_1, s8[384,512]{1,0:T(32,128)(4,1)} %get-tuple-element.47.cmp_2, s8[128,256]{1,0:T(32,128)(4,1)} %get-tuple-element.48.rcv_1, ...), custom_call_target="tpu_custom_call" | custom-call | flops 3000000000 | bytes 9000000 | tf_op jit(solution)/shard_map/normal_apply/pallas_call | solution.py:606
  75.4 3.5 %all-to-all-start.3 = ((f32[8,88,128]{2,1,0:T(8,128)}), f32[8,88,128]{2,1,0:T(8,128)S(1)}, u32[]{:S(2)}, u32[]{:S(2)}) async-start(f32[8,88,128]{2,1,0:T(8,128)} %bitcast.8), calls=%async_computation.3 | async-start | bytes 720896 | tf_op jit(solution)/shard_map/all_to_all | solution.py:652
  78.8 1.1 pack_owned.2.refs_0_
  79.9 7.4 %all-to-all-done.3 = f32[8,88,128]{2,1,0:T(8,128)S(1)} async-done(((f32[8,88,128]{2,1,0:T(8,128)}), f32[8,88,128]{2,1,0:T(8,128)S(1)}, u32[]{:S(2)}, u32[]{:S(2)}) %all-to-all-start.3) | async-done | bytes 360480 | tf_op jit(solution)/shard_map/all_to_all | solution.py:652
  87.4 11.0 %all_to_all.54 = f32[8,88,128]{2,1,0:T(8,128)S(1)} all-to-all(f32[8,88,128]{2,1,0:T(8,128)S(1)} %sum_shares.3), channel_id=1, replica_groups=mesh['shot'=16,'rcv'=8] {'rcv'}, dimensions={0} | all-to-all | bytes 720896 | tf_op jit(solution)/shard_map/all_to_all | solution.py:652
  98.3 1.1 pack_owned.3
  99.4 3.9 %all-to-all-start.5 = ((f32[16,160,128]{2,1,0:T(8,128)}), f32[16,160,128]{2,1,0:T(8,128)S(1)}, u32[]{:S(2)}, u32[]{:S(2)}) async-start(f32[16,160,128]{2,1,0:T(8,128)} %pack_owned.3), calls=%async_computation.5 | async-start | bytes 2621440 | tf_op jit(solution)/shard_map/all_to_all | solution.py:652
  103.3 3.0 %norm_sums.1 = f32[1,128]{1,0:T(1,128)S(1)} custom-call(bf16[1024,896]{1,0:T(8,128)(2,1)} %get-tuple-element.41.first, bf16[1024,896]{1,0:T(8,128)(2,1)} %get-tuple-element.45.last, s8[384,512]{1,0:T(32,128)(4,1)} %get-tuple-element.46.cmp_1, s8[384,512]{1,0:T(32,128)(4,1)} %get-tuple-element.47.cmp_2, s8[128,256]{1,0:T(32,128)(4,1)} %get-tuple-element.48.rcv_1, ...), custom_call_target="tpu_custom_call" | custom-call | flops 2000000000 | bytes 6000000 | tf_op jit(solution)/shard_map/norm_sums/pallas_call | solution.py:625
  106.4 1.1 collective-permute-done
  108.0 3.0 %collective-permute-done.1 = f32[1,128]{1,0:T(1,128)S(1)} collective-permute-done((f32[1,128]{1,0:T(1,128)S(1)}, f32[1,128]{1,0:T(1,128)S(1)}, u32[]{:S(2)}, u32[]{:S(2)}) %collective-permute-start.1) | collective-permute-done | bytes 544 | tf_op jit(solution)/shard_map/ppermute | solution.py:712
  111.0 1.2 collective-permute-start.2
  112.2 3.6 %collective-permute-done.2 = f32[1,128]{1,0:T(1,128)S(1)} collective-permute-done((f32[1,128]{1,0:T(1,128)S(1)}, f32[1,128]{1,0:T(1,128)S(1)}, u32[]{:S(2)}, u32[]{:S(2)}) %collective-permute-start.2) | collective-permute-done | bytes 544 | tf_op jit(solution)/shard_map/ppermute | solution.py:712
  115.8 1.6 %collective-permute-start.3 = (f32[16,128]{1,0:T(8,128)S(1)}, f32[16,128]{1,0:T(8,128)S(1)}, u32[]{:S(2)}, u32[]{:S(2)}) collective-permute-start(f32[16,128]{1,0:T(8,128)S(1)} %broadcast_select_fusion), channel_id=1, source_target_pairs={{0,8},{8,0},{16,24},{24,16},{32,40},{40,32},{48,56},{56,48},{64,72... | collective-permute-start | bytes 24584 | tf_op jit(solution)/shard_map/ppermute | solution.py:712
  117.5 2.2 %collective-permute-done.3 = f32[16,128]{1,0:T(8,128)S(1)} collective-permute-done((f32[16,128]{1,0:T(8,128)S(1)}, f32[16,128]{1,0:T(8,128)S(1)}, u32[]{:S(2)}, u32[]{:S(2)}) %collective-permute-start.3) | collective-permute-done | bytes 8224 | tf_op jit(solution)/shard_map/ppermute | solution.py:712
  119.7 2.7 %collective-permute-start.4 = (f32[16,128]{1,0:T(8,128)S(1)}, f32[16,128]{1,0:T(8,128)S(1)}, u32[]{:S(2)}, u32[]{:S(2)}) collective-permute-start(f32[16,128]{1,0:T(8,128)S(1)} %fusion), channel_id=1, source_target_pairs={{0,24},{8,16},{16,8},{24,0},{32,56},{40,48},{48,40},{56,32},{64,88... | collective-permute-start | bytes 24584 | tf_op jit(solution)/shard_map/ppermute | solution.py:712
  122.4 2.2 %collective-permute-done.4 = f32[16,128]{1,0:T(8,128)S(1)} collective-permute-done((f32[16,128]{1,0:T(8,128)S(1)}, f32[16,128]{1,0:T(8,128)S(1)}, u32[]{:S(2)}, u32[]{:S(2)}) %collective-permute-start.4) | collective-permute-done | bytes 8224 | tf_op jit(solution)/shard_map/ppermute | solution.py:712
  124.7 1.6 %collective-permute-start.5 = (f32[16,128]{1,0:T(8,128)S(1)}, f32[16,128]{1,0:T(8,128)S(1)}, u32[]{:S(2)}, u32[]{:S(2)}) collective-permute-start(f32[16,128]{1,0:T(8,128)S(1)} %fusion.1), channel_id=1, source_target_pairs={{0,32},{8,40},{16,48},{24,56},{32,0},{40,8},{48,16},{56,24},{64,96... | collective-permute-start | bytes 24584 | tf_op jit(solution)/shard_map/ppermute | solution.py:712
  126.3 2.0 %collective-permute-done.5 = f32[16,128]{1,0:T(8,128)S(1)} collective-permute-done((f32[16,128]{1,0:T(8,128)S(1)}, f32[16,128]{1,0:T(8,128)S(1)}, u32[]{:S(2)}, u32[]{:S(2)}) %collective-permute-start.5) | collective-permute-done | bytes 8224 | tf_op jit(solution)/shard_map/ppermute | solution.py:712
  128.4 2.9 %collective-permute-start.6 = (f32[16,128]{1,0:T(8,128)S(1)}, f32[16,128]{1,0:T(8,128)S(1)}, u32[]{:S(2)}, u32[]{:S(2)}) collective-permute-start(f32[16,128]{1,0:T(8,128)S(1)} %add.26), channel_id=1, source_target_pairs={{0,96},{8,104},{16,112},{24,120},{32,64},{40,72},{48,80},{56,88},{... | collective-permute-start | bytes 24584 | tf_op jit(solution)/shard_map/ppermute | solution.py:712
  131.2 2.0 %collective-permute-done.6 = f32[16,128]{1,0:T(8,128)S(1)} collective-permute-done((f32[16,128]{1,0:T(8,128)S(1)}, f32[16,128]{1,0:T(8,128)S(1)}, u32[]{:S(2)}, u32[]{:S(2)}) %collective-permute-start.6) | collective-permute-done | bytes 8224 | tf_op jit(solution)/shard_map/ppermute | solution.py:712
  133.2 1.7 %finish.1 = (f32[128,512]{1,0:T(8,128)}, f32[1,16,512]{2,1,0:T(8,128)}, f32[128,512]{1,0:T(8,128)}, f32[32,512]{1,0:T(8,128)}) custom-call(f32[16,128]{1,0:T(8,128)S(1)} %add.27.sums, f32[16,160,128]{2,1,0:T(8,128)S(1)} %all-to-all-done.5.owned), custom_call_target="tpu_custom_call" | custom-call | tf_op jit(solution)/shard_map/finish/pallas_call | solution.py:770
  (16 shorter events, 1.7 us)
Async XLA Ops:
  43.2 13.9 %all-to-all-start.1 = ((f32[8,88,128]{2,1,0:T(8,128)}), f32[8,88,128]{2,1,0:T(8,128)S(1)}, u32[]{:S(2)}, u32[]{:S(2)}) async-start(f32[8,88,128]{2,1,0:T(8,128)} %bitcast.2), calls=%async_computation.1 | async-start | bytes 720896 | tf_op jit(solution)/shard_map/all_to_all | solution.py:652
  57.9 12.0 %all-to-all-start.2 = ((f32[8,88,128]{2,1,0:T(8,128)}), f32[8,88,128]{2,1,0:T(8,128)S(1)}, u32[]{:S(2)}, u32[]{:S(2)}) async-start(f32[8,88,128]{2,1,0:T(8,128)} %bitcast.6), calls=%async_computation.2 | async-start | bytes 720896 | tf_op jit(solution)/shard_map/all_to_all | solution.py:652
  66.6 1.3 copy-start
  69.9 1.5 %copy-start.1 = (bf16[1024,896]{1,0:T(8,128)(2,1)S(1)}, bf16[1024,896]{1,0:T(8,128)(2,1)}, u32[]{:S(2)}) copy-start(bf16[1024,896]{1,0:T(8,128)(2,1)} %copy-done) | copy-start | bytes 5505028
  75.4 12.0 %all-to-all-start.3 = ((f32[8,88,128]{2,1,0:T(8,128)}), f32[8,88,128]{2,1,0:T(8,128)S(1)}, u32[]{:S(2)}, u32[]{:S(2)}) async-start(f32[8,88,128]{2,1,0:T(8,128)} %bitcast.8), calls=%async_computation.3 | async-start | bytes 720896 | tf_op jit(solution)/shard_map/all_to_all | solution.py:652
  99.4 33.8 %all-to-all-start.5 = ((f32[16,160,128]{2,1,0:T(8,128)}), f32[16,160,128]{2,1,0:T(8,128)S(1)}, u32[]{:S(2)}, u32[]{:S(2)}) async-start(f32[16,160,128]{2,1,0:T(8,128)} %pack_owned.3), calls=%async_computation.5 | async-start | bytes 2621440 | tf_op jit(solution)/shard_map/all_to_all | solution.py:652
  106.3 1.2 collective-permute-start
  107.5 3.5 %collective-permute-start.1 = (f32[1,128]{1,0:T(1,128)S(1)}, f32[1,128]{1,0:T(1,128)S(1)}, u32[]{:S(2)}, u32[]{:S(2)}) collective-permute-start(f32[1,128]{1,0:T(1,128)S(1)} %add.21), channel_id=1, source_target_pairs={{0,2},{1,3},{2,0},{3,1},{4,6},{5,7},{6,4},{7,5},{8,10},{9,11},{10,... | collective-permute-start | bytes 1544 | tf_op jit(solution)/shard_map/ppermute | solution.py:712
  111.0 4.8 %collective-permute-start.2 = (f32[1,128]{1,0:T(1,128)S(1)}, f32[1,128]{1,0:T(1,128)S(1)}, u32[]{:S(2)}, u32[]{:S(2)}) collective-permute-start(f32[1,128]{1,0:T(1,128)S(1)} %add.22), channel_id=1, source_target_pairs={{0,6},{1,7},{2,4},{3,5},{4,2},{5,3},{6,0},{7,1},{8,14},{9,15},{10,... | collective-permute-start | bytes 1544 | tf_op jit(solution)/shard_map/ppermute | solution.py:712
  115.8 3.8 %collective-permute-start.3 = (f32[16,128]{1,0:T(8,128)S(1)}, f32[16,128]{1,0:T(8,128)S(1)}, u32[]{:S(2)}, u32[]{:S(2)}) collective-permute-start(f32[16,128]{1,0:T(8,128)S(1)} %broadcast_select_fusion), channel_id=1, source_target_pairs={{0,8},{8,0},{16,24},{24,16},{32,40},{40,32},{48,56},{56,48},{64,72... | collective-permute-start | bytes 24584 | tf_op jit(solution)/shard_map/ppermute | solution.py:712
  119.7 4.9 %collective-permute-start.4 = (f32[16,128]{1,0:T(8,128)S(1)}, f32[16,128]{1,0:T(8,128)S(1)}, u32[]{:S(2)}, u32[]{:S(2)}) collective-permute-start(f32[16,128]{1,0:T(8,128)S(1)} %fusion), channel_id=1, source_target_pairs={{0,24},{8,16},{16,8},{24,0},{32,56},{40,48},{48,40},{56,32},{64,88... | collective-permute-start | bytes 24584 | tf_op jit(solution)/shard_map/ppermute | solution.py:712
  124.7 3.7 %collective-permute-start.5 = (f32[16,128]{1,0:T(8,128)S(1)}, f32[16,128]{1,0:T(8,128)S(1)}, u32[]{:S(2)}, u32[]{:S(2)}) collective-permute-start(f32[16,128]{1,0:T(8,128)S(1)} %fusion.1), channel_id=1, source_target_pairs={{0,32},{8,40},{16,48},{24,56},{32,0},{40,8},{48,16},{56,24},{64,96... | collective-permute-start | bytes 24584 | tf_op jit(solution)/shard_map/ppermute | solution.py:712
  128.4 4.9 %collective-permute-start.6 = (f32[16,128]{1,0:T(8,128)S(1)}, f32[16,128]{1,0:T(8,128)S(1)}, u32[]{:S(2)}, u32[]{:S(2)}) collective-permute-start(f32[16,128]{1,0:T(8,128)S(1)} %add.26), channel_id=1, source_target_pairs={{0,96},{8,104},{16,112},{24,120},{32,64},{40,72},{48,80},{56,88},{... | collective-permute-start | bytes 24584 | tf_op jit(solution)/shard_map/ppermute | solution.py:712

commit v4 on v3

--- a/solution.py
+++ b/solution.py
@@ -306,9 +306,8 @@
 
 
 def count_kernel(
-    index, kept, to_cmp_kept, to_rcv_kept, most, diag, *refs, first
+    index, kept, to_cmp_kept, to_rcv_kept, most, diag, hot_even, hot_odd, ids, to_cmp, to_rcv, *, first
 ):
-    *handed, hot_even, hot_odd, ids, to_cmp, to_rcv = refs
     step = pl.program_id(0)
     even = first + 2 * step
 
@@ -326,9 +325,7 @@
         to_cmp[...] += cmp_counts
         to_rcv[...] += rcv_counts
         diag[...] += jnp.sum(rows, axis=0, keepdims=True)
-        part = kept_part(rows)
-        for out in [kept] + handed:
-            out[place * SRC_G : (place + 1) * SRC_G] = part
+        kept[place * SRC_G : (place + 1) * SRC_G] = kept_part(rows)
         most[...] = jnp.maximum(most[...], peak(rows))
 
     fill_hot(index[even + 1], ids, hot_odd)
@@ -338,8 +335,8 @@
 
     @pl.when(step == COUNT_STEPS - 1)
     def _():
-        to_cmp_kept[...] = (to_cmp[...].astype(jnp.int32) & (EXACT - 1)).astype(jnp.int8)
-        to_rcv_kept[...] = (to_rcv[...].astype(jnp.int32) & (EXACT - 1)).astype(jnp.int8)
+        to_cmp_kept[...] = kept_part(to_cmp[...])
+        to_rcv_kept[...] = kept_part(to_rcv[...])
         most[...] = jnp.maximum(most[...], jnp.maximum(peak(to_cmp[...]), peak(to_rcv[...])))
 
 
@@ -364,24 +361,8 @@
             use_both(left_over(to_cmp[...]), left_over(to_rcv[...]))
 
 
-def fetch_counts(refs, held, held_cmp, held_rcv, sems):
-    *halves, cmp_1, cmp_2, rcv_1, rcv_2 = refs
-    pieces = []
-    for half, source in enumerate(halves):
-        for chunk in range(CHUNKS // 2):
-            start = chunk * CHUNK_ROWS
-            place = held.at[half * (CHUNKS // 2) + chunk]
-            pieces.append((source.at[start : start + CHUNK_ROWS], place))
-    pieces += [(cmp_1, held_cmp.at[0]), (cmp_2, held_cmp.at[1])]
-    pieces += [(rcv_1, held_rcv.at[0]), (rcv_2, held_rcv.at[1])]
-    copies = [pltpu.make_async_copy(a, b, sems.at[k]) for k, (a, b) in enumerate(pieces)]
-    for copy in copies:
-        copy.start()
-    return copies
-
-
-def sum_halves(held):
-    return (held[0].astype(F32) + held[1].astype(F32)).astype(BF16)
+def sum_halves(first, last):
+    return (first[...].astype(F32) + last[...].astype(F32)).astype(BF16)
 
 
 def load_halves(tab, rcv, own, shared):
@@ -396,24 +377,18 @@
 
 
 def normal_kernel(
-    first, cmp_1, cmp_2, rcv_1, rcv_2, tab_in, rcv_in, last, diag_1, diag_2, most_1, most_2, index,
-    tab, rcv, own_count, own, shared, to_shared, to_own,
-    held, held_cmp, held_rcv, sems, hot, ids, exact_cmp, exact_rcv,
+    first, last, cmp_1, cmp_2, rcv_1, rcv_2, tab_in, rcv_in, diag_1, diag_2, most_1, most_2, index,
+    tab, rcv, own_count, own, shared, to_shared, to_own, hot, ids, exact_cmp, exact_rcv,
 ):
-    counts = (first, cmp_1, cmp_2, rcv_1, rcv_2)
-    copies = fetch_counts(counts, held, held_cmp, held_rcv, sems)
     top = 2 * SLICE
     half = HALF * SRC_G
     load_halves(tab_in, rcv_in, own, shared)
     lanes = lax.broadcasted_iota(jnp.int32, (16, SHARED), 1)
     shared[top:] = jnp.where(lanes < LANES, 1.0, 0.0).astype(BF16)
-    to_shared[...] = jnp.dot(own[:, half:], last[...], preferred_element_type=F32)
+    sums = jnp.dot(own[:, :half], first[...], preferred_element_type=F32)
+    to_shared[...] = sums + jnp.dot(own[:, half:], last[...], preferred_element_type=F32)
+    to_own[:, :half] = nt_dot(shared[...], first[...])
     to_own[:, half:] = nt_dot(shared[...], last[...])
-    for chunk in range(CHUNKS // 2):
-        copies[chunk].wait()
-        span = slice(chunk * CHUNK_ROWS, (chunk + 1) * CHUNK_ROWS)
-        to_shared[...] += jnp.dot(own[:, span], held[chunk], preferred_element_type=F32)
-        to_own[:, span] = nt_dot(shared[...], held[chunk])
 
     def others(to_cmp, to_rcv):
         cmp_sums = jnp.dot(shared[:top, :OR], to_cmp, preferred_element_type=F32)
@@ -428,9 +403,7 @@
         to_shared[...] += jnp.dot(own[:, span], rows, preferred_element_type=F32)
         to_own[:, span] += nt_dot(shared[...], rows)
 
-    for copy in copies[-4:]:
-        copy.wait()
-    others(sum_halves(held_cmp), sum_halves(held_rcv))
+    others(sum_halves(cmp_1, cmp_2), sum_halves(rcv_1, rcv_2))
     add_left_over(most_1, most_2, index, hot, ids, exact_cmp, exact_rcv, others, use_rows)
     diag = diag_1[...] + diag_2[...]
     for tile in range(N_SHOT):
@@ -463,11 +436,8 @@
 def norm_kernel(
     first, last, cmp_1, cmp_2, rcv_1, rcv_2,
     tab_b, rcv_b, tab_y, rcv_y, diag_1, diag_2, most_1, most_2, index, own_count,
-    out, tab_z, rcv_z, own, shared, to_shared,
-    held, held_cmp, held_rcv, sems, hot, ids, exact_cmp, exact_rcv,
+    out, tab_z, rcv_z, own, shared, to_shared, hot, ids, exact_cmp, exact_rcv,
 ):
-    counts = (first, last, cmp_1, cmp_2, rcv_1, rcv_2)
-    copies = fetch_counts(counts, held, held_cmp, held_rcv, sems)
     shared_b = tab_b[:LIVE_ROWS]
     shared_y = tab_y[:LIVE_ROWS]
     shift = all_sum(shared_b * shared_y) / all_sum(shared_b * shared_b)
@@ -477,11 +447,9 @@
     tab_z[...] = shared_z
     rcv_z[...] = own_z
     load_halves(tab_z, rcv_z, own, shared)
-    for chunk in range(CHUNKS):
-        copies[chunk].wait()
-        span = slice(chunk * CHUNK_ROWS, (chunk + 1) * CHUNK_ROWS)
-        sums = jnp.dot(own[:, span], held[chunk], preferred_element_type=F32)
-        to_shared[...] = sums if chunk == 0 else to_shared[...] + sums
+    half = HALF * SRC_G
+    sums = jnp.dot(own[:, :half], first[...], preferred_element_type=F32)
+    to_shared[...] = sums + jnp.dot(own[:, half:], last[...], preferred_element_type=F32)
 
     def whole(tabs, own):
         return all_sum(tabs) * (1.0 / N_RCV) + all_sum(own)
@@ -496,9 +464,7 @@
         span = pl.ds(pl.multiple_of(block * SRC_G, SRC_G), SRC_G)
         to_shared[...] += jnp.dot(own[:, span], rows, preferred_element_type=F32)
 
-    for copy in copies[-4:]:
-        copy.wait()
-    others(sum_halves(held_cmp), sum_halves(held_rcv))
+    others(sum_halves(cmp_1, cmp_2), sum_halves(rcv_1, rcv_2))
     add_left_over(most_1, most_2, index, hot, ids, exact_cmp, exact_rcv, others, use_rows)
     tiles = [tab_z[at(OFF_TILE)]] + [rcv_z[tile] for tile in range(RCV_TILES)]
     tiles += [tab_z[at(tile)] for tile in range(CMP_TILE, LIVE_TILES)]
@@ -559,53 +525,41 @@
 def count_call(index, first):
     rows = pl.BlockSpec((2 * SRC_G, SHARED), lambda c: (c, 0))
     small = [whole_spec(*TO_CMP), whole_spec(*TO_RCV), whole_spec(1, LANES), whole_spec(1, SHARED)]
-    handed = [] if first == 0 else [jax.ShapeDtypeStruct(COUNTS, BF16)]
     return pl.pallas_call(
         functools.partial(count_kernel, first=first),
         grid=(COUNT_STEPS,),
         in_specs=[whole_spec(*INDEX)],
-        out_specs=[rows] + small + [rows] * len(handed),
+        out_specs=[rows] + small,
         out_shape=[
-            pltpu.HBM(COUNTS, BF16),
-            pltpu.HBM(TO_CMP, jnp.int8),
-            pltpu.HBM(TO_RCV, jnp.int8),
+            VMEM(COUNTS, BF16),
+            VMEM(TO_CMP, BF16),
+            VMEM(TO_RCV, BF16),
             jax.ShapeDtypeStruct((1, LANES), F32),
             jax.ShapeDtypeStruct((1, SHARED), F32),
-        ]
-        + handed,
+        ],
         scratch_shapes=[VMEM((ROWS, TR_DEV), FP8)] * 2
         + [VMEM((256, LANES), BF16), VMEM(TO_CMP, F32), VMEM(TO_RCV, F32)],
-        compiler_params=params(24),
+        compiler_params=params(16),
         cost_estimate=cost(6),
         name="count_pairs",
     )(index)
 
 
-def count_scratch(chunks):
-    return (
-        [
-            VMEM((chunks, CHUNK_ROWS, SHARED), BF16),
-            VMEM((2,) + TO_CMP, jnp.int8),
-            VMEM((2,) + TO_RCV, jnp.int8),
-            pltpu.SemaphoreType.DMA((chunks + 4,)),
-        ]
-        + hot_scratch()
-        + [VMEM(TO_CMP, F32), VMEM(TO_RCV, F32)]
-    )
+def exact_scratch():
+    return hot_scratch() + [VMEM(TO_CMP, F32), VMEM(TO_RCV, F32)]
 
 
 def count_operands(counts):
-    big = in_hbm(*[array for pair in zip(counts[0][:3], counts[1][:3]) for array in pair])
-    (most_1, diag_1), (most_2, diag_2) = counts[0][3:5], counts[1][3:5]
+    pairs = [array for pair in zip(counts[0][:3], counts[1][:3]) for array in pair]
+    big = [pltpu.with_memory_space_constraint(array, VMEM) for array in pairs]
+    (most_1, diag_1), (most_2, diag_2) = counts[0][3:], counts[1][3:]
     return big, [diag_1, diag_2, most_1, most_2]
 
 
 def normal_apply(tab, rcv, index, counts):
-    (first, _, *rest), small = count_operands(counts)
-    last = counts[1][5]
+    big, small = count_operands(counts)
     return pl.pallas_call(
         normal_kernel,
-        in_specs=[ANYWHERE] * 5 + [IN_VMEM] * 8,
         out_shape=table_shapes() + [jax.ShapeDtypeStruct((N_SHOT, LANES), F32)],
         scratch_shapes=[
             VMEM((2 * SLICE, N_SHOT * SRC_G), BF16),
@@ -613,18 +567,17 @@
             VMEM((2 * SLICE, SHARED), F32),
             VMEM((2 * SLICE + 16, N_SHOT * SRC_G), F32),
         ]
-        + count_scratch(CHUNKS // 2),
-        compiler_params=params(24),
+        + exact_scratch(),
+        compiler_params=params(16),
         cost_estimate=cost(3),
         name="normal_apply",
-    )(first, *rest, tab, rcv, last, *small, index)
+    )(*big, tab, rcv, *small, index)
 
 
 def norm_sums(tab_b, rcv_b, tab_y, rcv_y, own_count, index, counts):
     big, small = count_operands(counts)
     return pl.pallas_call(
         norm_kernel,
-        in_specs=[ANYWHERE] * 6 + [IN_VMEM] * 10,
         out_shape=jax.ShapeDtypeStruct((1, LANES), F32),
         scratch_shapes=[
             VMEM((LIVE_ROWS, LANES), F32),
@@ -633,8 +586,8 @@
             VMEM((2 * SLICE, SHARED), BF16),
             VMEM((2 * SLICE, SHARED), F32),
         ]
-        + count_scratch(CHUNKS),
-        compiler_params=params(24),
+        + exact_scratch(),
+        compiler_params=params(16),
         cost_estimate=cost(2),
         name="norm_sums",
     )(*big, tab_b, rcv_b, tab_y, rcv_y, *small, index, own_count)

time: 136 us -> 136 us (level)
  Pallas kernels: 34.2 us -> 29.8 us
  local copies, waits for them, and re-layouts: 2.76 us -> 6.73 us
    unnamed x4 -> x48, local copies, waits for them, and re-layouts: 2.76 us -> 6.73 us
    pallas_call x2, Pallas kernels: 6.93 us -> 4.2 us  [the longest x1 2.86 us: normal_apply(): pl.pallas_call(normal_kernel, out_shape=table_shapes() + [jax.ShapeDtypeS...]
    pallas_call x2, Pallas kernels: 10.5 us -> 8.72 us  [count_call(): pl.pallas_call(functools.partial(count_kernel, first=first), grid=(COUNT_...]
  transfers between devices with their start and end apart: 11 -> 11, of which waited for: 10 -> 10; matrix products, arithmetic and copies ran while one was open for 0% -> 0% of each run, Pallas kernels for 11% -> 8%
where the time goes in v4:
time: 136 us; the launch traced here: 135 us
  blocking collectives  41.4 us (30%)
  Pallas kernels  29.8 us (22%)
  waiting for transfers between devices  29.2 us (21%)
  starting transfers between devices  27.1 us (20%)
  local copies, waits for them, and re-layouts  6.73 us (5%)
    all_to_all x2, blocking collectives, exchange(): return lax.all_to_all(array, axis, split_axis=0, concat_axis=0, tiled=True)  41.4 us
    all_to_all x4, starting transfers between devices, exchange(): return lax.all_to_all(array, axis, split_axis=0, concat_axis=0, tiled=True)  16.2 us
    ppermute x7, waiting for transfers between devices, swapped(): return lax.ppermute(value, axis, [(s, s ^ bit) for s in range(size)])  15.7 us
    all_to_all x4, waiting for transfers between devices, exchange(): return lax.all_to_all(array, axis, split_axis=0, concat_axis=0, tiled=True)  13.6 us
    ppermute x7, starting transfers between devices, swapped(): return lax.ppermute(value, axis, [(s, s ^ bit) for s in range(size)])  10.9 us
    pallas_call x2, Pallas kernels, count_call(): pl.pallas_call(functools.partial(count_kernel, first=first), grid=(COUNT_...  8.72 us
    pallas_call x1, Pallas kernels, adjoint_apply(): pl.pallas_call(adjoint_kernel, out_shape=table_shapes() + [jax.ShapeDtype...  7.49 us
    unnamed x48, local copies, waits for them, and re-layouts  6.73 us
  transfers between devices with their start and end apart: 11, of which 10 were waited for; matrix products, arithmetic and copies ran while one was open for 0% of the time, Pallas kernels for 8%

profile of v4, /device:TPU:0, one launch (start us, length us, event | category | flops | bytes accessed | tf_op | source)
XLA Modules:
  0.0 135.4 jit_solution(17708149443988502376)
XLA Ops:
  0.6 4.7 %spectra.1 = f32[16,200,128]{2,1,0:T(8,128)S(1)} custom-call(bf16[640,1024]{1,0:T(8,128)(2,1)} %traces.1, bf16[1024,1024]{1,0:T(8,128)(2,1)} %constant.10.clone.waves, s32[16,80]{1,0:T(8,128)} %bitcast.19, s32[1,16]{1,0:T(1,128)} %refs_1_.1, s32[16,80]{1,0:T(8,128)} %bitcast.20, s32[640]{0:T(1024)} %refs_3_.1, s32[640]{0:T(1024)} %refs_4_.1, s32[640]{0:T(1024)} %refs_5_.1), custom_call_target="tpu_custom_call" | custom-call | flops 5000000000 | bytes 15000000 | tf_op jit(solution)/shard_map/spectra/pallas_call | solution.py:172
  5.4 30.4 %all_to_all.53.data = f32[16,200,128]{2,1,0:T(8,128)S(1)} all-to-all(f32[16,200,128]{2,1,0:T(8,128)S(1)} %spectra.1), channel_id=1, replica_groups=mesh['shot'=16,'rcv'=8] {'shot'}, dimensions={0} | all-to-all | bytes 3276800 | tf_op jit(solution)/shard_map/all_to_all | solution.py:605
  35.8 7.5 %adjoint_apply.1 = (f32[704,128]{1,0:T(8,128)}, f32[2,32,128]{2,1,0:T(8,128)S(1)}, s32[16,24,128]{2,1,0:T(8,128)S(1)}) custom-call(f32[16,200,128]{2,1,0:T(8,128)S(1)} %all_to_all.53.data), custom_call_target="tpu_custom_call" | custom-call | flops 8000000000 | bytes 24000000 | tf_op jit(solution)/shard_map/adjoint_apply/pallas_call | solution.py:509
  43.3 5.3 %all-to-all-start.1 = ((f32[8,88,128]{2,1,0:T(8,128)}), f32[8,88,128]{2,1,0:T(8,128)S(1)}, u32[]{:S(2)}, u32[]{:S(2)}) async-start(f32[8,88,128]{2,1,0:T(8,128)} %bitcast.2), calls=%async_computation.1 | async-start | bytes 720896 | tf_op jit(solution)/shard_map/all_to_all | solution.py:605
  48.6 4.4 %count_pairs.2 = (bf16[1024,896]{1,0:T(8,128)(2,1)S(1)}, bf16[384,512]{1,0:T(8,128)(2,1)S(1)}, bf16[128,256]{1,0:T(8,128)(2,1)S(1)}, f32[1,128]{1,0:T(1,128)S(1)}, f32[1,896]{1,0:T(1,128)S(1)}) custom-call(s32[16,24,128]{2,1,0:T(8,128)S(1)} %get-tuple-element.43.index), custom_call_target="tpu_custom_call" | custom-call | flops 6000000000 | bytes 18000000 | tf_op jit(solution)/shard_map/count_pairs/pallas_call | solution.py:528
  53.0 4.2 %all-to-all-done.1 = f32[8,88,128]{2,1,0:T(8,128)S(1)} async-done(((f32[8,88,128]{2,1,0:T(8,128)}), f32[8,88,128]{2,1,0:T(8,128)S(1)}, u32[]{:S(2)}, u32[]{:S(2)}) %all-to-all-start.1) | async-done | bytes 360480 | tf_op jit(solution)/shard_map/all_to_all | solution.py:605
  57.9 3.4 %all-to-all-start.2 = ((f32[8,88,128]{2,1,0:T(8,128)}), f32[8,88,128]{2,1,0:T(8,128)S(1)}, u32[]{:S(2)}, u32[]{:S(2)}) async-start(f32[8,88,128]{2,1,0:T(8,128)} %bitcast.6), calls=%async_computation.2 | async-start | bytes 720896 | tf_op jit(solution)/shard_map/all_to_all | solution.py:605
  62.3 4.4 %count_pairs.3 = (bf16[1024,896]{1,0:T(8,128)(2,1)S(1)}, bf16[384,512]{1,0:T(8,128)(2,1)S(1)}, bf16[128,256]{1,0:T(8,128)(2,1)S(1)}, f32[1,128]{1,0:T(1,128)S(1)}, f32[1,896]{1,0:T(1,128)S(1)}) custom-call(s32[16,24,128]{2,1,0:T(8,128)S(1)} %copy-done.10), custom_call_target="tpu_custom_call" | custom-call | flops 6000000000 | bytes 18000000 | tf_op jit(solution)/shard_map/count_pairs/pallas_call | solution.py:528
  66.7 1.2 copy-done.2
  67.9 2.0 %all-to-all-done.2 = f32[8,88,128]{2,1,0:T(8,128)S(1)} async-done(((f32[8,88,128]{2,1,0:T(8,128)}), f32[8,88,128]{2,1,0:T(8,128)S(1)}, u32[]{:S(2)}, u32[]{:S(2)}) %all-to-all-start.2) | async-done | bytes 360480 | tf_op jit(solution)/shard_map/all_to_all | solution.py:605
  69.9 1.5 %copy-done.3 = bf16[1024,896]{1,0:T(8,128)(2,1)S(1)} copy-done((bf16[1024,896]{1,0:T(8,128)(2,1)S(1)}, bf16[1024,896]{1,0:T(8,128)(2,1)}, u32[]{:S(2)}) %copy-start.3) | copy-done | bytes 1835032
  71.4 2.9 %normal_apply.1 = (f32[704,128]{1,0:T(8,128)}, f32[2,32,128]{2,1,0:T(8,128)S(1)}, f32[16,128]{1,0:T(8,128)S(1)}) custom-call(bf16[1024,896]{1,0:T(8,128)(2,1)S(1)} %get-tuple-element.40.first, bf16[1024,896]{1,0:T(8,128)(2,1)S(1)} %copy-done.3, bf16[384,512]{1,0:T(8,128)(2,1)S(1)} %get-tuple-element.45.cmp_1, bf16[384,512]{1,0:T(8,128)(2,1)S(1)} %get-tuple-element.46.cmp_2, ...), custom_call_target="tpu_custom_call" | custom-call | flops 3000000000 | bytes 9000000 | tf_op jit(solution)/shard_map/normal_apply/pallas_call | solution.py:561
  74.3 3.4 %all-to-all-start.3 = ((f32[8,88,128]{2,1,0:T(8,128)}), f32[8,88,128]{2,1,0:T(8,128)S(1)}, u32[]{:S(2)}, u32[]{:S(2)}) async-start(f32[8,88,128]{2,1,0:T(8,128)} %bitcast.8), calls=%async_computation.3 | async-start | bytes 720896 | tf_op jit(solution)/shard_map/all_to_all | solution.py:605
  78.8 7.4 %all-to-all-done.3 = f32[8,88,128]{2,1,0:T(8,128)S(1)} async-done(((f32[8,88,128]{2,1,0:T(8,128)}), f32[8,88,128]{2,1,0:T(8,128)S(1)}, u32[]{:S(2)}, u32[]{:S(2)}) %all-to-all-start.3) | async-done | bytes 360480 | tf_op jit(solution)/shard_map/all_to_all | solution.py:605
  86.3 11.0 %all_to_all.54 = f32[8,88,128]{2,1,0:T(8,128)S(1)} all-to-all(f32[8,88,128]{2,1,0:T(8,128)S(1)} %sum_shares.3), channel_id=1, replica_groups=mesh['shot'=16,'rcv'=8] {'rcv'}, dimensions={0} | all-to-all | bytes 720896 | tf_op jit(solution)/shard_map/all_to_all | solution.py:605
  98.4 4.0 %all-to-all-start.5 = ((f32[16,160,128]{2,1,0:T(8,128)}), f32[16,160,128]{2,1,0:T(8,128)S(1)}, u32[]{:S(2)}, u32[]{:S(2)}) async-start(f32[16,160,128]{2,1,0:T(8,128)} %pack_owned.3), calls=%async_computation.5 | async-start | bytes 2621440 | tf_op jit(solution)/shard_map/all_to_all | solution.py:605
  102.6 1.5 %copy-done.1 = bf16[1024,896]{1,0:T(8,128)(2,1)S(1)} copy-done((bf16[1024,896]{1,0:T(8,128)(2,1)S(1)}, bf16[1024,896]{1,0:T(8,128)(2,1)}, u32[]{:S(2)}) %copy-start.1) | copy-done | bytes 1835032
  104.1 1.5 %copy-done.4 = bf16[1024,896]{1,0:T(8,128)(2,1)S(1)} copy-done((bf16[1024,896]{1,0:T(8,128)(2,1)S(1)}, bf16[1024,896]{1,0:T(8,128)(2,1)}, u32[]{:S(2)}) %copy-start.4) | copy-done | bytes 1835032
  105.6 1.3 norm_sums.1
  107.0 1.1 collective-permute-done
  108.7 3.0 %collective-permute-done.1 = f32[1,128]{1,0:T(1,128)S(1)} collective-permute-done((f32[1,128]{1,0:T(1,128)S(1)}, f32[1,128]{1,0:T(1,128)S(1)}, u32[]{:S(2)}, u32[]{:S(2)}) %collective-permute-start.1) | collective-permute-done | bytes 544 | tf_op jit(solution)/shard_map/ppermute | solution.py:665
  111.6 1.2 collective-permute-start.2
  112.8 3.6 %collective-permute-done.2 = f32[1,128]{1,0:T(1,128)S(1)} collective-permute-done((f32[1,128]{1,0:T(1,128)S(1)}, f32[1,128]{1,0:T(1,128)S(1)}, u32[]{:S(2)}, u32[]{:S(2)}) %collective-permute-start.2) | collective-permute-done | bytes 544 | tf_op jit(solution)/shard_map/ppermute | solution.py:665
  116.5 1.6 %collective-permute-start.3 = (f32[16,128]{1,0:T(8,128)S(1)}, f32[16,128]{1,0:T(8,128)S(1)}, u32[]{:S(2)}, u32[]{:S(2)}) collective-permute-start(f32[16,128]{1,0:T(8,128)S(1)} %broadcast_select_fusion), channel_id=1, source_target_pairs={{0,8},{8,0},{16,24},{24,16},{32,40},{40,32},{48,56},{56,48},{64,72... | collective-permute-start | bytes 24584 | tf_op jit(solution)/shard_map/ppermute | solution.py:665
  118.1 2.0 %collective-permute-done.3 = f32[16,128]{1,0:T(8,128)S(1)} collective-permute-done((f32[16,128]{1,0:T(8,128)S(1)}, f32[16,128]{1,0:T(8,128)S(1)}, u32[]{:S(2)}, u32[]{:S(2)}) %collective-permute-start.3) | collective-permute-done | bytes 8224 | tf_op jit(solution)/shard_map/ppermute | solution.py:665
  120.2 2.9 %collective-permute-start.4 = (f32[16,128]{1,0:T(8,128)S(1)}, f32[16,128]{1,0:T(8,128)S(1)}, u32[]{:S(2)}, u32[]{:S(2)}) collective-permute-start(f32[16,128]{1,0:T(8,128)S(1)} %fusion), channel_id=1, source_target_pairs={{0,24},{8,16},{16,8},{24,0},{32,56},{40,48},{48,40},{56,32},{64,88... | collective-permute-start | bytes 24584 | tf_op jit(solution)/shard_map/ppermute | solution.py:665
  123.1 2.0 %collective-permute-done.4 = f32[16,128]{1,0:T(8,128)S(1)} collective-permute-done((f32[16,128]{1,0:T(8,128)S(1)}, f32[16,128]{1,0:T(8,128)S(1)}, u32[]{:S(2)}, u32[]{:S(2)}) %collective-permute-start.4) | collective-permute-done | bytes 8224 | tf_op jit(solution)/shard_map/ppermute | solution.py:665
  125.2 1.7 %collective-permute-start.5 = (f32[16,128]{1,0:T(8,128)S(1)}, f32[16,128]{1,0:T(8,128)S(1)}, u32[]{:S(2)}, u32[]{:S(2)}) collective-permute-start(f32[16,128]{1,0:T(8,128)S(1)} %fusion.1), channel_id=1, source_target_pairs={{0,32},{8,40},{16,48},{24,56},{32,0},{40,8},{48,16},{56,24},{64,96... | collective-permute-start | bytes 24584 | tf_op jit(solution)/shard_map/ppermute | solution.py:665
  126.8 2.0 %collective-permute-done.5 = f32[16,128]{1,0:T(8,128)S(1)} collective-permute-done((f32[16,128]{1,0:T(8,128)S(1)}, f32[16,128]{1,0:T(8,128)S(1)}, u32[]{:S(2)}, u32[]{:S(2)}) %collective-permute-start.5) | collective-permute-done | bytes 8224 | tf_op jit(solution)/shard_map/ppermute | solution.py:665
  128.8 2.9 %collective-permute-start.6 = (f32[16,128]{1,0:T(8,128)S(1)}, f32[16,128]{1,0:T(8,128)S(1)}, u32[]{:S(2)}, u32[]{:S(2)}) collective-permute-start(f32[16,128]{1,0:T(8,128)S(1)} %add.26), channel_id=1, source_target_pairs={{0,96},{8,104},{16,112},{24,120},{32,64},{40,72},{48,80},{56,88},{... | collective-permute-start | bytes 24584 | tf_op jit(solution)/shard_map/ppermute | solution.py:665
  131.7 2.0 %collective-permute-done.6 = f32[16,128]{1,0:T(8,128)S(1)} collective-permute-done((f32[16,128]{1,0:T(8,128)S(1)}, f32[16,128]{1,0:T(8,128)S(1)}, u32[]{:S(2)}, u32[]{:S(2)}) %collective-permute-start.6) | collective-permute-done | bytes 8224 | tf_op jit(solution)/shard_map/ppermute | solution.py:665
  133.7 1.7 %finish.1 = (f32[128,512]{1,0:T(8,128)}, f32[1,16,512]{2,1,0:T(8,128)}, f32[128,512]{1,0:T(8,128)}, f32[32,512]{1,0:T(8,128)}) custom-call(f32[16,128]{1,0:T(8,128)S(1)} %add.27.sums, f32[16,160,128]{2,1,0:T(8,128)S(1)} %all-to-all-done.5.owned), custom_call_target="tpu_custom_call" | custom-call | tf_op jit(solution)/shard_map/finish/pallas_call | solution.py:723
  (60 shorter events, 4.8 us)
Async XLA Ops:
  43.3 9.7 %copy-start.9 = (s32[16,24,128]{2,1,0:T(8,128)}, s32[16,24,128]{2,1,0:T(8,128)S(1)}, u32[]{:S(2)}) copy-start(s32[16,24,128]{2,1,0:T(8,128)S(1)} %get-tuple-element.43.index) | copy-start | bytes 589828
  43.3 34.5 %copy-start.17 = (f32[2,32,128]{2,1,0:T(8,128)}, f32[2,32,128]{2,1,0:T(8,128)S(1)}, u32[]{:S(2)}) copy-start(f32[2,32,128]{2,1,0:T(8,128)S(1)} %get-tuple-element.50.rcv_in.rcv.rcv_b) | copy-start | bytes 98308
  43.3 13.9 %all-to-all-start.1 = ((f32[8,88,128]{2,1,0:T(8,128)}), f32[8,88,128]{2,1,0:T(8,128)S(1)}, u32[]{:S(2)}, u32[]{:S(2)}) async-start(f32[8,88,128]{2,1,0:T(8,128)} %bitcast.2), calls=%async_computation.1 | async-start | bytes 720896 | tf_op jit(solution)/shard_map/all_to_all | solution.py:605
  53.0 5.0 %copy-start.19 = (f32[1,128]{1,0:T(1,128)}, f32[1,128]{1,0:T(1,128)S(1)}, u32[]{:S(2)}) copy-start(f32[1,128]{1,0:T(1,128)S(1)} %get-tuple-element.53.most_1) | copy-start | bytes 1540
  53.0 16.9 %copy-start = (bf16[1024,896]{1,0:T(8,128)(2,1)}, bf16[1024,896]{1,0:T(8,128)(2,1)S(1)}, u32[]{:S(2)}) copy-start(bf16[1024,896]{1,0:T(8,128)(2,1)S(1)} %get-tuple-element.40.first) | copy-start | bytes 5505028
  53.0 16.9 %copy-start.5 = (bf16[384,512]{1,0:T(8,128)(2,1)}, bf16[384,512]{1,0:T(8,128)(2,1)S(1)}, u32[]{:S(2)}) copy-start(bf16[384,512]{1,0:T(8,128)(2,1)S(1)} %get-tuple-element.45.cmp_1) | copy-start | bytes 1179652
  53.0 16.9 %copy-start.13 = (bf16[128,256]{1,0:T(8,128)(2,1)}, bf16[128,256]{1,0:T(8,128)(2,1)S(1)}, u32[]{:S(2)}) copy-start(bf16[128,256]{1,0:T(8,128)(2,1)S(1)} %get-tuple-element.47.rcv_1) | copy-start | bytes 196612
  57.9 12.0 %all-to-all-start.2 = ((f32[8,88,128]{2,1,0:T(8,128)}), f32[8,88,128]{2,1,0:T(8,128)S(1)}, u32[]{:S(2)}, u32[]{:S(2)}) async-start(f32[8,88,128]{2,1,0:T(8,128)} %bitcast.6), calls=%async_computation.2 | async-start | bytes 720896 | tf_op jit(solution)/shard_map/all_to_all | solution.py:605
  62.3 7.6 %copy-start.11 = (s32[16,24,128]{2,1,0:T(8,128)S(1)}, s32[16,24,128]{2,1,0:T(8,128)}, u32[]{:S(2)}) copy-start(s32[16,24,128]{2,1,0:T(8,128)} %copy-done.9) | copy-start | bytes 589828
  62.3 7.6 %copy-start.20 = (f32[1,128]{1,0:T(1,128)S(1)}, f32[1,128]{1,0:T(1,128)}, u32[]{:S(2)}) copy-start(f32[1,128]{1,0:T(1,128)} %copy-done.19) | copy-start | bytes 1540
  67.9 6.4 %copy-start.7 = (bf16[384,512]{1,0:T(8,128)(2,1)}, bf16[384,512]{1,0:T(8,128)(2,1)S(1)}, u32[]{:S(2)}) copy-start(bf16[384,512]{1,0:T(8,128)(2,1)S(1)} %get-tuple-element.46.cmp_2) | copy-start | bytes 1179652
  67.9 6.4 %copy-start.15 = (bf16[128,256]{1,0:T(8,128)(2,1)}, bf16[128,256]{1,0:T(8,128)(2,1)S(1)}, u32[]{:S(2)}) copy-start(bf16[128,256]{1,0:T(8,128)(2,1)S(1)} %get-tuple-element.48.rcv_2) | copy-start | bytes 196612
  67.9 6.4 %copy-start.22 = (f32[1,128]{1,0:T(1,128)}, f32[1,128]{1,0:T(1,128)S(1)}, u32[]{:S(2)}) copy-start(f32[1,128]{1,0:T(1,128)S(1)} %get-tuple-element.54.most_2) | copy-start | bytes 1540
  69.9 1.5 %copy-start.3 = (bf16[1024,896]{1,0:T(8,128)(2,1)S(1)}, bf16[1024,896]{1,0:T(8,128)(2,1)}, u32[]{:S(2)}) copy-start(bf16[1024,896]{1,0:T(8,128)(2,1)} %copy-done.2) | copy-start | bytes 5505028
  74.3 12.0 %all-to-all-start.3 = ((f32[8,88,128]{2,1,0:T(8,128)}), f32[8,88,128]{2,1,0:T(8,128)S(1)}, u32[]{:S(2)}, u32[]{:S(2)}) async-start(f32[8,88,128]{2,1,0:T(8,128)} %bitcast.8), calls=%async_computation.3 | async-start | bytes 720896 | tf_op jit(solution)/shard_map/all_to_all | solution.py:605
  98.3 4.1 %copy-start.6 = (bf16[384,512]{1,0:T(8,128)(2,1)S(1)}, bf16[384,512]{1,0:T(8,128)(2,1)}, u32[]{:S(2)}) copy-start(bf16[384,512]{1,0:T(8,128)(2,1)} %copy-done.5) | copy-start | bytes 1179652
  98.4 4.1 %copy-start.8 = (bf16[384,512]{1,0:T(8,128)(2,1)S(1)}, bf16[384,512]{1,0:T(8,128)(2,1)}, u32[]{:S(2)}) copy-start(bf16[384,512]{1,0:T(8,128)(2,1)} %copy-done.7) | copy-start | bytes 1179652
  98.4 4.1 %copy-start.12 = (s32[16,24,128]{2,1,0:T(8,128)S(1)}, s32[16,24,128]{2,1,0:T(8,128)}, u32[]{:S(2)}) copy-start(s32[16,24,128]{2,1,0:T(8,128)} %copy-done.9) | copy-start | bytes 589828
  98.4 4.1 %copy-start.14 = (bf16[128,256]{1,0:T(8,128)(2,1)S(1)}, bf16[128,256]{1,0:T(8,128)(2,1)}, u32[]{:S(2)}) copy-start(bf16[128,256]{1,0:T(8,128)(2,1)} %copy-done.13) | copy-start | bytes 196612
  98.4 4.1 %copy-start.16 = (bf16[128,256]{1,0:T(8,128)(2,1)S(1)}, bf16[128,256]{1,0:T(8,128)(2,1)}, u32[]{:S(2)}) copy-start(bf16[128,256]{1,0:T(8,128)(2,1)} %copy-done.15) | copy-start | bytes 196612
  98.4 4.1 %copy-start.18 = (f32[2,32,128]{2,1,0:T(8,128)S(1)}, f32[2,32,128]{2,1,0:T(8,128)}, u32[]{:S(2)}) copy-start(f32[2,32,128]{2,1,0:T(8,128)} %copy-done.17) | copy-start | bytes 98308
  98.4 4.1 %copy-start.21 = (f32[1,128]{1,0:T(1,128)S(1)}, f32[1,128]{1,0:T(1,128)}, u32[]{:S(2)}) copy-start(f32[1,128]{1,0:T(1,128)} %copy-done.19) | copy-start | bytes 1540
  98.4 4.1 %copy-start.23 = (f32[1,128]{1,0:T(1,128)S(1)}, f32[1,128]{1,0:T(1,128)}, u32[]{:S(2)}) copy-start(f32[1,128]{1,0:T(1,128)} %copy-done.22) | copy-start | bytes 1540
  98.4 35.3 %all-to-all-start.5 = ((f32[16,160,128]{2,1,0:T(8,128)}), f32[16,160,128]{2,1,0:T(8,128)S(1)}, u32[]{:S(2)}, u32[]{:S(2)}) async-start(f32[16,160,128]{2,1,0:T(8,128)} %pack_owned.3), calls=%async_computation.5 | async-start | bytes 2621440 | tf_op jit(solution)/shard_map/all_to_all | solution.py:605
  102.5 1.5 %copy-start.1 = (bf16[1024,896]{1,0:T(8,128)(2,1)S(1)}, bf16[1024,896]{1,0:T(8,128)(2,1)}, u32[]{:S(2)}) copy-start(bf16[1024,896]{1,0:T(8,128)(2,1)} %copy-done) | copy-start | bytes 5505028
  106.9 1.2 collective-permute-start
  108.1 3.5 %collective-permute-start.1 = (f32[1,128]{1,0:T(1,128)S(1)}, f32[1,128]{1,0:T(1,128)S(1)}, u32[]{:S(2)}, u32[]{:S(2)}) collective-permute-start(f32[1,128]{1,0:T(1,128)S(1)} %add.21), channel_id=1, source_target_pairs={{0,2},{1,3},{2,0},{3,1},{4,6},{5,7},{6,4},{7,5},{8,10},{9,11},{10,... | collective-permute-start | bytes 1544 | tf_op jit(solution)/shard_map/ppermute | solution.py:665
  111.6 4.8 %collective-permute-start.2 = (f32[1,128]{1,0:T(1,128)S(1)}, f32[1,128]{1,0:T(1,128)S(1)}, u32[]{:S(2)}, u32[]{:S(2)}) collective-permute-start(f32[1,128]{1,0:T(1,128)S(1)} %add.22), channel_id=1, source_target_pairs={{0,6},{1,7},{2,4},{3,5},{4,2},{5,3},{6,0},{7,1},{8,14},{9,15},{10,... | collective-permute-start | bytes 1544 | tf_op jit(solution)/shard_map/ppermute | solution.py:665
  116.5 3.7 %collective-permute-start.3 = (f32[16,128]{1,0:T(8,128)S(1)}, f32[16,128]{1,0:T(8,128)S(1)}, u32[]{:S(2)}, u32[]{:S(2)}) collective-permute-start(f32[16,128]{1,0:T(8,128)S(1)} %broadcast_select_fusion), channel_id=1, source_target_pairs={{0,8},{8,0},{16,24},{24,16},{32,40},{40,32},{48,56},{56,48},{64,72... | collective-permute-start | bytes 24584 | tf_op jit(solution)/shard_map/ppermute | solution.py:665
  120.2 4.9 %collective-permute-start.4 = (f32[16,128]{1,0:T(8,128)S(1)}, f32[16,128]{1,0:T(8,128)S(1)}, u32[]{:S(2)}, u32[]{:S(2)}) collective-permute-start(f32[16,128]{1,0:T(8,128)S(1)} %fusion), channel_id=1, source_target_pairs={{0,24},{8,16},{16,8},{24,0},{32,56},{40,48},{48,40},{56,32},{64,88... | collective-permute-start | bytes 24584 | tf_op jit(solution)/shard_map/ppermute | solution.py:665
  125.2 3.7 %collective-permute-start.5 = (f32[16,128]{1,0:T(8,128)S(1)}, f32[16,128]{1,0:T(8,128)S(1)}, u32[]{:S(2)}, u32[]{:S(2)}) collective-permute-start(f32[16,128]{1,0:T(8,128)S(1)} %fusion.1), channel_id=1, source_target_pairs={{0,32},{8,40},{16,48},{24,56},{32,0},{40,8},{48,16},{56,24},{64,96... | collective-permute-start | bytes 24584 | tf_op jit(solution)/shard_map/ppermute | solution.py:665
  128.8 4.9 %collective-permute-start.6 = (f32[16,128]{1,0:T(8,128)S(1)}, f32[16,128]{1,0:T(8,128)S(1)}, u32[]{:S(2)}, u32[]{:S(2)}) collective-permute-start(f32[16,128]{1,0:T(8,128)S(1)} %add.26), channel_id=1, source_target_pairs={{0,96},{8,104},{16,112},{24,120},{32,64},{40,72},{48,80},{56,88},{... | collective-permute-start | bytes 24584 | tf_op jit(solution)/shard_map/ppermute | solution.py:665
  (3 other events, 3.7 us)

commit v5 on v4

--- a/solution.py
+++ b/solution.py
@@ -306,7 +306,8 @@
 
 
 def count_kernel(
-    index, kept, to_cmp_kept, to_rcv_kept, most, diag, hot_even, hot_odd, ids, to_cmp, to_rcv, *, first
+    index, kept, cmp_kept, rcv_kept, most, diag, near, cmp_near, rcv_near,
+    hot_even, hot_odd, ids, to_cmp, to_rcv, *, first
 ):
     step = pl.program_id(0)
     even = first + 2 * step
@@ -325,7 +326,9 @@
         to_cmp[...] += cmp_counts
         to_rcv[...] += rcv_counts
         diag[...] += jnp.sum(rows, axis=0, keepdims=True)
-        kept[place * SRC_G : (place + 1) * SRC_G] = kept_part(rows)
+        part = kept_part(rows)
+        for out in (kept, near):
+            out[place * SRC_G : (place + 1) * SRC_G] = part
         most[...] = jnp.maximum(most[...], peak(rows))
 
     fill_hot(index[even + 1], ids, hot_odd)
@@ -335,8 +338,8 @@
 
     @pl.when(step == COUNT_STEPS - 1)
     def _():
-        to_cmp_kept[...] = kept_part(to_cmp[...])
-        to_rcv_kept[...] = kept_part(to_rcv[...])
+        cmp_kept[...] = cmp_near[...] = kept_part(to_cmp[...])
+        rcv_kept[...] = rcv_near[...] = kept_part(to_rcv[...])
         most[...] = jnp.maximum(most[...], jnp.maximum(peak(to_cmp[...]), peak(to_rcv[...])))
 
 
@@ -359,6 +362,21 @@
                 use_rows(block, left_over(rows))
 
             use_both(left_over(to_cmp[...]), left_over(to_rcv[...]))
+
+
+def fetch_counts(refs, held, held_cmp, held_rcv, sems):
+    first, last, cmp_1, cmp_2, rcv_1, rcv_2 = refs
+    pieces = []
+    for chunk in range(CHUNKS):
+        source = first if chunk < CHUNKS // 2 else last
+        start = chunk % (CHUNKS // 2) * CHUNK_ROWS
+        pieces.append((source.at[start : start + CHUNK_ROWS], held.at[chunk]))
+    pieces += [(cmp_1, held_cmp.at[0]), (cmp_2, held_cmp.at[1])]
+    pieces += [(rcv_1, held_rcv.at[0]), (rcv_2, held_rcv.at[1])]
+    copies = [pltpu.make_async_copy(a, b, sems.at[k]) for k, (a, b) in enumerate(pieces)]
+    for copy in copies:
+        copy.start()
+    return copies
 
 
 def sum_halves(first, last):
@@ -436,8 +454,11 @@
 def norm_kernel(
     first, last, cmp_1, cmp_2, rcv_1, rcv_2,
     tab_b, rcv_b, tab_y, rcv_y, diag_1, diag_2, most_1, most_2, index, own_count,
-    out, tab_z, rcv_z, own, shared, to_shared, hot, ids, exact_cmp, exact_rcv,
+    out, tab_z, rcv_z, own, shared, to_shared,
+    held, held_cmp, held_rcv, sems, hot, ids, exact_cmp, exact_rcv,
 ):
+    counts = (first, last, cmp_1, cmp_2, rcv_1, rcv_2)
+    copies = fetch_counts(counts, held, held_cmp, held_rcv, sems)
     shared_b = tab_b[:LIVE_ROWS]
     shared_y = tab_y[:LIVE_ROWS]
     shift = all_sum(shared_b * shared_y) / all_sum(shared_b * shared_b)
@@ -447,9 +468,11 @@
     tab_z[...] = shared_z
     rcv_z[...] = own_z
     load_halves(tab_z, rcv_z, own, shared)
-    half = HALF * SRC_G
-    sums = jnp.dot(own[:, :half], first[...], preferred_element_type=F32)
-    to_shared[...] = sums + jnp.dot(own[:, half:], last[...], preferred_element_type=F32)
+    for chunk in range(CHUNKS):
+        copies[chunk].wait()
+        span = slice(chunk * CHUNK_ROWS, (chunk + 1) * CHUNK_ROWS)
+        sums = jnp.dot(own[:, span], held[chunk], preferred_element_type=F32)
+        to_shared[...] = sums if chunk == 0 else to_shared[...] + sums
 
     def whole(tabs, own):
         return all_sum(tabs) * (1.0 / N_RCV) + all_sum(own)
@@ -464,7 +487,10 @@
         span = pl.ds(pl.multiple_of(block * SRC_G, SRC_G), SRC_G)
         to_shared[...] += jnp.dot(own[:, span], rows, preferred_element_type=F32)
 
-    others(sum_halves(cmp_1, cmp_2), sum_halves(rcv_1, rcv_2))
+    for copy in copies[CHUNKS:]:
+        copy.wait()
+    both_cmp = sum_halves(held_cmp.at[0], held_cmp.at[1])
+    others(both_cmp, sum_halves(held_rcv.at[0], held_rcv.at[1]))
     add_left_over(most_1, most_2, index, hot, ids, exact_cmp, exact_rcv, others, use_rows)
     tiles = [tab_z[at(OFF_TILE)]] + [rcv_z[tile] for tile in range(RCV_TILES)]
     tiles += [tab_z[at(tile)] for tile in range(CMP_TILE, LIVE_TILES)]
@@ -529,14 +555,10 @@
         functools.partial(count_kernel, first=first),
         grid=(COUNT_STEPS,),
         in_specs=[whole_spec(*INDEX)],
-        out_specs=[rows] + small,
-        out_shape=[
-            VMEM(COUNTS, BF16),
-            VMEM(TO_CMP, BF16),
-            VMEM(TO_RCV, BF16),
-            jax.ShapeDtypeStruct((1, LANES), F32),
-            jax.ShapeDtypeStruct((1, SHARED), F32),
-        ],
+        out_specs=[rows] + small + [rows] + small[:2],
+        out_shape=[pltpu.HBM(shape, BF16) for shape in (COUNTS, TO_CMP, TO_RCV)]
+        + [jax.ShapeDtypeStruct((1, LANES), F32), jax.ShapeDtypeStruct((1, SHARED), F32)]
+        + [VMEM(shape, BF16) for shape in (COUNTS, TO_CMP, TO_RCV)],
         scratch_shapes=[VMEM((ROWS, TR_DEV), FP8)] * 2
         + [VMEM((256, LANES), BF16), VMEM(TO_CMP, F32), VMEM(TO_RCV, F32)],
         compiler_params=params(16),
@@ -549,15 +571,17 @@
     return hot_scratch() + [VMEM(TO_CMP, F32), VMEM(TO_RCV, F32)]
 
 
-def count_operands(counts):
-    pairs = [array for pair in zip(counts[0][:3], counts[1][:3]) for array in pair]
-    big = [pltpu.with_memory_space_constraint(array, VMEM) for array in pairs]
-    (most_1, diag_1), (most_2, diag_2) = counts[0][3:], counts[1][3:]
+def count_operands(counts, first, space):
+    pairs = zip(counts[0][first : first + 3], counts[1][first : first + 3])
+    big = [
+        pltpu.with_memory_space_constraint(array, space) for pair in pairs for array in pair
+    ]
+    (most_1, diag_1), (most_2, diag_2) = counts[0][3:5], counts[1][3:5]
     return big, [diag_1, diag_2, most_1, most_2]
 
 
 def normal_apply(tab, rcv, index, counts):
-    big, small = count_operands(counts)
+    big, small = count_operands(counts, 5, VMEM)
     return pl.pallas_call(
         normal_kernel,
         out_shape=table_shapes() + [jax.ShapeDtypeStruct((N_SHOT, LANES), F32)],
@@ -575,9 +599,10 @@
 
 
 def norm_sums(tab_b, rcv_b, tab_y, rcv_y, own_count, index, counts):
-    big, small = count_operands(counts)
+    big, small = count_operands(counts, 0, pltpu.HBM)
     return pl.pallas_call(
         norm_kernel,
+        in_specs=[ANYWHERE] * 6 + [IN_VMEM] * 10,
         out_shape=jax.ShapeDtypeStruct((1, LANES), F32),
         scratch_shapes=[
             VMEM((LIVE_ROWS, LANES), F32),
@@ -585,9 +610,13 @@
             VMEM((2 * SLICE, N_SHOT * SRC_G), BF16),
             VMEM((2 * SLICE, SHARED), BF16),
             VMEM((2 * SLICE, SHARED), F32),
+            VMEM((CHUNKS, CHUNK_ROWS, SHARED), BF16),
+            VMEM((2,) + TO_CMP, BF16),
+            VMEM((2,) + TO_RCV, BF16),
+            pltpu.SemaphoreType.DMA((CHUNKS + 4,)),
         ]
         + exact_scratch(),
-        compiler_params=params(16),
+        compiler_params=params(24),
         cost_estimate=cost(2),
         name="norm_sums",
     )(*big, tab_b, rcv_b, tab_y, rcv_y, *small, index, own_count)

time: 136 us -> 136 us (level)
  Pallas kernels: 29.8 us -> 33.4 us
  waiting for transfers between devices: 29.2 us -> 27.5 us
    all_to_all x4, waiting for transfers between devices: 13.6 us -> 11.3 us  [exchange(): return lax.all_to_all(array, axis, split_axis=0, concat_axis=0, tiled=True)]
    pallas_call x2, Pallas kernels: 8.72 us -> 10.7 us  [count_call(): pl.pallas_call(functools.partial(count_kernel, first=first), grid=(COUNT_...]
    pallas_call x1, Pallas kernels: 1.34 us -> 2.91 us  [norm_sums(): pl.pallas_call(norm_kernel, in_specs=[ANYWHERE] * 6 + [IN_VMEM] * 10, out...]
    unnamed x48 -> x8, local copies, waits for them, and re-layouts: 6.73 us -> 5.52 us
  transfers between devices with their start and end apart: 11 -> 11, of which waited for: 10 -> 10; matrix products, arithmetic and copies ran while one was open for 0% -> 0% of each run, Pallas kernels for 8% -> 11%
where the time goes in v5:
time: 136 us; the launch traced here: 135 us
  blocking collectives  41.4 us (30%)
  Pallas kernels  33.4 us (25%)
  waiting for transfers between devices  27.5 us (20%)
  starting transfers between devices  26.7 us (20%)
  local copies, waits for them, and re-layouts  5.52 us (4%)
    all_to_all x2, blocking collectives, exchange(): return lax.all_to_all(array, axis, split_axis=0, concat_axis=0, tiled=True)  41.4 us
    ppermute x7, waiting for transfers between devices, swapped(): return lax.ppermute(value, axis, [(s, s ^ bit) for s in range(size)])  16.1 us
    all_to_all x4, starting transfers between devices, exchange(): return lax.all_to_all(array, axis, split_axis=0, concat_axis=0, tiled=True)  16.1 us
    all_to_all x4, waiting for transfers between devices, exchange(): return lax.all_to_all(array, axis, split_axis=0, concat_axis=0, tiled=True)  11.3 us
    pallas_call x2, Pallas kernels, count_call(): pl.pallas_call(functools.partial(count_kernel, first=first), grid=(COUNT_...  10.7 us
    ppermute x7, starting transfers between devices, swapped(): return lax.ppermute(value, axis, [(s, s ^ bit) for s in range(size)])  10.6 us
    pallas_call x1, Pallas kernels, adjoint_apply(): pl.pallas_call(adjoint_kernel, out_shape=table_shapes() + [jax.ShapeDtype...  7.44 us
    unnamed x8, local copies, waits for them, and re-layouts  5.52 us
  transfers between devices with their start and end apart: 11, of which 10 were waited for; matrix products, arithmetic and copies ran while one was open for 0% of the time, Pallas kernels for 11%

profile of v5, /device:TPU:0, one launch (start us, length us, event | category | flops | bytes accessed | tf_op | source)
XLA Modules:
  0.0 135.4 jit_solution(11699457659645363679)
XLA Ops:
  0.6 4.7 %spectra.1 = f32[16,200,128]{2,1,0:T(8,128)S(1)} custom-call(bf16[640,1024]{1,0:T(8,128)(2,1)} %traces.1, bf16[1024,1024]{1,0:T(8,128)(2,1)} %constant.10.clone.waves, s32[16,80]{1,0:T(8,128)} %bitcast.19, s32[1,16]{1,0:T(1,128)} %refs_1_.1, s32[16,80]{1,0:T(8,128)} %bitcast.20, s32[640]{0:T(1024)} %refs_3_.1, s32[640]{0:T(1024)} %refs_4_.1, s32[640]{0:T(1024)} %refs_5_.1), custom_call_target="tpu_custom_call" | custom-call | flops 5000000000 | bytes 15000000 | tf_op jit(solution)/shard_map/spectra/pallas_call | solution.py:172
  5.4 30.4 %all_to_all.53.data = f32[16,200,128]{2,1,0:T(8,128)S(1)} all-to-all(f32[16,200,128]{2,1,0:T(8,128)S(1)} %spectra.1), channel_id=1, replica_groups=mesh['shot'=16,'rcv'=8] {'shot'}, dimensions={0} | all-to-all | bytes 3276800 | tf_op jit(solution)/shard_map/all_to_all | solution.py:634
  35.8 7.4 %adjoint_apply.1 = (f32[704,128]{1,0:T(8,128)}, f32[2,32,128]{2,1,0:T(8,128)S(1)}, s32[16,24,128]{2,1,0:T(8,128)S(1)}) custom-call(f32[16,200,128]{2,1,0:T(8,128)S(1)} %all_to_all.53.data), custom_call_target="tpu_custom_call" | custom-call | flops 8000000000 | bytes 24000000 | tf_op jit(solution)/shard_map/adjoint_apply/pallas_call | solution.py:535
  43.2 5.3 %all-to-all-start.1 = ((f32[8,88,128]{2,1,0:T(8,128)}), f32[8,88,128]{2,1,0:T(8,128)S(1)}, u32[]{:S(2)}, u32[]{:S(2)}) async-start(f32[8,88,128]{2,1,0:T(8,128)} %bitcast.2), calls=%async_computation.1 | async-start | bytes 720896 | tf_op jit(solution)/shard_map/all_to_all | solution.py:634
  48.5 5.3 %count_pairs.2 = (bf16[1024,896]{1,0:T(8,128)(2,1)}, bf16[384,512]{1,0:T(8,128)(2,1)}, bf16[128,256]{1,0:T(8,128)(2,1)}, f32[1,128]{1,0:T(1,128)S(1)}, f32[1,896...) custom-call(s32[16,24,128]{2,1,0:T(8,128)S(1)} %get-tuple-element.55.index), custom_call_target="tpu_custom_call" | custom-call | flops 6000000000 | bytes 18000000 | tf_op jit(solution)/shard_map/count_pairs/pallas_call | solution.py:554
  53.9 1.3 copy-done
  55.1 2.0 %all-to-all-done.1 = f32[8,88,128]{2,1,0:T(8,128)S(1)} async-done(((f32[8,88,128]{2,1,0:T(8,128)}), f32[8,88,128]{2,1,0:T(8,128)S(1)}, u32[]{:S(2)}, u32[]{:S(2)}) %all-to-all-start.1) | async-done | bytes 360480 | tf_op jit(solution)/shard_map/all_to_all | solution.py:634
  58.0 3.4 %all-to-all-start.2 = ((f32[8,88,128]{2,1,0:T(8,128)}), f32[8,88,128]{2,1,0:T(8,128)S(1)}, u32[]{:S(2)}, u32[]{:S(2)}) async-start(f32[8,88,128]{2,1,0:T(8,128)} %bitcast.6), calls=%async_computation.2 | async-start | bytes 720896 | tf_op jit(solution)/shard_map/all_to_all | solution.py:634
  61.4 5.4 %count_pairs.3 = (bf16[1024,896]{1,0:T(8,128)(2,1)}, bf16[384,512]{1,0:T(8,128)(2,1)}, bf16[128,256]{1,0:T(8,128)(2,1)}, f32[1,128]{1,0:T(1,128)S(1)}, f32[1,896...) custom-call(s32[16,24,128]{2,1,0:T(8,128)S(1)} %get-tuple-element.55.index), custom_call_target="tpu_custom_call" | custom-call | flops 6000000000 | bytes 18000000 | tf_op jit(solution)/shard_map/count_pairs/pallas_call | solution.py:554
  66.8 1.3 copy-done.2
  68.0 1.9 %all-to-all-done.2 = f32[8,88,128]{2,1,0:T(8,128)S(1)} async-done(((f32[8,88,128]{2,1,0:T(8,128)}), f32[8,88,128]{2,1,0:T(8,128)S(1)}, u32[]{:S(2)}, u32[]{:S(2)}) %all-to-all-start.2) | async-done | bytes 360480 | tf_op jit(solution)/shard_map/all_to_all | solution.py:634
  69.9 1.5 %copy-done.1 = bf16[1024,896]{1,0:T(8,128)(2,1)S(1)} copy-done((bf16[1024,896]{1,0:T(8,128)(2,1)S(1)}, bf16[1024,896]{1,0:T(8,128)(2,1)}, u32[]{:S(2)}) %copy-start.1) | copy-done | bytes 1835032
  71.4 1.5 %copy-done.3 = bf16[1024,896]{1,0:T(8,128)(2,1)S(1)} copy-done((bf16[1024,896]{1,0:T(8,128)(2,1)S(1)}, bf16[1024,896]{1,0:T(8,128)(2,1)}, u32[]{:S(2)}) %copy-start.3) | copy-done | bytes 1835032
  72.9 2.9 %normal_apply.1 = (f32[704,128]{1,0:T(8,128)}, f32[2,32,128]{2,1,0:T(8,128)S(1)}, f32[16,128]{1,0:T(8,128)S(1)}) custom-call(bf16[1024,896]{1,0:T(8,128)(2,1)S(1)} %copy-done.1, bf16[1024,896]{1,0:T(8,128)(2,1)S(1)} %copy-done.3, bf16[384,512]{1,0:T(8,128)(2,1)S(1)} %get-tuple-element.65.cmp_1, bf16[384,512]{1,0:T(8,128)(2,1)S(1)} %get-tuple-element.66.cmp_2, ...), custom_call_target="tpu_custom_call" | custom-call | flops 3000000000 | bytes 9000000 | tf_op jit(solution)/shard_map/normal_apply/pallas_call | solution.py:585
  75.8 3.4 %all-to-all-start.3 = ((f32[8,88,128]{2,1,0:T(8,128)}), f32[8,88,128]{2,1,0:T(8,128)S(1)}, u32[]{:S(2)}, u32[]{:S(2)}) async-start(f32[8,88,128]{2,1,0:T(8,128)} %bitcast.8), calls=%async_computation.3 | async-start | bytes 720896 | tf_op jit(solution)/shard_map/all_to_all | solution.py:634
  80.3 7.4 %all-to-all-done.3 = f32[8,88,128]{2,1,0:T(8,128)S(1)} async-done(((f32[8,88,128]{2,1,0:T(8,128)}), f32[8,88,128]{2,1,0:T(8,128)S(1)}, u32[]{:S(2)}, u32[]{:S(2)}) %all-to-all-start.3) | async-done | bytes 360480 | tf_op jit(solution)/shard_map/all_to_all | solution.py:634
  87.8 11.0 %all_to_all.54 = f32[8,88,128]{2,1,0:T(8,128)S(1)} all-to-all(f32[8,88,128]{2,1,0:T(8,128)S(1)} %sum_shares.3), channel_id=1, replica_groups=mesh['shot'=16,'rcv'=8] {'rcv'}, dimensions={0} | all-to-all | bytes 720896 | tf_op jit(solution)/shard_map/all_to_all | solution.py:634
  99.9 3.9 %all-to-all-start.5 = ((f32[16,160,128]{2,1,0:T(8,128)}), f32[16,160,128]{2,1,0:T(8,128)S(1)}, u32[]{:S(2)}, u32[]{:S(2)}) async-start(f32[16,160,128]{2,1,0:T(8,128)} %pack_owned.3), calls=%async_computation.5 | async-start | bytes 2621440 | tf_op jit(solution)/shard_map/all_to_all | solution.py:634
  103.8 2.9 %norm_sums.1 = f32[1,128]{1,0:T(1,128)S(1)} custom-call(bf16[1024,896]{1,0:T(8,128)(2,1)} %get-tuple-element.52.first, bf16[1024,896]{1,0:T(8,128)(2,1)} %get-tuple-element.56.last, bf16[384,512]{1,0:T(8,128)(2,1)} %get-tuple-element.57.cmp_1, bf16[384,512]{1,0:T(8,128)(2,1)} %get-tuple-element.58.cmp_2, bf16[128,256]{1,0:T(8,128)(2,1)} %get-tuple-element.59.rcv_1, ...), custom_call_target="tpu_custom_call" | custom-call | flops 2000000000 | bytes 6000000 | tf_op jit(solution)/shard_map/norm_sums/pallas_call | solution.py:603
  106.8 1.1 collective-permute-done
  108.4 3.0 %collective-permute-done.1 = f32[1,128]{1,0:T(1,128)S(1)} collective-permute-done((f32[1,128]{1,0:T(1,128)S(1)}, f32[1,128]{1,0:T(1,128)S(1)}, u32[]{:S(2)}, u32[]{:S(2)}) %collective-permute-start.1) | collective-permute-done | bytes 544 | tf_op jit(solution)/shard_map/ppermute | solution.py:694
  111.4 1.2 collective-permute-start.2
  112.6 3.6 %collective-permute-done.2 = f32[1,128]{1,0:T(1,128)S(1)} collective-permute-done((f32[1,128]{1,0:T(1,128)S(1)}, f32[1,128]{1,0:T(1,128)S(1)}, u32[]{:S(2)}, u32[]{:S(2)}) %collective-permute-start.2) | collective-permute-done | bytes 544 | tf_op jit(solution)/shard_map/ppermute | solution.py:694
  116.2 1.6 %collective-permute-start.3 = (f32[16,128]{1,0:T(8,128)S(1)}, f32[16,128]{1,0:T(8,128)S(1)}, u32[]{:S(2)}, u32[]{:S(2)}) collective-permute-start(f32[16,128]{1,0:T(8,128)S(1)} %broadcast_select_fusion), channel_id=1, source_target_pairs={{0,8},{8,0},{16,24},{24,16},{32,40},{40,32},{48,56},{56,48},{64,72... | collective-permute-start | bytes 24584 | tf_op jit(solution)/shard_map/ppermute | solution.py:694
  117.9 2.2 %collective-permute-done.3 = f32[16,128]{1,0:T(8,128)S(1)} collective-permute-done((f32[16,128]{1,0:T(8,128)S(1)}, f32[16,128]{1,0:T(8,128)S(1)}, u32[]{:S(2)}, u32[]{:S(2)}) %collective-permute-start.3) | collective-permute-done | bytes 8224 | tf_op jit(solution)/shard_map/ppermute | solution.py:694
  120.2 2.7 %collective-permute-start.4 = (f32[16,128]{1,0:T(8,128)S(1)}, f32[16,128]{1,0:T(8,128)S(1)}, u32[]{:S(2)}, u32[]{:S(2)}) collective-permute-start(f32[16,128]{1,0:T(8,128)S(1)} %fusion), channel_id=1, source_target_pairs={{0,24},{8,16},{16,8},{24,0},{32,56},{40,48},{48,40},{56,32},{64,88... | collective-permute-start | bytes 24584 | tf_op jit(solution)/shard_map/ppermute | solution.py:694
  122.9 2.2 %collective-permute-done.4 = f32[16,128]{1,0:T(8,128)S(1)} collective-permute-done((f32[16,128]{1,0:T(8,128)S(1)}, f32[16,128]{1,0:T(8,128)S(1)}, u32[]{:S(2)}, u32[]{:S(2)}) %collective-permute-start.4) | collective-permute-done | bytes 8224 | tf_op jit(solution)/shard_map/ppermute | solution.py:694
  125.1 1.6 %collective-permute-start.5 = (f32[16,128]{1,0:T(8,128)S(1)}, f32[16,128]{1,0:T(8,128)S(1)}, u32[]{:S(2)}, u32[]{:S(2)}) collective-permute-start(f32[16,128]{1,0:T(8,128)S(1)} %fusion.1), channel_id=1, source_target_pairs={{0,32},{8,40},{16,48},{24,56},{32,0},{40,8},{48,16},{56,24},{64,96... | collective-permute-start | bytes 24584 | tf_op jit(solution)/shard_map/ppermute | solution.py:694
  126.8 2.0 %collective-permute-done.5 = f32[16,128]{1,0:T(8,128)S(1)} collective-permute-done((f32[16,128]{1,0:T(8,128)S(1)}, f32[16,128]{1,0:T(8,128)S(1)}, u32[]{:S(2)}, u32[]{:S(2)}) %collective-permute-start.5) | collective-permute-done | bytes 8224 | tf_op jit(solution)/shard_map/ppermute | solution.py:694
  128.8 2.9 %collective-permute-start.6 = (f32[16,128]{1,0:T(8,128)S(1)}, f32[16,128]{1,0:T(8,128)S(1)}, u32[]{:S(2)}, u32[]{:S(2)}) collective-permute-start(f32[16,128]{1,0:T(8,128)S(1)} %add.26), channel_id=1, source_target_pairs={{0,96},{8,104},{16,112},{24,120},{32,64},{40,72},{48,80},{56,88},{... | collective-permute-start | bytes 24584 | tf_op jit(solution)/shard_map/ppermute | solution.py:694
  131.7 2.0 %collective-permute-done.6 = f32[16,128]{1,0:T(8,128)S(1)} collective-permute-done((f32[16,128]{1,0:T(8,128)S(1)}, f32[16,128]{1,0:T(8,128)S(1)}, u32[]{:S(2)}, u32[]{:S(2)}) %collective-permute-start.6) | collective-permute-done | bytes 8224 | tf_op jit(solution)/shard_map/ppermute | solution.py:694
  133.7 1.7 %finish.1 = (f32[128,512]{1,0:T(8,128)}, f32[1,16,512]{2,1,0:T(8,128)}, f32[128,512]{1,0:T(8,128)}, f32[32,512]{1,0:T(8,128)}) custom-call(f32[16,128]{1,0:T(8,128)S(1)} %add.27.sums, f32[16,160,128]{2,1,0:T(8,128)S(1)} %all-to-all-done.5.owned), custom_call_target="tpu_custom_call" | custom-call | tf_op jit(solution)/shard_map/finish/pallas_call | solution.py:752
  (20 shorter events, 3.9 us)
Async XLA Ops:
  43.2 13.9 %all-to-all-start.1 = ((f32[8,88,128]{2,1,0:T(8,128)}), f32[8,88,128]{2,1,0:T(8,128)S(1)}, u32[]{:S(2)}, u32[]{:S(2)}) async-start(f32[8,88,128]{2,1,0:T(8,128)} %bitcast.2), calls=%async_computation.1 | async-start | bytes 720896 | tf_op jit(solution)/shard_map/all_to_all | solution.py:634
  53.9 1.3 copy-start
  58.0 12.0 %all-to-all-start.2 = ((f32[8,88,128]{2,1,0:T(8,128)}), f32[8,88,128]{2,1,0:T(8,128)S(1)}, u32[]{:S(2)}, u32[]{:S(2)}) async-start(f32[8,88,128]{2,1,0:T(8,128)} %bitcast.6), calls=%async_computation.2 | async-start | bytes 720896 | tf_op jit(solution)/shard_map/all_to_all | solution.py:634
  66.8 1.3 copy-start.2
  69.9 1.5 %copy-start.1 = (bf16[1024,896]{1,0:T(8,128)(2,1)S(1)}, bf16[1024,896]{1,0:T(8,128)(2,1)}, u32[]{:S(2)}) copy-start(bf16[1024,896]{1,0:T(8,128)(2,1)} %copy-done) | copy-start | bytes 5505028
  71.4 1.5 %copy-start.3 = (bf16[1024,896]{1,0:T(8,128)(2,1)S(1)}, bf16[1024,896]{1,0:T(8,128)(2,1)}, u32[]{:S(2)}) copy-start(bf16[1024,896]{1,0:T(8,128)(2,1)} %copy-done.2) | copy-start | bytes 5505028
  75.8 12.0 %all-to-all-start.3 = ((f32[8,88,128]{2,1,0:T(8,128)}), f32[8,88,128]{2,1,0:T(8,128)S(1)}, u32[]{:S(2)}, u32[]{:S(2)}) async-start(f32[8,88,128]{2,1,0:T(8,128)} %bitcast.8), calls=%async_computation.3 | async-start | bytes 720896 | tf_op jit(solution)/shard_map/all_to_all | solution.py:634
  99.9 33.8 %all-to-all-start.5 = ((f32[16,160,128]{2,1,0:T(8,128)}), f32[16,160,128]{2,1,0:T(8,128)S(1)}, u32[]{:S(2)}, u32[]{:S(2)}) async-start(f32[16,160,128]{2,1,0:T(8,128)} %pack_owned.3), calls=%async_computation.5 | async-start | bytes 2621440 | tf_op jit(solution)/shard_map/all_to_all | solution.py:634
  106.7 1.2 collective-permute-start
  107.9 3.5 %collective-permute-start.1 = (f32[1,128]{1,0:T(1,128)S(1)}, f32[1,128]{1,0:T(1,128)S(1)}, u32[]{:S(2)}, u32[]{:S(2)}) collective-permute-start(f32[1,128]{1,0:T(1,128)S(1)} %add.21), channel_id=1, source_target_pairs={{0,2},{1,3},{2,0},{3,1},{4,6},{5,7},{6,4},{7,5},{8,10},{9,11},{10,... | collective-permute-start | bytes 1544 | tf_op jit(solution)/shard_map/ppermute | solution.py:694
  111.4 4.8 %collective-permute-start.2 = (f32[1,128]{1,0:T(1,128)S(1)}, f32[1,128]{1,0:T(1,128)S(1)}, u32[]{:S(2)}, u32[]{:S(2)}) collective-permute-start(f32[1,128]{1,0:T(1,128)S(1)} %add.22), channel_id=1, source_target_pairs={{0,6},{1,7},{2,4},{3,5},{4,2},{5,3},{6,0},{7,1},{8,14},{9,15},{10,... | collective-permute-start | bytes 1544 | tf_op jit(solution)/shard_map/ppermute | solution.py:694
  116.2 3.9 %collective-permute-start.3 = (f32[16,128]{1,0:T(8,128)S(1)}, f32[16,128]{1,0:T(8,128)S(1)}, u32[]{:S(2)}, u32[]{:S(2)}) collective-permute-start(f32[16,128]{1,0:T(8,128)S(1)} %broadcast_select_fusion), channel_id=1, source_target_pairs={{0,8},{8,0},{16,24},{24,16},{32,40},{40,32},{48,56},{56,48},{64,72... | collective-permute-start | bytes 24584 | tf_op jit(solution)/shard_map/ppermute | solution.py:694
  120.2 4.9 %collective-permute-start.4 = (f32[16,128]{1,0:T(8,128)S(1)}, f32[16,128]{1,0:T(8,128)S(1)}, u32[]{:S(2)}, u32[]{:S(2)}) collective-permute-start(f32[16,128]{1,0:T(8,128)S(1)} %fusion), channel_id=1, source_target_pairs={{0,24},{8,16},{16,8},{24,0},{32,56},{40,48},{48,40},{56,32},{64,88... | collective-permute-start | bytes 24584 | tf_op jit(solution)/shard_map/ppermute | solution.py:694
  125.1 3.7 %collective-permute-start.5 = (f32[16,128]{1,0:T(8,128)S(1)}, f32[16,128]{1,0:T(8,128)S(1)}, u32[]{:S(2)}, u32[]{:S(2)}) collective-permute-start(f32[16,128]{1,0:T(8,128)S(1)} %fusion.1), channel_id=1, source_target_pairs={{0,32},{8,40},{16,48},{24,56},{32,0},{40,8},{48,16},{56,24},{64,96... | collective-permute-start | bytes 24584 | tf_op jit(solution)/shard_map/ppermute | solution.py:694
  128.8 4.9 %collective-permute-start.6 = (f32[16,128]{1,0:T(8,128)S(1)}, f32[16,128]{1,0:T(8,128)S(1)}, u32[]{:S(2)}, u32[]{:S(2)}) collective-permute-start(f32[16,128]{1,0:T(8,128)S(1)} %add.26), channel_id=1, source_target_pairs={{0,96},{8,104},{16,112},{24,120},{32,64},{40,72},{48,80},{56,88},{... | collective-permute-start | bytes 24584 | tf_op jit(solution)/shard_map/ppermute | solution.py:694

commit v6 on v3

--- a/solution.py
+++ b/solution.py
@@ -45,6 +45,7 @@
 DATA_ROWS = INDEX_AT + INDEX_ROWS
 STEPS = 2
 OWN_ROWS = 2 * SLICE + SLICE // 2
+TURNED_ROWS = 2 * LANES + CMP_G + RCV_G // N_SHOT
 PACK = LANES // CMP_G
 
 VMEM = pltpu.VMEM
@@ -306,9 +307,8 @@
 
 
 def count_kernel(
-    index, kept, to_cmp_kept, to_rcv_kept, most, diag, *refs, first
+    index, kept, to_cmp_kept, to_rcv_kept, most, diag, hot_even, hot_odd, ids, to_cmp, to_rcv, *, first
 ):
-    *handed, hot_even, hot_odd, ids, to_cmp, to_rcv = refs
     step = pl.program_id(0)
     even = first + 2 * step
 
@@ -326,9 +326,7 @@
         to_cmp[...] += cmp_counts
         to_rcv[...] += rcv_counts
         diag[...] += jnp.sum(rows, axis=0, keepdims=True)
-        part = kept_part(rows)
-        for out in [kept] + handed:
-            out[place * SRC_G : (place + 1) * SRC_G] = part
+        kept[place * SRC_G : (place + 1) * SRC_G] = kept_part(rows)
         most[...] = jnp.maximum(most[...], peak(rows))
 
     fill_hot(index[even + 1], ids, hot_odd)
@@ -396,23 +394,21 @@
 
 
 def normal_kernel(
-    first, cmp_1, cmp_2, rcv_1, rcv_2, tab_in, rcv_in, last, diag_1, diag_2, most_1, most_2, index,
+    first, last, cmp_1, cmp_2, rcv_1, rcv_2, tab_in, rcv_in, diag_1, diag_2, most_1, most_2, index,
     tab, rcv, own_count, own, shared, to_shared, to_own,
     held, held_cmp, held_rcv, sems, hot, ids, exact_cmp, exact_rcv,
 ):
-    counts = (first, cmp_1, cmp_2, rcv_1, rcv_2)
+    counts = (first, last, cmp_1, cmp_2, rcv_1, rcv_2)
     copies = fetch_counts(counts, held, held_cmp, held_rcv, sems)
     top = 2 * SLICE
-    half = HALF * SRC_G
     load_halves(tab_in, rcv_in, own, shared)
     lanes = lax.broadcasted_iota(jnp.int32, (16, SHARED), 1)
     shared[top:] = jnp.where(lanes < LANES, 1.0, 0.0).astype(BF16)
-    to_shared[...] = jnp.dot(own[:, half:], last[...], preferred_element_type=F32)
-    to_own[:, half:] = nt_dot(shared[...], last[...])
-    for chunk in range(CHUNKS // 2):
+    for chunk in range(CHUNKS):
         copies[chunk].wait()
         span = slice(chunk * CHUNK_ROWS, (chunk + 1) * CHUNK_ROWS)
-        to_shared[...] += jnp.dot(own[:, span], held[chunk], preferred_element_type=F32)
+        sums = jnp.dot(own[:, span], held[chunk], preferred_element_type=F32)
+        to_shared[...] = sums if chunk == 0 else to_shared[...] + sums
         to_own[:, span] = nt_dot(shared[...], held[chunk])
 
     def others(to_cmp, to_rcv):
@@ -559,20 +555,18 @@
 def count_call(index, first):
     rows = pl.BlockSpec((2 * SRC_G, SHARED), lambda c: (c, 0))
     small = [whole_spec(*TO_CMP), whole_spec(*TO_RCV), whole_spec(1, LANES), whole_spec(1, SHARED)]
-    handed = [] if first == 0 else [jax.ShapeDtypeStruct(COUNTS, BF16)]
     return pl.pallas_call(
         functools.partial(count_kernel, first=first),
         grid=(COUNT_STEPS,),
         in_specs=[whole_spec(*INDEX)],
-        out_specs=[rows] + small + [rows] * len(handed),
+        out_specs=[rows] + small,
         out_shape=[
             pltpu.HBM(COUNTS, BF16),
             pltpu.HBM(TO_CMP, jnp.int8),
             pltpu.HBM(TO_RCV, jnp.int8),
             jax.ShapeDtypeStruct((1, LANES), F32),
             jax.ShapeDtypeStruct((1, SHARED), F32),
-        ]
-        + handed,
+        ],
         scratch_shapes=[VMEM((ROWS, TR_DEV), FP8)] * 2
         + [VMEM((256, LANES), BF16), VMEM(TO_CMP, F32), VMEM(TO_RCV, F32)],
         compiler_params=params(24),
@@ -601,11 +595,10 @@
 
 
 def normal_apply(tab, rcv, index, counts):
-    (first, _, *rest), small = count_operands(counts)
-    last = counts[1][5]
+    big, small = count_operands(counts)
     return pl.pallas_call(
         normal_kernel,
-        in_specs=[ANYWHERE] * 5 + [IN_VMEM] * 8,
+        in_specs=[ANYWHERE] * 6 + [IN_VMEM] * 7,
         out_shape=table_shapes() + [jax.ShapeDtypeStruct((N_SHOT, LANES), F32)],
         scratch_shapes=[
             VMEM((2 * SLICE, N_SHOT * SRC_G), BF16),
@@ -613,11 +606,11 @@
             VMEM((2 * SLICE, SHARED), F32),
             VMEM((2 * SLICE + 16, N_SHOT * SRC_G), F32),
         ]
-        + count_scratch(CHUNKS // 2),
+        + count_scratch(CHUNKS),
         compiler_params=params(24),
         cost_estimate=cost(3),
         name="normal_apply",
-    )(first, *rest, tab, rcv, last, *small, index)
+    )(*big, tab, rcv, *small, index)
 
 
 def norm_sums(tab_b, rcv_b, tab_y, rcv_y, own_count, index, counts):
@@ -722,7 +715,38 @@
     return rows
 
 
-def finish_kernel(sums, owned, source, receiver, offset, cmp):
+def turn_kernel(owned, turned):
+    def spread_halves(tile):
+        return jnp.concatenate([tile, pltpu.roll(tile, LANES // 2, 1)], axis=0)
+
+    per_tile = LANES // SLICE
+    for which in range(2):
+        first = which * OWN_ROWS
+        for group in range(N_SHOT // per_tile):
+            span = slice(group * LANES, (group + 1) * LANES)
+            senders = range(group * per_tile, (group + 1) * per_tile)
+            for place in range(2):
+                start = first + place * SLICE
+                tile = [owned[i, start : start + SLICE] for i in senders]
+                rows = slice(place * LANES, (place + 1) * LANES)
+                turned[which, rows, span] = jnp.concatenate(tile, axis=0).T
+            start = first + 2 * SLICE
+            rest = [spread_halves(owned[i, start : start + SLICE // 2]) for i in senders]
+            rest = jnp.concatenate(rest, axis=0).T
+            turned[which, 2 * LANES :, span] = rest[: TURNED_ROWS - 2 * LANES]
+
+
+def turn(owned):
+    return pl.pallas_call(
+        turn_kernel,
+        out_shape=jax.ShapeDtypeStruct((2, TURNED_ROWS, FREQS), F32),
+        compiler_params=params(16),
+        cost_estimate=cost(2),
+        name="turn_owned",
+    )(owned)
+
+
+def finish_kernel(sums, turned, source, receiver, offset, cmp):
     rows = sums[...]
     norm_b, cross, norm_z, norm_az, shift = (rows[:, lane : lane + 1] for lane in range(5))
     shift = shift * (1.0 / N_RCV)
@@ -744,29 +768,16 @@
     scale_b = (first + second) / det
     scale_y = 1.0 / det
 
-    def combine(sender, start, stop):
-        part_y = owned[sender, OWN_ROWS + start : OWN_ROWS + stop]
-        return scale_b * owned[sender, start:stop] - scale_y * part_y
-
-    def spread_halves(tile):
-        return jnp.concatenate([tile, pltpu.roll(tile, LANES // 2, 1)], axis=0)
-
-    per_tile = LANES // SLICE
-    for group in range(N_SHOT // per_tile):
-        span = slice(group * LANES, (group + 1) * LANES)
-        senders = range(group * per_tile, (group + 1) * per_tile)
-        source[:, span] = jnp.concatenate([combine(i, 0, SLICE) for i in senders], axis=0).T
-        offset[:, span] = jnp.concatenate(
-            [combine(i, SLICE, 2 * SLICE) for i in senders], axis=0
-        ).T
-        rest = jnp.concatenate(
-            [spread_halves(combine(i, 2 * SLICE, OWN_ROWS)) for i in senders], axis=0
-        ).T
-        cmp[:, span] = rest[:CMP_G]
-        receiver[0, :, span] = rest[CMP_G : CMP_G + RCV_G // N_SHOT]
-
-
-def finish(sums, owned):
+    def combine(start, stop):
+        return scale_b * turned[0, start:stop] - scale_y * turned[1, start:stop]
+
+    source[...] = combine(0, LANES)
+    offset[...] = combine(LANES, 2 * LANES)
+    cmp[...] = combine(2 * LANES, 2 * LANES + CMP_G)
+    receiver[0] = combine(2 * LANES + CMP_G, TURNED_ROWS)
+
+
+def finish(sums, turned):
     return pl.pallas_call(
         finish_kernel,
         out_shape=[
@@ -775,9 +786,10 @@
             jax.ShapeDtypeStruct((128, FREQS), F32),
             jax.ShapeDtypeStruct((CMP_G, FREQS), F32),
         ],
-        compiler_params=params(),
+        compiler_params=params(16),
+        cost_estimate=cost(1),
         name="finish",
-    )(sums, owned)
+    )(sums, turned)
 
 
 def per_device(basis, traces, src_index, rcv_index, off_index, send_rows, send_counts, recv_bins):
@@ -804,7 +816,7 @@
     tab_y, packed = lax.optimization_barrier((tab_y, packed))
     owned = exchange(packed, "shot")
     sums = norm_sums(tab_b, rcv_b, tab_y, rcv_y, own_count, index, counts)
-    return tuple(finish(gather_sums(sums), owned))
+    return tuple(finish(gather_sums(sums), turn(owned)))
 
 
 def solution(mesh):

time: 136 us -> 135 us (level)
  local copies, waits for them, and re-layouts: 2.76 us -> 0 us
    unnamed x4 -> x0, local copies, waits for them, and re-layouts: 2.76 us -> none
    pallas_call x1 -> x2, Pallas kernels: 3.98 us -> 5.28 us  [the longest x1 4.74 us: normal_apply(): pl.pallas_call(normal_kernel, in_specs=[ANYWHERE] * 6 + [IN_VMEM] * 7, ou...]
where the time goes in v6:
time: 135 us; the launch traced here: 134 us
  blocking collectives  41.4 us (31%)
  Pallas kernels  35.2 us (26%)
  waiting for transfers between devices  30.1 us (22%)
  starting transfers between devices  26.8 us (20%)
    all_to_all x2, blocking collectives, exchange(): return lax.all_to_all(array, axis, split_axis=0, concat_axis=0, tiled=True)  41.4 us
    all_to_all x4, starting transfers between devices, exchange(): return lax.all_to_all(array, axis, split_axis=0, concat_axis=0, tiled=True)  16.1 us
    ppermute x7, waiting for transfers between devices, swapped(): return lax.ppermute(value, axis, [(s, s ^ bit) for s in range(size)])  16 us
    all_to_all x4, waiting for transfers between devices, exchange(): return lax.all_to_all(array, axis, split_axis=0, concat_axis=0, tiled=True)  14.1 us
    ppermute x7, starting transfers between devices, swapped(): return lax.ppermute(value, axis, [(s, s ^ bit) for s in range(size)])  10.7 us
    pallas_call x2, Pallas kernels, count_call(): pl.pallas_call(functools.partial(count_kernel, first=first), grid=(COUNT_...  10.5 us
    pallas_call x1, Pallas kernels, adjoint_apply(): pl.pallas_call(adjoint_kernel, out_shape=table_shapes() + [jax.ShapeDtype...  7.45 us
    pallas_call x1, Pallas kernels, normal_apply(): pl.pallas_call(normal_kernel, in_specs=[ANYWHERE] * 6 + [IN_VMEM] * 7, ou...  4.74 us
  transfers between devices with their start and end apart: 11, of which 10 were waited for; matrix products, arithmetic and copies ran while one was open for 0% of the time, Pallas kernels for 11%

profile of v6, /device:TPU:0, one launch (start us, length us, event | category | flops | bytes accessed | tf_op | source)
XLA Modules:
  0.0 134.4 jit_solution(12128820867770967731)
XLA Ops:
  0.6 4.7 %spectra.1 = f32[16,200,128]{2,1,0:T(8,128)S(1)} custom-call(bf16[640,1024]{1,0:T(8,128)(2,1)} %traces.1, bf16[1024,1024]{1,0:T(8,128)(2,1)} %constant.10.clone.waves, s32[16,80]{1,0:T(8,128)} %bitcast.19, s32[1,16]{1,0:T(1,128)} %refs_1_.1, s32[16,80]{1,0:T(8,128)} %bitcast.20, s32[640]{0:T(1024)} %refs_3_.1, s32[640]{0:T(1024)} %refs_4_.1, s32[640]{0:T(1024)} %refs_5_.1), custom_call_target="tpu_custom_call" | custom-call | flops 5000000000 | bytes 15000000 | tf_op jit(solution)/shard_map/spectra/pallas_call | solution.py:173
  5.4 30.4 %all_to_all.53.data = f32[16,200,128]{2,1,0:T(8,128)S(1)} all-to-all(f32[16,200,128]{2,1,0:T(8,128)S(1)} %spectra.1), channel_id=1, replica_groups=mesh['shot'=16,'rcv'=8] {'shot'}, dimensions={0} | all-to-all | bytes 3276800 | tf_op jit(solution)/shard_map/all_to_all | solution.py:645
  35.8 7.4 %adjoint_apply.1 = (f32[704,128]{1,0:T(8,128)}, f32[2,32,128]{2,1,0:T(8,128)S(1)}, s32[16,24,128]{2,1,0:T(8,128)S(1)}) custom-call(f32[16,200,128]{2,1,0:T(8,128)S(1)} %all_to_all.53.data), custom_call_target="tpu_custom_call" | custom-call | flops 8000000000 | bytes 24000000 | tf_op jit(solution)/shard_map/adjoint_apply/pallas_call | solution.py:539
  43.2 5.3 %all-to-all-start.1 = ((f32[8,88,128]{2,1,0:T(8,128)}), f32[8,88,128]{2,1,0:T(8,128)S(1)}, u32[]{:S(2)}, u32[]{:S(2)}) async-start(f32[8,88,128]{2,1,0:T(8,128)} %bitcast.2), calls=%async_computation.1 | async-start | bytes 720896 | tf_op jit(solution)/shard_map/all_to_all | solution.py:645
  48.5 5.2 %count_pairs.2 = (bf16[1024,896]{1,0:T(8,128)(2,1)}, s8[384,512]{1,0:T(32,128)(4,1)}, s8[128,256]{1,0:T(32,128)(4,1)}, f32[1,128]{1,0:T(1,128)S(1)}, f32[1,896]{1,0:T(1,128)S(1)}) custom-call(s32[16,24,128]{2,1,0:T(8,128)S(1)} %get-tuple-element.43.index), custom_call_target="tpu_custom_call" | custom-call | flops 6000000000 | bytes 18000000 | tf_op jit(solution)/shard_map/count_pairs/pallas_call | solution.py:558
  53.8 3.4 %all-to-all-done.1 = f32[8,88,128]{2,1,0:T(8,128)S(1)} async-done(((f32[8,88,128]{2,1,0:T(8,128)}), f32[8,88,128]{2,1,0:T(8,128)S(1)}, u32[]{:S(2)}, u32[]{:S(2)}) %all-to-all-start.1) | async-done | bytes 360480 | tf_op jit(solution)/shard_map/all_to_all | solution.py:645
  57.1 0.8 sum_shares.2
  57.9 3.4 %all-to-all-start.2 = ((f32[8,88,128]{2,1,0:T(8,128)}), f32[8,88,128]{2,1,0:T(8,128)S(1)}, u32[]{:S(2)}, u32[]{:S(2)}) async-start(f32[8,88,128]{2,1,0:T(8,128)} %bitcast.6), calls=%async_computation.2 | async-start | bytes 720896 | tf_op jit(solution)/shard_map/all_to_all | solution.py:645
  61.3 5.2 %count_pairs.3 = (bf16[1024,896]{1,0:T(8,128)(2,1)}, s8[384,512]{1,0:T(32,128)(4,1)}, s8[128,256]{1,0:T(32,128)(4,1)}, f32[1,128]{1,0:T(1,128)S(1)}, f32[1,896]{1,0:T(1,128)S(1)}) custom-call(s32[16,24,128]{2,1,0:T(8,128)S(1)} %get-tuple-element.43.index), custom_call_target="tpu_custom_call" | custom-call | flops 6000000000 | bytes 18000000 | tf_op jit(solution)/shard_map/count_pairs/pallas_call | solution.py:558
  66.6 3.3 %all-to-all-done.2 = f32[8,88,128]{2,1,0:T(8,128)S(1)} async-done(((f32[8,88,128]{2,1,0:T(8,128)}), f32[8,88,128]{2,1,0:T(8,128)S(1)}, u32[]{:S(2)}, u32[]{:S(2)}) %all-to-all-start.2) | async-done | bytes 360480 | tf_op jit(solution)/shard_map/all_to_all | solution.py:645
  69.9 4.7 %normal_apply.1 = (f32[704,128]{1,0:T(8,128)}, f32[2,32,128]{2,1,0:T(8,128)S(1)}, f32[16,128]{1,0:T(8,128)S(1)}) custom-call(bf16[1024,896]{1,0:T(8,128)(2,1)} %get-tuple-element.40.first, bf16[1024,896]{1,0:T(8,128)(2,1)} %get-tuple-element.44.last, s8[384,512]{1,0:T(32,128)(4,1)} %get-tuple-element.45.cmp_1, s8[384,512]{1,0:T(32,128)(4,1)} %get-tuple-element.46.cmp_2, ...), custom_call_target="tpu_custom_call" | custom-call | flops 3000000000 | bytes 9000000 | tf_op jit(solution)/shard_map/normal_apply/pallas_call | solution.py:599
  74.6 3.5 %all-to-all-start.3 = ((f32[8,88,128]{2,1,0:T(8,128)}), f32[8,88,128]{2,1,0:T(8,128)S(1)}, u32[]{:S(2)}, u32[]{:S(2)}) async-start(f32[8,88,128]{2,1,0:T(8,128)} %bitcast.8), calls=%async_computation.3 | async-start | bytes 720896 | tf_op jit(solution)/shard_map/all_to_all | solution.py:645
  78.1 1.1 pack_owned.2.refs_0_
  79.1 7.4 %all-to-all-done.3 = f32[8,88,128]{2,1,0:T(8,128)S(1)} async-done(((f32[8,88,128]{2,1,0:T(8,128)}), f32[8,88,128]{2,1,0:T(8,128)S(1)}, u32[]{:S(2)}, u32[]{:S(2)}) %all-to-all-start.3) | async-done | bytes 360480 | tf_op jit(solution)/shard_map/all_to_all | solution.py:645
  86.6 11.0 %all_to_all.54 = f32[8,88,128]{2,1,0:T(8,128)S(1)} all-to-all(f32[8,88,128]{2,1,0:T(8,128)S(1)} %sum_shares.3), channel_id=1, replica_groups=mesh['shot'=16,'rcv'=8] {'rcv'}, dimensions={0} | all-to-all | bytes 720896 | tf_op jit(solution)/shard_map/all_to_all | solution.py:645
  97.6 1.1 pack_owned.3
  98.6 3.9 %all-to-all-start.5 = ((f32[16,160,128]{2,1,0:T(8,128)}), f32[16,160,128]{2,1,0:T(8,128)S(1)}, u32[]{:S(2)}, u32[]{:S(2)}) async-start(f32[16,160,128]{2,1,0:T(8,128)} %pack_owned.3), calls=%async_computation.5 | async-start | bytes 2621440 | tf_op jit(solution)/shard_map/all_to_all | solution.py:645
  102.6 3.0 %norm_sums.1 = f32[1,128]{1,0:T(1,128)S(1)} custom-call(bf16[1024,896]{1,0:T(8,128)(2,1)} %get-tuple-element.40.first, bf16[1024,896]{1,0:T(8,128)(2,1)} %get-tuple-element.44.last, s8[384,512]{1,0:T(32,128)(4,1)} %get-tuple-element.45.cmp_1, s8[384,512]{1,0:T(32,128)(4,1)} %get-tuple-element.46.cmp_2, s8[128,256]{1,0:T(32,128)(4,1)} %get-tuple-element.47.rcv_1, ...), custom_call_target="tpu_custom_call" | custom-call | flops 2000000000 | bytes 6000000 | tf_op jit(solution)/shard_map/norm_sums/pallas_call | solution.py:618
  105.6 1.1 collective-permute-done
  106.7 0.6 collective-permute-start.1
  107.3 3.0 %collective-permute-done.1 = f32[1,128]{1,0:T(1,128)S(1)} collective-permute-done((f32[1,128]{1,0:T(1,128)S(1)}, f32[1,128]{1,0:T(1,128)S(1)}, u32[]{:S(2)}, u32[]{:S(2)}) %collective-permute-start.1) | collective-permute-done | bytes 544 | tf_op jit(solution)/shard_map/ppermute | solution.py:705
  110.3 1.2 collective-permute-start.2
  111.4 3.6 %collective-permute-done.2 = f32[1,128]{1,0:T(1,128)S(1)} collective-permute-done((f32[1,128]{1,0:T(1,128)S(1)}, f32[1,128]{1,0:T(1,128)S(1)}, u32[]{:S(2)}, u32[]{:S(2)}) %collective-permute-start.2) | collective-permute-done | bytes 544 | tf_op jit(solution)/shard_map/ppermute | solution.py:705
  115.1 1.6 %collective-permute-start.3 = (f32[16,128]{1,0:T(8,128)S(1)}, f32[16,128]{1,0:T(8,128)S(1)}, u32[]{:S(2)}, u32[]{:S(2)}) collective-permute-start(f32[16,128]{1,0:T(8,128)S(1)} %broadcast_select_fusion), channel_id=1, source_target_pairs={{0,8},{8,0},{16,24},{24,16},{32,40},{40,32},{48,56},{56,48},{64,72... | collective-permute-start | bytes 24584 | tf_op jit(solution)/shard_map/ppermute | solution.py:705
  116.7 2.2 %collective-permute-done.3 = f32[16,128]{1,0:T(8,128)S(1)} collective-permute-done((f32[16,128]{1,0:T(8,128)S(1)}, f32[16,128]{1,0:T(8,128)S(1)}, u32[]{:S(2)}, u32[]{:S(2)}) %collective-permute-start.3) | collective-permute-done | bytes 8224 | tf_op jit(solution)/shard_map/ppermute | solution.py:705
  119.0 2.7 %collective-permute-start.4 = (f32[16,128]{1,0:T(8,128)S(1)}, f32[16,128]{1,0:T(8,128)S(1)}, u32[]{:S(2)}, u32[]{:S(2)}) collective-permute-start(f32[16,128]{1,0:T(8,128)S(1)} %fusion), channel_id=1, source_target_pairs={{0,24},{8,16},{16,8},{24,0},{32,56},{40,48},{48,40},{56,32},{64,88... | collective-permute-start | bytes 24584 | tf_op jit(solution)/shard_map/ppermute | solution.py:705
  121.7 2.2 %collective-permute-done.4 = f32[16,128]{1,0:T(8,128)S(1)} collective-permute-done((f32[16,128]{1,0:T(8,128)S(1)}, f32[16,128]{1,0:T(8,128)S(1)}, u32[]{:S(2)}, u32[]{:S(2)}) %collective-permute-start.4) | collective-permute-done | bytes 8224 | tf_op jit(solution)/shard_map/ppermute | solution.py:705
  123.9 1.6 %collective-permute-start.5 = (f32[16,128]{1,0:T(8,128)S(1)}, f32[16,128]{1,0:T(8,128)S(1)}, u32[]{:S(2)}, u32[]{:S(2)}) collective-permute-start(f32[16,128]{1,0:T(8,128)S(1)} %fusion.1), channel_id=1, source_target_pairs={{0,32},{8,40},{16,48},{24,56},{32,0},{40,8},{48,16},{56,24},{64,96... | collective-permute-start | bytes 24584 | tf_op jit(solution)/shard_map/ppermute | solution.py:705
  125.6 2.0 %collective-permute-done.5 = f32[16,128]{1,0:T(8,128)S(1)} collective-permute-done((f32[16,128]{1,0:T(8,128)S(1)}, f32[16,128]{1,0:T(8,128)S(1)}, u32[]{:S(2)}, u32[]{:S(2)}) %collective-permute-start.5) | collective-permute-done | bytes 8224 | tf_op jit(solution)/shard_map/ppermute | solution.py:705
  127.6 2.9 %collective-permute-start.6 = (f32[16,128]{1,0:T(8,128)S(1)}, f32[16,128]{1,0:T(8,128)S(1)}, u32[]{:S(2)}, u32[]{:S(2)}) collective-permute-start(f32[16,128]{1,0:T(8,128)S(1)} %add.26), channel_id=1, source_target_pairs={{0,96},{8,104},{16,112},{24,120},{32,64},{40,72},{48,80},{56,88},{... | collective-permute-start | bytes 24584 | tf_op jit(solution)/shard_map/ppermute | solution.py:705
  130.5 2.0 %collective-permute-done.6 = f32[16,128]{1,0:T(8,128)S(1)} collective-permute-done((f32[16,128]{1,0:T(8,128)S(1)}, f32[16,128]{1,0:T(8,128)S(1)}, u32[]{:S(2)}, u32[]{:S(2)}) %collective-permute-start.6) | collective-permute-done | bytes 8224 | tf_op jit(solution)/shard_map/ppermute | solution.py:705
  133.0 1.4 %finish.1 = (f32[128,512]{1,0:T(8,128)}, f32[1,16,512]{2,1,0:T(8,128)}, f32[128,512]{1,0:T(8,128)}, f32[32,512]{1,0:T(8,128)}) custom-call(f32[16,128]{1,0:T(8,128)S(1)} %add.27.sums, f32[2,304,512]{2,1,0:T(8,128)S(1)} %turn_owned.1.turned), custom_call_target="tpu_custom_call" | custom-call | flops 1000000000 | bytes 3000000 | tf_op jit(solution)/shard_map/finish/pallas_call | solution.py:781
  (13 shorter events, 0.9 us)
Async XLA Ops:
  43.2 13.9 %all-to-all-start.1 = ((f32[8,88,128]{2,1,0:T(8,128)}), f32[8,88,128]{2,1,0:T(8,128)S(1)}, u32[]{:S(2)}, u32[]{:S(2)}) async-start(f32[8,88,128]{2,1,0:T(8,128)} %bitcast.2), calls=%async_computation.1 | async-start | bytes 720896 | tf_op jit(solution)/shard_map/all_to_all | solution.py:645
  57.9 12.0 %all-to-all-start.2 = ((f32[8,88,128]{2,1,0:T(8,128)}), f32[8,88,128]{2,1,0:T(8,128)S(1)}, u32[]{:S(2)}, u32[]{:S(2)}) async-start(f32[8,88,128]{2,1,0:T(8,128)} %bitcast.6), calls=%async_computation.2 | async-start | bytes 720896 | tf_op jit(solution)/shard_map/all_to_all | solution.py:645
  74.6 12.0 %all-to-all-start.3 = ((f32[8,88,128]{2,1,0:T(8,128)}), f32[8,88,128]{2,1,0:T(8,128)S(1)}, u32[]{:S(2)}, u32[]{:S(2)}) async-start(f32[8,88,128]{2,1,0:T(8,128)} %bitcast.8), calls=%async_computation.3 | async-start | bytes 720896 | tf_op jit(solution)/shard_map/all_to_all | solution.py:645
  98.6 33.8 %all-to-all-start.5 = ((f32[16,160,128]{2,1,0:T(8,128)}), f32[16,160,128]{2,1,0:T(8,128)S(1)}, u32[]{:S(2)}, u32[]{:S(2)}) async-start(f32[16,160,128]{2,1,0:T(8,128)} %pack_owned.3), calls=%async_computation.5 | async-start | bytes 2621440 | tf_op jit(solution)/shard_map/all_to_all | solution.py:645
  105.5 1.2 collective-permute-start
  106.7 3.5 %collective-permute-start.1 = (f32[1,128]{1,0:T(1,128)S(1)}, f32[1,128]{1,0:T(1,128)S(1)}, u32[]{:S(2)}, u32[]{:S(2)}) collective-permute-start(f32[1,128]{1,0:T(1,128)S(1)} %add.21), channel_id=1, source_target_pairs={{0,2},{1,3},{2,0},{3,1},{4,6},{5,7},{6,4},{7,5},{8,10},{9,11},{10,... | collective-permute-start | bytes 1544 | tf_op jit(solution)/shard_map/ppermute | solution.py:705
  110.3 4.8 %collective-permute-start.2 = (f32[1,128]{1,0:T(1,128)S(1)}, f32[1,128]{1,0:T(1,128)S(1)}, u32[]{:S(2)}, u32[]{:S(2)}) collective-permute-start(f32[1,128]{1,0:T(1,128)S(1)} %add.22), channel_id=1, source_target_pairs={{0,6},{1,7},{2,4},{3,5},{4,2},{5,3},{6,0},{7,1},{8,14},{9,15},{10,... | collective-permute-start | bytes 1544 | tf_op jit(solution)/shard_map/ppermute | solution.py:705
  115.1 3.8 %collective-permute-start.3 = (f32[16,128]{1,0:T(8,128)S(1)}, f32[16,128]{1,0:T(8,128)S(1)}, u32[]{:S(2)}, u32[]{:S(2)}) collective-permute-start(f32[16,128]{1,0:T(8,128)S(1)} %broadcast_select_fusion), channel_id=1, source_target_pairs={{0,8},{8,0},{16,24},{24,16},{32,40},{40,32},{48,56},{56,48},{64,72... | collective-permute-start | bytes 24584 | tf_op jit(solution)/shard_map/ppermute | solution.py:705
  119.0 4.9 %collective-permute-start.4 = (f32[16,128]{1,0:T(8,128)S(1)}, f32[16,128]{1,0:T(8,128)S(1)}, u32[]{:S(2)}, u32[]{:S(2)}) collective-permute-start(f32[16,128]{1,0:T(8,128)S(1)} %fusion), channel_id=1, source_target_pairs={{0,24},{8,16},{16,8},{24,0},{32,56},{40,48},{48,40},{56,32},{64,88... | collective-permute-start | bytes 24584 | tf_op jit(solution)/shard_map/ppermute | solution.py:705
  123.9 3.7 %collective-permute-start.5 = (f32[16,128]{1,0:T(8,128)S(1)}, f32[16,128]{1,0:T(8,128)S(1)}, u32[]{:S(2)}, u32[]{:S(2)}) collective-permute-start(f32[16,128]{1,0:T(8,128)S(1)} %fusion.1), channel_id=1, source_target_pairs={{0,32},{8,40},{16,48},{24,56},{32,0},{40,8},{48,16},{56,24},{64,96... | collective-permute-start | bytes 24584 | tf_op jit(solution)/shard_map/ppermute | solution.py:705
  127.6 4.9 %collective-permute-start.6 = (f32[16,128]{1,0:T(8,128)S(1)}, f32[16,128]{1,0:T(8,128)S(1)}, u32[]{:S(2)}, u32[]{:S(2)}) collective-permute-start(f32[16,128]{1,0:T(8,128)S(1)} %add.26), channel_id=1, source_target_pairs={{0,96},{8,104},{16,112},{24,120},{32,64},{40,72},{48,80},{56,88},{... | collective-permute-start | bytes 24584 | tf_op jit(solution)/shard_map/ppermute | solution.py:705

commit v7 on v3

--- a/solution.py
+++ b/solution.py
@@ -38,6 +38,7 @@
 COUNT_STEPS = HALF // 2
 CHUNKS = 4
 CHUNK_ROWS = N_SHOT * SRC_G // CHUNKS
+PARTS = N_SHOT // CHUNKS
 TRACE_TILES = TR_DEV // LANES
 BINS_AT = TRACE_TILES * SLICE
 INDEX_AT = BINS_AT + N_SHOT
@@ -306,9 +307,8 @@
 
 
 def count_kernel(
-    index, kept, to_cmp_kept, to_rcv_kept, most, diag, *refs, first
+    index, kept, to_cmp_kept, to_rcv_kept, most, diag, hot_even, hot_odd, ids, to_cmp, to_rcv, *, first
 ):
-    *handed, hot_even, hot_odd, ids, to_cmp, to_rcv = refs
     step = pl.program_id(0)
     even = first + 2 * step
 
@@ -326,9 +326,7 @@
         to_cmp[...] += cmp_counts
         to_rcv[...] += rcv_counts
         diag[...] += jnp.sum(rows, axis=0, keepdims=True)
-        part = kept_part(rows)
-        for out in [kept] + handed:
-            out[place * SRC_G : (place + 1) * SRC_G] = part
+        kept[place * SRC_G : (place + 1) * SRC_G] = kept_part(rows)
         most[...] = jnp.maximum(most[...], peak(rows))
 
     fill_hot(index[even + 1], ids, hot_odd)
@@ -367,17 +365,26 @@
 def fetch_counts(refs, held, held_cmp, held_rcv, sems):
     *halves, cmp_1, cmp_2, rcv_1, rcv_2 = refs
     pieces = []
-    for half, source in enumerate(halves):
-        for chunk in range(CHUNKS // 2):
-            start = chunk * CHUNK_ROWS
-            place = held.at[half * (CHUNKS // 2) + chunk]
-            pieces.append((source.at[start : start + CHUNK_ROWS], place))
+    for block in range(N_SHOT):
+        start = block % HALF * SRC_G
+        place = block % PARTS * SRC_G
+        target = held.at[block // PARTS, place : place + SRC_G]
+        pieces.append((halves[block // HALF].at[start : start + SRC_G], target))
     pieces += [(cmp_1, held_cmp.at[0]), (cmp_2, held_cmp.at[1])]
     pieces += [(rcv_1, held_rcv.at[0]), (rcv_2, held_rcv.at[1])]
     copies = [pltpu.make_async_copy(a, b, sems.at[k]) for k, (a, b) in enumerate(pieces)]
-    for copy in copies:
+    for copy in copies[: 2 * PARTS]:
         copy.start()
     return copies
+
+
+def next_chunk(copies, chunk):
+    for copy in copies[chunk * PARTS : (chunk + 1) * PARTS]:
+        copy.wait()
+    if chunk + 2 < CHUNKS:
+        last = len(copies) if chunk + 3 == CHUNKS else (chunk + 3) * PARTS
+        for copy in copies[(chunk + 2) * PARTS : last]:
+            copy.start()
 
 
 def sum_halves(held):
@@ -396,23 +403,21 @@
 
 
 def normal_kernel(
-    first, cmp_1, cmp_2, rcv_1, rcv_2, tab_in, rcv_in, last, diag_1, diag_2, most_1, most_2, index,
+    first, last, cmp_1, cmp_2, rcv_1, rcv_2, tab_in, rcv_in, diag_1, diag_2, most_1, most_2, index,
     tab, rcv, own_count, own, shared, to_shared, to_own,
     held, held_cmp, held_rcv, sems, hot, ids, exact_cmp, exact_rcv,
 ):
-    counts = (first, cmp_1, cmp_2, rcv_1, rcv_2)
+    counts = (first, last, cmp_1, cmp_2, rcv_1, rcv_2)
     copies = fetch_counts(counts, held, held_cmp, held_rcv, sems)
     top = 2 * SLICE
-    half = HALF * SRC_G
     load_halves(tab_in, rcv_in, own, shared)
     lanes = lax.broadcasted_iota(jnp.int32, (16, SHARED), 1)
     shared[top:] = jnp.where(lanes < LANES, 1.0, 0.0).astype(BF16)
-    to_shared[...] = jnp.dot(own[:, half:], last[...], preferred_element_type=F32)
-    to_own[:, half:] = nt_dot(shared[...], last[...])
-    for chunk in range(CHUNKS // 2):
-        copies[chunk].wait()
+    for chunk in range(CHUNKS):
+        next_chunk(copies, chunk)
         span = slice(chunk * CHUNK_ROWS, (chunk + 1) * CHUNK_ROWS)
-        to_shared[...] += jnp.dot(own[:, span], held[chunk], preferred_element_type=F32)
+        sums = jnp.dot(own[:, span], held[chunk], preferred_element_type=F32)
+        to_shared[...] = sums if chunk == 0 else to_shared[...] + sums
         to_own[:, span] = nt_dot(shared[...], held[chunk])
 
     def others(to_cmp, to_rcv):
@@ -478,7 +483,7 @@
     rcv_z[...] = own_z
     load_halves(tab_z, rcv_z, own, shared)
     for chunk in range(CHUNKS):
-        copies[chunk].wait()
+        next_chunk(copies, chunk)
         span = slice(chunk * CHUNK_ROWS, (chunk + 1) * CHUNK_ROWS)
         sums = jnp.dot(own[:, span], held[chunk], preferred_element_type=F32)
         to_shared[...] = sums if chunk == 0 else to_shared[...] + sums
@@ -559,20 +564,18 @@
 def count_call(index, first):
     rows = pl.BlockSpec((2 * SRC_G, SHARED), lambda c: (c, 0))
     small = [whole_spec(*TO_CMP), whole_spec(*TO_RCV), whole_spec(1, LANES), whole_spec(1, SHARED)]
-    handed = [] if first == 0 else [jax.ShapeDtypeStruct(COUNTS, BF16)]
     return pl.pallas_call(
         functools.partial(count_kernel, first=first),
         grid=(COUNT_STEPS,),
         in_specs=[whole_spec(*INDEX)],
-        out_specs=[rows] + small + [rows] * len(handed),
+        out_specs=[rows] + small,
         out_shape=[
             pltpu.HBM(COUNTS, BF16),
             pltpu.HBM(TO_CMP, jnp.int8),
             pltpu.HBM(TO_RCV, jnp.int8),
             jax.ShapeDtypeStruct((1, LANES), F32),
             jax.ShapeDtypeStruct((1, SHARED), F32),
-        ]
-        + handed,
+        ],
         scratch_shapes=[VMEM((ROWS, TR_DEV), FP8)] * 2
         + [VMEM((256, LANES), BF16), VMEM(TO_CMP, F32), VMEM(TO_RCV, F32)],
         compiler_params=params(24),
@@ -587,7 +590,7 @@
             VMEM((chunks, CHUNK_ROWS, SHARED), BF16),
             VMEM((2,) + TO_CMP, jnp.int8),
             VMEM((2,) + TO_RCV, jnp.int8),
-            pltpu.SemaphoreType.DMA((chunks + 4,)),
+            pltpu.SemaphoreType.DMA((N_SHOT + 4,)),
         ]
         + hot_scratch()
         + [VMEM(TO_CMP, F32), VMEM(TO_RCV, F32)]
@@ -601,11 +604,10 @@
 
 
 def normal_apply(tab, rcv, index, counts):
-    (first, _, *rest), small = count_operands(counts)
-    last = counts[1][5]
+    big, small = count_operands(counts)
     return pl.pallas_call(
         normal_kernel,
-        in_specs=[ANYWHERE] * 5 + [IN_VMEM] * 8,
+        in_specs=[ANYWHERE] * 6 + [IN_VMEM] * 7,
         out_shape=table_shapes() + [jax.ShapeDtypeStruct((N_SHOT, LANES), F32)],
         scratch_shapes=[
             VMEM((2 * SLICE, N_SHOT * SRC_G), BF16),
@@ -613,11 +615,11 @@
             VMEM((2 * SLICE, SHARED), F32),
             VMEM((2 * SLICE + 16, N_SHOT * SRC_G), F32),
         ]
-        + count_scratch(CHUNKS // 2),
+        + count_scratch(CHUNKS),
         compiler_params=params(24),
         cost_estimate=cost(3),
         name="normal_apply",
-    )(first, *rest, tab, rcv, last, *small, index)
+    )(*big, tab, rcv, *small, index)
 
 
 def norm_sums(tab_b, rcv_b, tab_y, rcv_y, own_count, index, counts):

time: 136 us -> 136 us (level)
  local copies, waits for them, and re-layouts: 2.76 us -> 0 us
  Pallas kernels: 34.2 us -> 36.1 us
    unnamed x4 -> x0, local copies, waits for them, and re-layouts: 2.76 us -> none
where the time goes in v7:
time: 136 us; the launch traced here: 135 us
  blocking collectives  41.4 us (30%)
  Pallas kernels  36.1 us (27%)
  waiting for transfers between devices  29.7 us (22%)
  starting transfers between devices  27 us (20%)
    all_to_all x2, blocking collectives, exchange(): return lax.all_to_all(array, axis, split_axis=0, concat_axis=0, tiled=True)  41.4 us
    all_to_all x4, starting transfers between devices, exchange(): return lax.all_to_all(array, axis, split_axis=0, concat_axis=0, tiled=True)  16.1 us
    ppermute x7, waiting for transfers between devices, swapped(): return lax.ppermute(value, axis, [(s, s ^ bit) for s in range(size)])  15.7 us
    all_to_all x4, waiting for transfers between devices, exchange(): return lax.all_to_all(array, axis, split_axis=0, concat_axis=0, tiled=True)  14.1 us
    ppermute x7, starting transfers between devices, swapped(): return lax.ppermute(value, axis, [(s, s ^ bit) for s in range(size)])  10.9 us
    pallas_call x2, Pallas kernels, count_call(): pl.pallas_call(functools.partial(count_kernel, first=first), grid=(COUNT_...  10.5 us
    pallas_call x1, Pallas kernels, adjoint_apply(): pl.pallas_call(adjoint_kernel, out_shape=table_shapes() + [jax.ShapeDtype...  7.45 us
    pallas_call x1, Pallas kernels, normal_apply(): pl.pallas_call(normal_kernel, in_specs=[ANYWHERE] * 6 + [IN_VMEM] * 7, ou...  5.05 us
  transfers between devices with their start and end apart: 11, of which 10 were waited for; matrix products, arithmetic and copies ran while one was open for 0% of the time, Pallas kernels for 11%

profile of v7, /device:TPU:0, one launch (start us, length us, event | category | flops | bytes accessed | tf_op | source)
XLA Modules:
  0.0 135.2 jit_solution(4134329487005319937)
XLA Ops:
  0.6 4.7 %spectra.1 = f32[16,200,128]{2,1,0:T(8,128)S(1)} custom-call(bf16[640,1024]{1,0:T(8,128)(2,1)} %traces.1, bf16[1024,1024]{1,0:T(8,128)(2,1)} %constant.10.clone.waves, s32[16,80]{1,0:T(8,128)} %bitcast.19, s32[1,16]{1,0:T(1,128)} %refs_1_.1, s32[16,80]{1,0:T(8,128)} %bitcast.20, s32[640]{0:T(1024)} %refs_3_.1, s32[640]{0:T(1024)} %refs_4_.1, s32[640]{0:T(1024)} %refs_5_.1), custom_call_target="tpu_custom_call" | custom-call | flops 5000000000 | bytes 15000000 | tf_op jit(solution)/shard_map/spectra/pallas_call | solution.py:173
  5.4 30.4 %all_to_all.53.data = f32[16,200,128]{2,1,0:T(8,128)S(1)} all-to-all(f32[16,200,128]{2,1,0:T(8,128)S(1)} %spectra.1), channel_id=1, replica_groups=mesh['shot'=16,'rcv'=8] {'shot'}, dimensions={0} | all-to-all | bytes 3276800 | tf_op jit(solution)/shard_map/all_to_all | solution.py:654
  35.8 7.4 %adjoint_apply.1 = (f32[704,128]{1,0:T(8,128)}, f32[2,32,128]{2,1,0:T(8,128)S(1)}, s32[16,24,128]{2,1,0:T(8,128)S(1)}) custom-call(f32[16,200,128]{2,1,0:T(8,128)S(1)} %all_to_all.53.data), custom_call_target="tpu_custom_call" | custom-call | flops 8000000000 | bytes 24000000 | tf_op jit(solution)/shard_map/adjoint_apply/pallas_call | solution.py:548
  43.2 5.3 %all-to-all-start.1 = ((f32[8,88,128]{2,1,0:T(8,128)}), f32[8,88,128]{2,1,0:T(8,128)S(1)}, u32[]{:S(2)}, u32[]{:S(2)}) async-start(f32[8,88,128]{2,1,0:T(8,128)} %bitcast.2), calls=%async_computation.1 | async-start | bytes 720896 | tf_op jit(solution)/shard_map/all_to_all | solution.py:654
  48.5 5.2 %count_pairs.2 = (bf16[1024,896]{1,0:T(8,128)(2,1)}, s8[384,512]{1,0:T(32,128)(4,1)}, s8[128,256]{1,0:T(32,128)(4,1)}, f32[1,128]{1,0:T(1,128)S(1)}, f32[1,896]{1,0:T(1,128)S(1)}) custom-call(s32[16,24,128]{2,1,0:T(8,128)S(1)} %get-tuple-element.43.index), custom_call_target="tpu_custom_call" | custom-call | flops 6000000000 | bytes 18000000 | tf_op jit(solution)/shard_map/count_pairs/pallas_call | solution.py:567
  53.8 3.4 %all-to-all-done.1 = f32[8,88,128]{2,1,0:T(8,128)S(1)} async-done(((f32[8,88,128]{2,1,0:T(8,128)}), f32[8,88,128]{2,1,0:T(8,128)S(1)}, u32[]{:S(2)}, u32[]{:S(2)}) %all-to-all-start.1) | async-done | bytes 360480 | tf_op jit(solution)/shard_map/all_to_all | solution.py:654
  57.1 0.8 sum_shares.2
  57.9 3.4 %all-to-all-start.2 = ((f32[8,88,128]{2,1,0:T(8,128)}), f32[8,88,128]{2,1,0:T(8,128)S(1)}, u32[]{:S(2)}, u32[]{:S(2)}) async-start(f32[8,88,128]{2,1,0:T(8,128)} %bitcast.6), calls=%async_computation.2 | async-start | bytes 720896 | tf_op jit(solution)/shard_map/all_to_all | solution.py:654
  61.3 5.2 %count_pairs.3 = (bf16[1024,896]{1,0:T(8,128)(2,1)}, s8[384,512]{1,0:T(32,128)(4,1)}, s8[128,256]{1,0:T(32,128)(4,1)}, f32[1,128]{1,0:T(1,128)S(1)}, f32[1,896]{1,0:T(1,128)S(1)}) custom-call(s32[16,24,128]{2,1,0:T(8,128)S(1)} %get-tuple-element.43.index), custom_call_target="tpu_custom_call" | custom-call | flops 6000000000 | bytes 18000000 | tf_op jit(solution)/shard_map/count_pairs/pallas_call | solution.py:567
  66.6 3.3 %all-to-all-done.2 = f32[8,88,128]{2,1,0:T(8,128)S(1)} async-done(((f32[8,88,128]{2,1,0:T(8,128)}), f32[8,88,128]{2,1,0:T(8,128)S(1)}, u32[]{:S(2)}, u32[]{:S(2)}) %all-to-all-start.2) | async-done | bytes 360480 | tf_op jit(solution)/shard_map/all_to_all | solution.py:654
  69.9 5.0 %normal_apply.1 = (f32[704,128]{1,0:T(8,128)}, f32[2,32,128]{2,1,0:T(8,128)S(1)}, f32[16,128]{1,0:T(8,128)S(1)}) custom-call(bf16[1024,896]{1,0:T(8,128)(2,1)} %get-tuple-element.40.first, bf16[1024,896]{1,0:T(8,128)(2,1)} %get-tuple-element.44.last, s8[384,512]{1,0:T(32,128)(4,1)} %get-tuple-element.45.cmp_1, s8[384,512]{1,0:T(32,128)(4,1)} %get-tuple-element.46.cmp_2, ...), custom_call_target="tpu_custom_call" | custom-call | flops 3000000000 | bytes 9000000 | tf_op jit(solution)/shard_map/normal_apply/pallas_call | solution.py:608
  74.9 3.5 %all-to-all-start.3 = ((f32[8,88,128]{2,1,0:T(8,128)}), f32[8,88,128]{2,1,0:T(8,128)S(1)}, u32[]{:S(2)}, u32[]{:S(2)}) async-start(f32[8,88,128]{2,1,0:T(8,128)} %bitcast.8), calls=%async_computation.3 | async-start | bytes 720896 | tf_op jit(solution)/shard_map/all_to_all | solution.py:654
  78.4 1.1 pack_owned.2.refs_0_
  79.4 7.4 %all-to-all-done.3 = f32[8,88,128]{2,1,0:T(8,128)S(1)} async-done(((f32[8,88,128]{2,1,0:T(8,128)}), f32[8,88,128]{2,1,0:T(8,128)S(1)}, u32[]{:S(2)}, u32[]{:S(2)}) %all-to-all-start.3) | async-done | bytes 360480 | tf_op jit(solution)/shard_map/all_to_all | solution.py:654
  86.9 11.0 %all_to_all.54 = f32[8,88,128]{2,1,0:T(8,128)S(1)} all-to-all(f32[8,88,128]{2,1,0:T(8,128)S(1)} %sum_shares.3), channel_id=1, replica_groups=mesh['shot'=16,'rcv'=8] {'rcv'}, dimensions={0} | all-to-all | bytes 720896 | tf_op jit(solution)/shard_map/all_to_all | solution.py:654
  97.9 1.1 pack_owned.3
  99.0 3.9 %all-to-all-start.5 = ((f32[16,160,128]{2,1,0:T(8,128)}), f32[16,160,128]{2,1,0:T(8,128)S(1)}, u32[]{:S(2)}, u32[]{:S(2)}) async-start(f32[16,160,128]{2,1,0:T(8,128)} %pack_owned.3), calls=%async_computation.5 | async-start | bytes 2621440 | tf_op jit(solution)/shard_map/all_to_all | solution.py:654
  102.9 3.8 %norm_sums.1 = f32[1,128]{1,0:T(1,128)S(1)} custom-call(bf16[1024,896]{1,0:T(8,128)(2,1)} %get-tuple-element.40.first, bf16[1024,896]{1,0:T(8,128)(2,1)} %get-tuple-element.44.last, s8[384,512]{1,0:T(32,128)(4,1)} %get-tuple-element.45.cmp_1, s8[384,512]{1,0:T(32,128)(4,1)} %get-tuple-element.46.cmp_2, s8[128,256]{1,0:T(32,128)(4,1)} %get-tuple-element.47.rcv_1, ...), custom_call_target="tpu_custom_call" | custom-call | flops 2000000000 | bytes 6000000 | tf_op jit(solution)/shard_map/norm_sums/pallas_call | solution.py:627
  106.8 1.1 collective-permute-done
  107.9 0.6 collective-permute-start.1
  108.5 3.0 %collective-permute-done.1 = f32[1,128]{1,0:T(1,128)S(1)} collective-permute-done((f32[1,128]{1,0:T(1,128)S(1)}, f32[1,128]{1,0:T(1,128)S(1)}, u32[]{:S(2)}, u32[]{:S(2)}) %collective-permute-start.1) | collective-permute-done | bytes 544 | tf_op jit(solution)/shard_map/ppermute | solution.py:714
  111.4 1.2 collective-permute-start.2
  112.6 3.6 %collective-permute-done.2 = f32[1,128]{1,0:T(1,128)S(1)} collective-permute-done((f32[1,128]{1,0:T(1,128)S(1)}, f32[1,128]{1,0:T(1,128)S(1)}, u32[]{:S(2)}, u32[]{:S(2)}) %collective-permute-start.2) | collective-permute-done | bytes 544 | tf_op jit(solution)/shard_map/ppermute | solution.py:714
  116.3 1.6 %collective-permute-start.3 = (f32[16,128]{1,0:T(8,128)S(1)}, f32[16,128]{1,0:T(8,128)S(1)}, u32[]{:S(2)}, u32[]{:S(2)}) collective-permute-start(f32[16,128]{1,0:T(8,128)S(1)} %broadcast_select_fusion), channel_id=1, source_target_pairs={{0,8},{8,0},{16,24},{24,16},{32,40},{40,32},{48,56},{56,48},{64,72... | collective-permute-start | bytes 24584 | tf_op jit(solution)/shard_map/ppermute | solution.py:714
  117.9 2.0 %collective-permute-done.3 = f32[16,128]{1,0:T(8,128)S(1)} collective-permute-done((f32[16,128]{1,0:T(8,128)S(1)}, f32[16,128]{1,0:T(8,128)S(1)}, u32[]{:S(2)}, u32[]{:S(2)}) %collective-permute-start.3) | collective-permute-done | bytes 8224 | tf_op jit(solution)/shard_map/ppermute | solution.py:714
  120.0 2.9 %collective-permute-start.4 = (f32[16,128]{1,0:T(8,128)S(1)}, f32[16,128]{1,0:T(8,128)S(1)}, u32[]{:S(2)}, u32[]{:S(2)}) collective-permute-start(f32[16,128]{1,0:T(8,128)S(1)} %fusion), channel_id=1, source_target_pairs={{0,24},{8,16},{16,8},{24,0},{32,56},{40,48},{48,40},{56,32},{64,88... | collective-permute-start | bytes 24584 | tf_op jit(solution)/shard_map/ppermute | solution.py:714
  122.9 2.0 %collective-permute-done.4 = f32[16,128]{1,0:T(8,128)S(1)} collective-permute-done((f32[16,128]{1,0:T(8,128)S(1)}, f32[16,128]{1,0:T(8,128)S(1)}, u32[]{:S(2)}, u32[]{:S(2)}) %collective-permute-start.4) | collective-permute-done | bytes 8224 | tf_op jit(solution)/shard_map/ppermute | solution.py:714
  124.9 1.7 %collective-permute-start.5 = (f32[16,128]{1,0:T(8,128)S(1)}, f32[16,128]{1,0:T(8,128)S(1)}, u32[]{:S(2)}, u32[]{:S(2)}) collective-permute-start(f32[16,128]{1,0:T(8,128)S(1)} %fusion.1), channel_id=1, source_target_pairs={{0,32},{8,40},{16,48},{24,56},{32,0},{40,8},{48,16},{56,24},{64,96... | collective-permute-start | bytes 24584 | tf_op jit(solution)/shard_map/ppermute | solution.py:714
  126.6 2.0 %collective-permute-done.5 = f32[16,128]{1,0:T(8,128)S(1)} collective-permute-done((f32[16,128]{1,0:T(8,128)S(1)}, f32[16,128]{1,0:T(8,128)S(1)}, u32[]{:S(2)}, u32[]{:S(2)}) %collective-permute-start.5) | collective-permute-done | bytes 8224 | tf_op jit(solution)/shard_map/ppermute | solution.py:714
  128.6 2.9 %collective-permute-start.6 = (f32[16,128]{1,0:T(8,128)S(1)}, f32[16,128]{1,0:T(8,128)S(1)}, u32[]{:S(2)}, u32[]{:S(2)}) collective-permute-start(f32[16,128]{1,0:T(8,128)S(1)} %add.26), channel_id=1, source_target_pairs={{0,96},{8,104},{16,112},{24,120},{32,64},{40,72},{48,80},{56,88},{... | collective-permute-start | bytes 24584 | tf_op jit(solution)/shard_map/ppermute | solution.py:714
  131.5 2.0 %collective-permute-done.6 = f32[16,128]{1,0:T(8,128)S(1)} collective-permute-done((f32[16,128]{1,0:T(8,128)S(1)}, f32[16,128]{1,0:T(8,128)S(1)}, u32[]{:S(2)}, u32[]{:S(2)}) %collective-permute-start.6) | collective-permute-done | bytes 8224 | tf_op jit(solution)/shard_map/ppermute | solution.py:714
  133.5 1.7 %finish.1 = (f32[128,512]{1,0:T(8,128)}, f32[1,16,512]{2,1,0:T(8,128)}, f32[128,512]{1,0:T(8,128)}, f32[32,512]{1,0:T(8,128)}) custom-call(f32[16,128]{1,0:T(8,128)S(1)} %add.27.sums, f32[16,160,128]{2,1,0:T(8,128)S(1)} %all-to-all-done.5.owned), custom_call_target="tpu_custom_call" | custom-call | tf_op jit(solution)/shard_map/finish/pallas_call | solution.py:772
  (12 shorter events, 0.4 us)
Async XLA Ops:
  43.2 13.9 %all-to-all-start.1 = ((f32[8,88,128]{2,1,0:T(8,128)}), f32[8,88,128]{2,1,0:T(8,128)S(1)}, u32[]{:S(2)}, u32[]{:S(2)}) async-start(f32[8,88,128]{2,1,0:T(8,128)} %bitcast.2), calls=%async_computation.1 | async-start | bytes 720896 | tf_op jit(solution)/shard_map/all_to_all | solution.py:654
  57.9 12.0 %all-to-all-start.2 = ((f32[8,88,128]{2,1,0:T(8,128)}), f32[8,88,128]{2,1,0:T(8,128)S(1)}, u32[]{:S(2)}, u32[]{:S(2)}) async-start(f32[8,88,128]{2,1,0:T(8,128)} %bitcast.6), calls=%async_computation.2 | async-start | bytes 720896 | tf_op jit(solution)/shard_map/all_to_all | solution.py:654
  74.9 12.0 %all-to-all-start.3 = ((f32[8,88,128]{2,1,0:T(8,128)}), f32[8,88,128]{2,1,0:T(8,128)S(1)}, u32[]{:S(2)}, u32[]{:S(2)}) async-start(f32[8,88,128]{2,1,0:T(8,128)} %bitcast.8), calls=%async_computation.3 | async-start | bytes 720896 | tf_op jit(solution)/shard_map/all_to_all | solution.py:654
  99.0 34.5 %all-to-all-start.5 = ((f32[16,160,128]{2,1,0:T(8,128)}), f32[16,160,128]{2,1,0:T(8,128)S(1)}, u32[]{:S(2)}, u32[]{:S(2)}) async-start(f32[16,160,128]{2,1,0:T(8,128)} %pack_owned.3), calls=%async_computation.5 | async-start | bytes 2621440 | tf_op jit(solution)/shard_map/all_to_all | solution.py:654
  106.7 1.2 collective-permute-start
  107.9 3.5 %collective-permute-start.1 = (f32[1,128]{1,0:T(1,128)S(1)}, f32[1,128]{1,0:T(1,128)S(1)}, u32[]{:S(2)}, u32[]{:S(2)}) collective-permute-start(f32[1,128]{1,0:T(1,128)S(1)} %add.21), channel_id=1, source_target_pairs={{0,2},{1,3},{2,0},{3,1},{4,6},{5,7},{6,4},{7,5},{8,10},{9,11},{10,... | collective-permute-start | bytes 1544 | tf_op jit(solution)/shard_map/ppermute | solution.py:714
  111.4 4.8 %collective-permute-start.2 = (f32[1,128]{1,0:T(1,128)S(1)}, f32[1,128]{1,0:T(1,128)S(1)}, u32[]{:S(2)}, u32[]{:S(2)}) collective-permute-start(f32[1,128]{1,0:T(1,128)S(1)} %add.22), channel_id=1, source_target_pairs={{0,6},{1,7},{2,4},{3,5},{4,2},{5,3},{6,0},{7,1},{8,14},{9,15},{10,... | collective-permute-start | bytes 1544 | tf_op jit(solution)/shard_map/ppermute | solution.py:714
  116.3 3.7 %collective-permute-start.3 = (f32[16,128]{1,0:T(8,128)S(1)}, f32[16,128]{1,0:T(8,128)S(1)}, u32[]{:S(2)}, u32[]{:S(2)}) collective-permute-start(f32[16,128]{1,0:T(8,128)S(1)} %broadcast_select_fusion), channel_id=1, source_target_pairs={{0,8},{8,0},{16,24},{24,16},{32,40},{40,32},{48,56},{56,48},{64,72... | collective-permute-start | bytes 24584 | tf_op jit(solution)/shard_map/ppermute | solution.py:714
  120.0 4.9 %collective-permute-start.4 = (f32[16,128]{1,0:T(8,128)S(1)}, f32[16,128]{1,0:T(8,128)S(1)}, u32[]{:S(2)}, u32[]{:S(2)}) collective-permute-start(f32[16,128]{1,0:T(8,128)S(1)} %fusion), channel_id=1, source_target_pairs={{0,24},{8,16},{16,8},{24,0},{32,56},{40,48},{48,40},{56,32},{64,88... | collective-permute-start | bytes 24584 | tf_op jit(solution)/shard_map/ppermute | solution.py:714
  124.9 3.7 %collective-permute-start.5 = (f32[16,128]{1,0:T(8,128)S(1)}, f32[16,128]{1,0:T(8,128)S(1)}, u32[]{:S(2)}, u32[]{:S(2)}) collective-permute-start(f32[16,128]{1,0:T(8,128)S(1)} %fusion.1), channel_id=1, source_target_pairs={{0,32},{8,40},{16,48},{24,56},{32,0},{40,8},{48,16},{56,24},{64,96... | collective-permute-start | bytes 24584 | tf_op jit(solution)/shard_map/ppermute | solution.py:714
  128.6 4.9 %collective-permute-start.6 = (f32[16,128]{1,0:T(8,128)S(1)}, f32[16,128]{1,0:T(8,128)S(1)}, u32[]{:S(2)}, u32[]{:S(2)}) collective-permute-start(f32[16,128]{1,0:T(8,128)S(1)} %add.26), channel_id=1, source_target_pairs={{0,96},{8,104},{16,112},{24,120},{32,64},{40,72},{48,80},{56,88},{... | collective-permute-start | bytes 24584 | tf_op jit(solution)/shard_map/ppermute | solution.py:714

commit v8 on v7

--- a/solution.py
+++ b/solution.py
@@ -38,7 +38,6 @@
 COUNT_STEPS = HALF // 2
 CHUNKS = 4
 CHUNK_ROWS = N_SHOT * SRC_G // CHUNKS
-PARTS = N_SHOT // CHUNKS
 TRACE_TILES = TR_DEV // LANES
 BINS_AT = TRACE_TILES * SLICE
 INDEX_AT = BINS_AT + N_SHOT
@@ -365,26 +364,17 @@
 def fetch_counts(refs, held, held_cmp, held_rcv, sems):
     *halves, cmp_1, cmp_2, rcv_1, rcv_2 = refs
     pieces = []
-    for block in range(N_SHOT):
-        start = block % HALF * SRC_G
-        place = block % PARTS * SRC_G
-        target = held.at[block // PARTS, place : place + SRC_G]
-        pieces.append((halves[block // HALF].at[start : start + SRC_G], target))
+    for half, source in enumerate(halves):
+        for chunk in range(CHUNKS // 2):
+            start = chunk * CHUNK_ROWS
+            place = held.at[half * (CHUNKS // 2) + chunk]
+            pieces.append((source.at[start : start + CHUNK_ROWS], place))
     pieces += [(cmp_1, held_cmp.at[0]), (cmp_2, held_cmp.at[1])]
     pieces += [(rcv_1, held_rcv.at[0]), (rcv_2, held_rcv.at[1])]
     copies = [pltpu.make_async_copy(a, b, sems.at[k]) for k, (a, b) in enumerate(pieces)]
-    for copy in copies[: 2 * PARTS]:
+    for copy in copies:
         copy.start()
     return copies
-
-
-def next_chunk(copies, chunk):
-    for copy in copies[chunk * PARTS : (chunk + 1) * PARTS]:
-        copy.wait()
-    if chunk + 2 < CHUNKS:
-        last = len(copies) if chunk + 3 == CHUNKS else (chunk + 3) * PARTS
-        for copy in copies[(chunk + 2) * PARTS : last]:
-            copy.start()
 
 
 def sum_halves(held):
@@ -414,7 +404,7 @@
     lanes = lax.broadcasted_iota(jnp.int32, (16, SHARED), 1)
     shared[top:] = jnp.where(lanes < LANES, 1.0, 0.0).astype(BF16)
     for chunk in range(CHUNKS):
-        next_chunk(copies, chunk)
+        copies[chunk].wait()
         span = slice(chunk * CHUNK_ROWS, (chunk + 1) * CHUNK_ROWS)
         sums = jnp.dot(own[:, span], held[chunk], preferred_element_type=F32)
         to_shared[...] = sums if chunk == 0 else to_shared[...] + sums
@@ -483,7 +473,7 @@
     rcv_z[...] = own_z
     load_halves(tab_z, rcv_z, own, shared)
     for chunk in range(CHUNKS):
-        next_chunk(copies, chunk)
+        copies[chunk].wait()
         span = slice(chunk * CHUNK_ROWS, (chunk + 1) * CHUNK_ROWS)
         sums = jnp.dot(own[:, span], held[chunk], preferred_element_type=F32)
         to_shared[...] = sums if chunk == 0 else to_shared[...] + sums
@@ -590,7 +580,7 @@
             VMEM((chunks, CHUNK_ROWS, SHARED), BF16),
             VMEM((2,) + TO_CMP, jnp.int8),
             VMEM((2,) + TO_RCV, jnp.int8),
-            pltpu.SemaphoreType.DMA((N_SHOT + 4,)),
+            pltpu.SemaphoreType.DMA((chunks + 4,)),
         ]
         + hot_scratch()
         + [VMEM(TO_CMP, F32), VMEM(TO_RCV, F32)]
@@ -714,18 +704,14 @@
     return lax.ppermute(value, axis, [(s, s ^ bit) for s in range(size)])
 
 
-def gather_sums(sums):
+def sum_over_rcv(sums):
     for bit in (1, 2, 6):
         sums = sums + swapped(sums, "rcv", N_RCV, bit)
-    here = jnp.arange(N_SHOT, dtype=jnp.int32)[:, None] == lax.axis_index("shot")
-    rows = jnp.where(here, sums, 0.0)
-    for bit in (1, 3, 4, 12):
-        rows = rows + swapped(rows, "shot", N_SHOT, bit)
-    return rows
+    return sums
 
 
 def finish_kernel(sums, owned, source, receiver, offset, cmp):
-    rows = sums[...]
+    rows = sums[...].reshape(N_SHOT, LANES)
     norm_b, cross, norm_z, norm_az, shift = (rows[:, lane : lane + 1] for lane in range(5))
     shift = shift * (1.0 / N_RCV)
 
@@ -805,8 +791,10 @@
     packed = pack_owned(tab_y, rcv_y, packed)
     tab_y, packed = lax.optimization_barrier((tab_y, packed))
     owned = exchange(packed, "shot")
-    sums = norm_sums(tab_b, rcv_b, tab_y, rcv_y, own_count, index, counts)
-    return tuple(finish(gather_sums(sums), owned))
+    sums = sum_over_rcv(norm_sums(tab_b, rcv_b, tab_y, rcv_y, own_count, index, counts))
+    owned, sums = lax.optimization_barrier((owned, sums))
+    sums = exchange(jnp.broadcast_to(sums[None], (N_SHOT, 1, LANES)), "shot")
+    return tuple(finish(sums, owned))
 
 
 def solution(mesh):

time: 136 us -> 136 us (level)
  blocking collectives: 41.4 us -> 51.9 us
  starting transfers between devices: 27 us -> 17.9 us
    all_to_all x2 -> x3, blocking collectives: 41.4 us -> 51.9 us  [exchange(): return lax.all_to_all(array, axis, split_axis=0, concat_axis=0, tiled=True)]
    ppermute x7 -> x3, starting transfers between devices: 10.9 us -> 1.82 us  [swapped(): return lax.ppermute(value, axis, [(s, s ^ bit) for s in range(size)])]
    all_to_all x4, waiting for transfers between devices: 14.1 us -> 22.5 us  [exchange(): return lax.all_to_all(array, axis, split_axis=0, concat_axis=0, tiled=True)]
    ppermute x7 -> x3, waiting for transfers between devices: 15.7 us -> 7.66 us  [swapped(): return lax.ppermute(value, axis, [(s, s ^ bit) for s in range(size)])]
  transfers between devices with their start and end apart: 11 -> 7, of which waited for: 10 -> 7; matrix products, arithmetic and copies ran while one was open for 0% -> 0% of each run, Pallas kernels for 11% -> 11%
where the time goes in v8:
time: 136 us
  blocking collectives  51.9 us (38%)
  Pallas kernels  34.8 us (26%)
  waiting for transfers between devices  30.2 us (22%)
  starting transfers between devices  17.9 us (13%)
    all_to_all x3, blocking collectives, exchange(): return lax.all_to_all(array, axis, split_axis=0, concat_axis=0, tiled=True)  51.9 us
    all_to_all x4, waiting for transfers between devices, exchange(): return lax.all_to_all(array, axis, split_axis=0, concat_axis=0, tiled=True)  22.5 us
    all_to_all x4, starting transfers between devices, exchange(): return lax.all_to_all(array, axis, split_axis=0, concat_axis=0, tiled=True)  16.1 us
    pallas_call x2, Pallas kernels, count_call(): pl.pallas_call(functools.partial(count_kernel, first=first), grid=(COUNT_...  10.5 us
    ppermute x3, waiting for transfers between devices, swapped(): return lax.ppermute(value, axis, [(s, s ^ bit) for s in range(size)])  7.66 us
    pallas_call x1, Pallas kernels, adjoint_apply(): pl.pallas_call(adjoint_kernel, out_shape=table_shapes() + [jax.ShapeDtype...  7.48 us
    pallas_call x1, Pallas kernels, log_spectra(): pl.pallas_call(spectra_kernel, in_specs=[ANYWHERE] * (2 + len(small)), ou...  4.72 us
    pallas_call x1, Pallas kernels, normal_apply(): pl.pallas_call(normal_kernel, in_specs=[ANYWHERE] * 6 + [IN_VMEM] * 7, ou...  4.72 us
  transfers between devices with their start and end apart: 7, of which 7 were waited for; matrix products, arithmetic and copies ran while one was open for 0% of the time, Pallas kernels for 11%

profile of v8, /device:TPU:0, one launch (start us, length us, event | category | flops | bytes accessed | tf_op | source)
XLA Modules:
  0.0 135.5 jit_solution(11962126720207376018)
XLA Ops:
  0.6 4.7 %spectra.1 = f32[16,200,128]{2,1,0:T(8,128)S(1)} custom-call(bf16[640,1024]{1,0:T(8,128)(2,1)} %traces.1, bf16[1024,1024]{1,0:T(8,128)(2,1)} %constant.2.clone.waves, s32[16,80]{1,0:T(8,128)} %bitcast.19, s32[1,16]{1,0:T(1,128)} %refs_1_.1, s32[16,80]{1,0:T(8,128)} %bitcast.20, s32[640]{0:T(1024)} %refs_3_.1, s32[640]{0:T(1024)} %refs_4_.1, s32[640]{0:T(1024)} %refs_5_.1), custom_call_target="tpu_custom_call" | custom-call | flops 5000000000 | bytes 15000000 | tf_op jit(solution)/shard_map/spectra/pallas_call | solution.py:172
  5.4 30.4 %all_to_all.58.data = f32[16,200,128]{2,1,0:T(8,128)S(1)} all-to-all(f32[16,200,128]{2,1,0:T(8,128)S(1)} %spectra.1), channel_id=1, replica_groups=mesh['shot'=16,'rcv'=8] {'shot'}, dimensions={0} | all-to-all | bytes 3276800 | tf_op jit(solution)/shard_map/all_to_all | solution.py:644
  35.8 7.5 %adjoint_apply.1 = (f32[704,128]{1,0:T(8,128)}, f32[2,32,128]{2,1,0:T(8,128)S(1)}, s32[16,24,128]{2,1,0:T(8,128)S(1)}) custom-call(f32[16,200,128]{2,1,0:T(8,128)S(1)} %all_to_all.58.data), custom_call_target="tpu_custom_call" | custom-call | flops 8000000000 | bytes 24000000 | tf_op jit(solution)/shard_map/adjoint_apply/pallas_call | solution.py:538
  43.3 5.3 %all-to-all-start.1 = ((f32[8,88,128]{2,1,0:T(8,128)}), f32[8,88,128]{2,1,0:T(8,128)S(1)}, u32[]{:S(2)}, u32[]{:S(2)}) async-start(f32[8,88,128]{2,1,0:T(8,128)} %bitcast.2), calls=%async_computation.1 | async-start | bytes 720896 | tf_op jit(solution)/shard_map/all_to_all | solution.py:644
  48.6 5.2 %count_pairs.2 = (bf16[1024,896]{1,0:T(8,128)(2,1)}, s8[384,512]{1,0:T(32,128)(4,1)}, s8[128,256]{1,0:T(32,128)(4,1)}, f32[1,128]{1,0:T(1,128)S(1)}, f32[1,896]{1,0:T(1,128)S(1)}) custom-call(s32[16,24,128]{2,1,0:T(8,128)S(1)} %get-tuple-element.45.index), custom_call_target="tpu_custom_call" | custom-call | flops 6000000000 | bytes 18000000 | tf_op jit(solution)/shard_map/count_pairs/pallas_call | solution.py:557
  53.8 3.4 %all-to-all-done.1 = f32[8,88,128]{2,1,0:T(8,128)S(1)} async-done(((f32[8,88,128]{2,1,0:T(8,128)}), f32[8,88,128]{2,1,0:T(8,128)S(1)}, u32[]{:S(2)}, u32[]{:S(2)}) %all-to-all-start.1) | async-done | bytes 360480 | tf_op jit(solution)/shard_map/all_to_all | solution.py:644
  57.2 0.8 sum_shares.2
  57.9 3.4 %all-to-all-start.2 = ((f32[8,88,128]{2,1,0:T(8,128)}), f32[8,88,128]{2,1,0:T(8,128)S(1)}, u32[]{:S(2)}, u32[]{:S(2)}) async-start(f32[8,88,128]{2,1,0:T(8,128)} %bitcast.6), calls=%async_computation.2 | async-start | bytes 720896 | tf_op jit(solution)/shard_map/all_to_all | solution.py:644
  61.4 5.2 %count_pairs.3 = (bf16[1024,896]{1,0:T(8,128)(2,1)}, s8[384,512]{1,0:T(32,128)(4,1)}, s8[128,256]{1,0:T(32,128)(4,1)}, f32[1,128]{1,0:T(1,128)S(1)}, f32[1,896]{1,0:T(1,128)S(1)}) custom-call(s32[16,24,128]{2,1,0:T(8,128)S(1)} %get-tuple-element.45.index), custom_call_target="tpu_custom_call" | custom-call | flops 6000000000 | bytes 18000000 | tf_op jit(solution)/shard_map/count_pairs/pallas_call | solution.py:557
  66.6 3.3 %all-to-all-done.2 = f32[8,88,128]{2,1,0:T(8,128)S(1)} async-done(((f32[8,88,128]{2,1,0:T(8,128)}), f32[8,88,128]{2,1,0:T(8,128)S(1)}, u32[]{:S(2)}, u32[]{:S(2)}) %all-to-all-start.2) | async-done | bytes 360480 | tf_op jit(solution)/shard_map/all_to_all | solution.py:644
  69.9 4.7 %normal_apply.1 = (f32[704,128]{1,0:T(8,128)}, f32[2,32,128]{2,1,0:T(8,128)S(1)}, f32[16,128]{1,0:T(8,128)S(1)}) custom-call(bf16[1024,896]{1,0:T(8,128)(2,1)} %get-tuple-element.42.first, bf16[1024,896]{1,0:T(8,128)(2,1)} %get-tuple-element.46.last, s8[384,512]{1,0:T(32,128)(4,1)} %get-tuple-element.47.cmp_1, s8[384,512]{1,0:T(32,128)(4,1)} %get-tuple-element.48.cmp_2, ...), custom_call_target="tpu_custom_call" | custom-call | flops 3000000000 | bytes 9000000 | tf_op jit(solution)/shard_map/normal_apply/pallas_call | solution.py:598
  74.6 3.5 %all-to-all-start.3 = ((f32[8,88,128]{2,1,0:T(8,128)}), f32[8,88,128]{2,1,0:T(8,128)S(1)}, u32[]{:S(2)}, u32[]{:S(2)}) async-start(f32[8,88,128]{2,1,0:T(8,128)} %bitcast.8), calls=%async_computation.3 | async-start | bytes 720896 | tf_op jit(solution)/shard_map/all_to_all | solution.py:644
  78.1 1.1 pack_owned.2.refs_0_
  79.2 7.4 %all-to-all-done.3 = f32[8,88,128]{2,1,0:T(8,128)S(1)} async-done(((f32[8,88,128]{2,1,0:T(8,128)}), f32[8,88,128]{2,1,0:T(8,128)S(1)}, u32[]{:S(2)}, u32[]{:S(2)}) %all-to-all-start.3) | async-done | bytes 360480 | tf_op jit(solution)/shard_map/all_to_all | solution.py:644
  86.6 11.0 %all_to_all.59 = f32[8,88,128]{2,1,0:T(8,128)S(1)} all-to-all(f32[8,88,128]{2,1,0:T(8,128)S(1)} %sum_shares.3), channel_id=1, replica_groups=mesh['shot'=16,'rcv'=8] {'rcv'}, dimensions={0} | all-to-all | bytes 720896 | tf_op jit(solution)/shard_map/all_to_all | solution.py:644
  97.6 1.1 pack_owned.3
  98.7 3.9 %all-to-all-start.5 = ((f32[16,160,128]{2,1,0:T(8,128)}), f32[16,160,128]{2,1,0:T(8,128)S(1)}, u32[]{:S(2)}, u32[]{:S(2)}) async-start(f32[16,160,128]{2,1,0:T(8,128)} %pack_owned.3), calls=%async_computation.5 | async-start | bytes 2621440 | tf_op jit(solution)/shard_map/all_to_all | solution.py:644
  102.6 3.0 %norm_sums.1 = f32[1,128]{1,0:T(1,128)S(1)} custom-call(bf16[1024,896]{1,0:T(8,128)(2,1)} %get-tuple-element.42.first, bf16[1024,896]{1,0:T(8,128)(2,1)} %get-tuple-element.46.last, s8[384,512]{1,0:T(32,128)(4,1)} %get-tuple-element.47.cmp_1, s8[384,512]{1,0:T(32,128)(4,1)} %get-tuple-element.48.cmp_2, s8[128,256]{1,0:T(32,128)(4,1)} %get-tuple-element.49.rcv_1, ...), custom_call_target="tpu_custom_call" | custom-call | flops 2000000000 | bytes 6000000 | tf_op jit(solution)/shard_map/norm_sums/pallas_call | solution.py:617
  105.6 0.1 collective-permute-start
  105.7 1.1 collective-permute-done
  106.8 0.6 collective-permute-start.1
  107.4 3.0 %collective-permute-done.1 = f32[1,128]{1,0:T(1,128)S(1)} collective-permute-done((f32[1,128]{1,0:T(1,128)S(1)}, f32[1,128]{1,0:T(1,128)S(1)}, u32[]{:S(2)}, u32[]{:S(2)}) %collective-permute-start.1) | collective-permute-done | bytes 544 | tf_op jit(solution)/shard_map/ppermute | solution.py:704
  110.3 1.2 collective-permute-start.2
  111.5 3.6 %collective-permute-done.2 = f32[1,128]{1,0:T(1,128)S(1)} collective-permute-done((f32[1,128]{1,0:T(1,128)S(1)}, f32[1,128]{1,0:T(1,128)S(1)}, u32[]{:S(2)}, u32[]{:S(2)}) %collective-permute-start.2) | collective-permute-done | bytes 544 | tf_op jit(solution)/shard_map/ppermute | solution.py:704
  115.1 8.5 %all-to-all-done.5.owned = f32[16,160,128]{2,1,0:T(8,128)S(1)} async-done(((f32[16,160,128]{2,1,0:T(8,128)}), f32[16,160,128]{2,1,0:T(8,128)S(1)}, u32[]{:S(2)}, u32[]{:S(2)}) %all-to-all-start.5) | async-done | bytes 1310752 | tf_op jit(solution)/shard_map/all_to_all | solution.py:644
  123.6 10.5 %all_to_all.60.sums = f32[16,1,128]{2,1,0:T(1,128)S(1)} all-to-all(f32[16,1,128]{2,1,0:T(1,128)S(1)} %broadcast_in_dim.9), channel_id=1, replica_groups=mesh['shot'=16,'rcv'=8] {'shot'}, dimensions={0} | all-to-all | bytes 16384 | tf_op jit(solution)/shard_map/all_to_all | solution.py:644
  134.1 1.5 %finish.1 = (f32[128,512]{1,0:T(8,128)}, f32[1,16,512]{2,1,0:T(8,128)}, f32[128,512]{1,0:T(8,128)}, f32[32,512]{1,0:T(8,128)}) custom-call(f32[16,1,128]{2,1,0:T(1,128)S(1)} %all_to_all.60.sums, f32[16,160,128]{2,1,0:T(8,128)S(1)} %all-to-all-done.5.owned), custom_call_target="tpu_custom_call" | custom-call | tf_op jit(solution)/shard_map/finish/pallas_call | solution.py:758
  (5 shorter events, 0.0 us)
Async XLA Ops:
  43.3 13.9 %all-to-all-start.1 = ((f32[8,88,128]{2,1,0:T(8,128)}), f32[8,88,128]{2,1,0:T(8,128)S(1)}, u32[]{:S(2)}, u32[]{:S(2)}) async-start(f32[8,88,128]{2,1,0:T(8,128)} %bitcast.2), calls=%async_computation.1 | async-start | bytes 720896 | tf_op jit(solution)/shard_map/all_to_all | solution.py:644
  57.9 12.0 %all-to-all-start.2 = ((f32[8,88,128]{2,1,0:T(8,128)}), f32[8,88,128]{2,1,0:T(8,128)S(1)}, u32[]{:S(2)}, u32[]{:S(2)}) async-start(f32[8,88,128]{2,1,0:T(8,128)} %bitcast.6), calls=%async_computation.2 | async-start | bytes 720896 | tf_op jit(solution)/shard_map/all_to_all | solution.py:644
  74.6 12.0 %all-to-all-start.3 = ((f32[8,88,128]{2,1,0:T(8,128)}), f32[8,88,128]{2,1,0:T(8,128)S(1)}, u32[]{:S(2)}, u32[]{:S(2)}) async-start(f32[8,88,128]{2,1,0:T(8,128)} %bitcast.8), calls=%async_computation.3 | async-start | bytes 720896 | tf_op jit(solution)/shard_map/all_to_all | solution.py:644
  98.7 24.8 %all-to-all-start.5 = ((f32[16,160,128]{2,1,0:T(8,128)}), f32[16,160,128]{2,1,0:T(8,128)S(1)}, u32[]{:S(2)}, u32[]{:S(2)}) async-start(f32[16,160,128]{2,1,0:T(8,128)} %pack_owned.3), calls=%async_computation.5 | async-start | bytes 2621440 | tf_op jit(solution)/shard_map/all_to_all | solution.py:644
  105.6 1.2 collective-permute-start
  106.8 3.5 %collective-permute-start.1 = (f32[1,128]{1,0:T(1,128)S(1)}, f32[1,128]{1,0:T(1,128)S(1)}, u32[]{:S(2)}, u32[]{:S(2)}) collective-permute-start(f32[1,128]{1,0:T(1,128)S(1)} %add.9), channel_id=1, source_target_pairs={{0,2},{1,3},{2,0},{3,1},{4,6},{5,7},{6,4},{7,5},{8,10},{9,11},{10,... | collective-permute-start | bytes 1544 | tf_op jit(solution)/shard_map/ppermute | solution.py:704
  110.3 4.8 %collective-permute-start.2 = (f32[1,128]{1,0:T(1,128)S(1)}, f32[1,128]{1,0:T(1,128)S(1)}, u32[]{:S(2)}, u32[]{:S(2)}) collective-permute-start(f32[1,128]{1,0:T(1,128)S(1)} %add.10), channel_id=1, source_target_pairs={{0,6},{1,7},{2,4},{3,5},{4,2},{5,3},{6,0},{7,1},{8,14},{9,15},{10,... | collective-permute-start | bytes 1544 | tf_op jit(solution)/shard_map/ppermute | solution.py:704

commit v9 on v8

--- a/solution.py
+++ b/solution.py
@@ -704,14 +704,18 @@
     return lax.ppermute(value, axis, [(s, s ^ bit) for s in range(size)])
 
 
-def sum_over_rcv(sums):
+def gather_sums(sums):
     for bit in (1, 2, 6):
         sums = sums + swapped(sums, "rcv", N_RCV, bit)
-    return sums
+    here = jnp.arange(N_SHOT, dtype=jnp.int32)[:, None] == lax.axis_index("shot")
+    rows = jnp.where(here, sums, 0.0)
+    for bit in (1, 3, 4, 12):
+        rows = rows + swapped(rows, "shot", N_SHOT, bit)
+    return rows
 
 
 def finish_kernel(sums, owned, source, receiver, offset, cmp):
-    rows = sums[...].reshape(N_SHOT, LANES)
+    rows = sums[...]
     norm_b, cross, norm_z, norm_az, shift = (rows[:, lane : lane + 1] for lane in range(5))
     shift = shift * (1.0 / N_RCV)
 
@@ -791,10 +795,8 @@
     packed = pack_owned(tab_y, rcv_y, packed)
     tab_y, packed = lax.optimization_barrier((tab_y, packed))
     owned = exchange(packed, "shot")
-    sums = sum_over_rcv(norm_sums(tab_b, rcv_b, tab_y, rcv_y, own_count, index, counts))
-    owned, sums = lax.optimization_barrier((owned, sums))
-    sums = exchange(jnp.broadcast_to(sums[None], (N_SHOT, 1, LANES)), "shot")
-    return tuple(finish(sums, owned))
+    sums = norm_sums(tab_b, rcv_b, tab_y, rcv_y, own_count, index, counts)
+    return tuple(finish(gather_sums(sums), owned))
 
 
 def solution(mesh):

time: 136 us -> 135 us (level)
  blocking collectives: 51.9 us -> 41.4 us
  starting transfers between devices: 17.9 us -> 26.8 us
    all_to_all x3 -> x2, blocking collectives: 51.9 us -> 41.4 us  [exchange(): return lax.all_to_all(array, axis, split_axis=0, concat_axis=0, tiled=True)]
    ppermute x3 -> x7, starting transfers between devices: 1.82 us -> 10.7 us  [swapped(): return lax.ppermute(value, axis, [(s, s ^ bit) for s in range(size)])]
    all_to_all x4, waiting for transfers between devices: 22.5 us -> 14.1 us  [exchange(): return lax.all_to_all(array, axis, split_axis=0, concat_axis=0, tiled=True)]
    ppermute x3 -> x7, waiting for transfers between devices: 7.66 us -> 16 us  [swapped(): return lax.ppermute(value, axis, [(s, s ^ bit) for s in range(size)])]
  transfers between devices with their start and end apart: 7 -> 11, of which waited for: 7 -> 10; matrix products, arithmetic and copies ran while one was open for 0% -> 0% of each run, Pallas kernels for 11% -> 11%
where the time goes in v9:
time: 135 us; the launch traced here: 134 us
  blocking collectives  41.4 us (31%)
  Pallas kernels  35 us (26%)
  waiting for transfers between devices  30.1 us (22%)
  starting transfers between devices  26.8 us (20%)
    all_to_all x2, blocking collectives, exchange(): return lax.all_to_all(array, axis, split_axis=0, concat_axis=0, tiled=True)  41.4 us
    all_to_all x4, starting transfers between devices, exchange(): return lax.all_to_all(array, axis, split_axis=0, concat_axis=0, tiled=True)  16.1 us
    ppermute x7, waiting for transfers between devices, swapped(): return lax.ppermute(value, axis, [(s, s ^ bit) for s in range(size)])  16 us
    all_to_all x4, waiting for transfers between devices, exchange(): return lax.all_to_all(array, axis, split_axis=0, concat_axis=0, tiled=True)  14.1 us
    ppermute x7, starting transfers between devices, swapped(): return lax.ppermute(value, axis, [(s, s ^ bit) for s in range(size)])  10.7 us
    pallas_call x2, Pallas kernels, count_call(): pl.pallas_call(functools.partial(count_kernel, first=first), grid=(COUNT_...  10.5 us
    pallas_call x1, Pallas kernels, adjoint_apply(): pl.pallas_call(adjoint_kernel, out_shape=table_shapes() + [jax.ShapeDtype...  7.45 us
    pallas_call x1, Pallas kernels, normal_apply(): pl.pallas_call(normal_kernel, in_specs=[ANYWHERE] * 6 + [IN_VMEM] * 7, ou...  4.74 us
  transfers between devices with their start and end apart: 11, of which 10 were waited for; matrix products, arithmetic and copies ran while one was open for 0% of the time, Pallas kernels for 11%

profile of v9, /device:TPU:0, one launch (start us, length us, event | category | flops | bytes accessed | tf_op | source)
XLA Modules:
  0.0 134.2 jit_solution(4901576312366219954)
XLA Ops:
  0.6 4.7 %spectra.1 = f32[16,200,128]{2,1,0:T(8,128)S(1)} custom-call(bf16[640,1024]{1,0:T(8,128)(2,1)} %traces.1, bf16[1024,1024]{1,0:T(8,128)(2,1)} %constant.10.clone.waves, s32[16,80]{1,0:T(8,128)} %bitcast.19, s32[1,16]{1,0:T(1,128)} %refs_1_.1, s32[16,80]{1,0:T(8,128)} %bitcast.20, s32[640]{0:T(1024)} %refs_3_.1, s32[640]{0:T(1024)} %refs_4_.1, s32[640]{0:T(1024)} %refs_5_.1), custom_call_target="tpu_custom_call" | custom-call | flops 5000000000 | bytes 15000000 | tf_op jit(solution)/shard_map/spectra/pallas_call | solution.py:172
  5.4 30.4 %all_to_all.53.data = f32[16,200,128]{2,1,0:T(8,128)S(1)} all-to-all(f32[16,200,128]{2,1,0:T(8,128)S(1)} %spectra.1), channel_id=1, replica_groups=mesh['shot'=16,'rcv'=8] {'shot'}, dimensions={0} | all-to-all | bytes 3276800 | tf_op jit(solution)/shard_map/all_to_all | solution.py:644
  35.8 7.4 %adjoint_apply.1 = (f32[704,128]{1,0:T(8,128)}, f32[2,32,128]{2,1,0:T(8,128)S(1)}, s32[16,24,128]{2,1,0:T(8,128)S(1)}) custom-call(f32[16,200,128]{2,1,0:T(8,128)S(1)} %all_to_all.53.data), custom_call_target="tpu_custom_call" | custom-call | flops 8000000000 | bytes 24000000 | tf_op jit(solution)/shard_map/adjoint_apply/pallas_call | solution.py:538
  43.2 5.3 %all-to-all-start.1 = ((f32[8,88,128]{2,1,0:T(8,128)}), f32[8,88,128]{2,1,0:T(8,128)S(1)}, u32[]{:S(2)}, u32[]{:S(2)}) async-start(f32[8,88,128]{2,1,0:T(8,128)} %bitcast.2), calls=%async_computation.1 | async-start | bytes 720896 | tf_op jit(solution)/shard_map/all_to_all | solution.py:644
  48.5 5.2 %count_pairs.2 = (bf16[1024,896]{1,0:T(8,128)(2,1)}, s8[384,512]{1,0:T(32,128)(4,1)}, s8[128,256]{1,0:T(32,128)(4,1)}, f32[1,128]{1,0:T(1,128)S(1)}, f32[1,896]{1,0:T(1,128)S(1)}) custom-call(s32[16,24,128]{2,1,0:T(8,128)S(1)} %get-tuple-element.43.index), custom_call_target="tpu_custom_call" | custom-call | flops 6000000000 | bytes 18000000 | tf_op jit(solution)/shard_map/count_pairs/pallas_call | solution.py:557
  53.8 3.4 %all-to-all-done.1 = f32[8,88,128]{2,1,0:T(8,128)S(1)} async-done(((f32[8,88,128]{2,1,0:T(8,128)}), f32[8,88,128]{2,1,0:T(8,128)S(1)}, u32[]{:S(2)}, u32[]{:S(2)}) %all-to-all-start.1) | async-done | bytes 360480 | tf_op jit(solution)/shard_map/all_to_all | solution.py:644
  57.1 0.8 sum_shares.2
  57.9 3.4 %all-to-all-start.2 = ((f32[8,88,128]{2,1,0:T(8,128)}), f32[8,88,128]{2,1,0:T(8,128)S(1)}, u32[]{:S(2)}, u32[]{:S(2)}) async-start(f32[8,88,128]{2,1,0:T(8,128)} %bitcast.6), calls=%async_computation.2 | async-start | bytes 720896 | tf_op jit(solution)/shard_map/all_to_all | solution.py:644
  61.3 5.2 %count_pairs.3 = (bf16[1024,896]{1,0:T(8,128)(2,1)}, s8[384,512]{1,0:T(32,128)(4,1)}, s8[128,256]{1,0:T(32,128)(4,1)}, f32[1,128]{1,0:T(1,128)S(1)}, f32[1,896]{1,0:T(1,128)S(1)}) custom-call(s32[16,24,128]{2,1,0:T(8,128)S(1)} %get-tuple-element.43.index), custom_call_target="tpu_custom_call" | custom-call | flops 6000000000 | bytes 18000000 | tf_op jit(solution)/shard_map/count_pairs/pallas_call | solution.py:557
  66.6 3.3 %all-to-all-done.2 = f32[8,88,128]{2,1,0:T(8,128)S(1)} async-done(((f32[8,88,128]{2,1,0:T(8,128)}), f32[8,88,128]{2,1,0:T(8,128)S(1)}, u32[]{:S(2)}, u32[]{:S(2)}) %all-to-all-start.2) | async-done | bytes 360480 | tf_op jit(solution)/shard_map/all_to_all | solution.py:644
  69.9 4.7 %normal_apply.1 = (f32[704,128]{1,0:T(8,128)}, f32[2,32,128]{2,1,0:T(8,128)S(1)}, f32[16,128]{1,0:T(8,128)S(1)}) custom-call(bf16[1024,896]{1,0:T(8,128)(2,1)} %get-tuple-element.40.first, bf16[1024,896]{1,0:T(8,128)(2,1)} %get-tuple-element.44.last, s8[384,512]{1,0:T(32,128)(4,1)} %get-tuple-element.45.cmp_1, s8[384,512]{1,0:T(32,128)(4,1)} %get-tuple-element.46.cmp_2, ...), custom_call_target="tpu_custom_call" | custom-call | flops 3000000000 | bytes 9000000 | tf_op jit(solution)/shard_map/normal_apply/pallas_call | solution.py:598
  74.6 3.5 %all-to-all-start.3 = ((f32[8,88,128]{2,1,0:T(8,128)}), f32[8,88,128]{2,1,0:T(8,128)S(1)}, u32[]{:S(2)}, u32[]{:S(2)}) async-start(f32[8,88,128]{2,1,0:T(8,128)} %bitcast.8), calls=%async_computation.3 | async-start | bytes 720896 | tf_op jit(solution)/shard_map/all_to_all | solution.py:644
  78.1 1.1 pack_owned.2.refs_0_
  79.1 7.4 %all-to-all-done.3 = f32[8,88,128]{2,1,0:T(8,128)S(1)} async-done(((f32[8,88,128]{2,1,0:T(8,128)}), f32[8,88,128]{2,1,0:T(8,128)S(1)}, u32[]{:S(2)}, u32[]{:S(2)}) %all-to-all-start.3) | async-done | bytes 360480 | tf_op jit(solution)/shard_map/all_to_all | solution.py:644
  86.6 11.0 %all_to_all.54 = f32[8,88,128]{2,1,0:T(8,128)S(1)} all-to-all(f32[8,88,128]{2,1,0:T(8,128)S(1)} %sum_shares.3), channel_id=1, replica_groups=mesh['shot'=16,'rcv'=8] {'rcv'}, dimensions={0} | all-to-all | bytes 720896 | tf_op jit(solution)/shard_map/all_to_all | solution.py:644
  97.6 1.1 pack_owned.3
  98.6 3.9 %all-to-all-start.5 = ((f32[16,160,128]{2,1,0:T(8,128)}), f32[16,160,128]{2,1,0:T(8,128)S(1)}, u32[]{:S(2)}, u32[]{:S(2)}) async-start(f32[16,160,128]{2,1,0:T(8,128)} %pack_owned.3), calls=%async_computation.5 | async-start | bytes 2621440 | tf_op jit(solution)/shard_map/all_to_all | solution.py:644
  102.6 3.0 %norm_sums.1 = f32[1,128]{1,0:T(1,128)S(1)} custom-call(bf16[1024,896]{1,0:T(8,128)(2,1)} %get-tuple-element.40.first, bf16[1024,896]{1,0:T(8,128)(2,1)} %get-tuple-element.44.last, s8[384,512]{1,0:T(32,128)(4,1)} %get-tuple-element.45.cmp_1, s8[384,512]{1,0:T(32,128)(4,1)} %get-tuple-element.46.cmp_2, s8[128,256]{1,0:T(32,128)(4,1)} %get-tuple-element.47.rcv_1, ...), custom_call_target="tpu_custom_call" | custom-call | flops 2000000000 | bytes 6000000 | tf_op jit(solution)/shard_map/norm_sums/pallas_call | solution.py:617
  105.6 1.1 collective-permute-done
  106.7 0.6 collective-permute-start.1
  107.3 3.0 %collective-permute-done.1 = f32[1,128]{1,0:T(1,128)S(1)} collective-permute-done((f32[1,128]{1,0:T(1,128)S(1)}, f32[1,128]{1,0:T(1,128)S(1)}, u32[]{:S(2)}, u32[]{:S(2)}) %collective-permute-start.1) | collective-permute-done | bytes 544 | tf_op jit(solution)/shard_map/ppermute | solution.py:704
  110.3 1.2 collective-permute-start.2
  111.4 3.6 %collective-permute-done.2 = f32[1,128]{1,0:T(1,128)S(1)} collective-permute-done((f32[1,128]{1,0:T(1,128)S(1)}, f32[1,128]{1,0:T(1,128)S(1)}, u32[]{:S(2)}, u32[]{:S(2)}) %collective-permute-start.2) | collective-permute-done | bytes 544 | tf_op jit(solution)/shard_map/ppermute | solution.py:704
  115.1 1.6 %collective-permute-start.3 = (f32[16,128]{1,0:T(8,128)S(1)}, f32[16,128]{1,0:T(8,128)S(1)}, u32[]{:S(2)}, u32[]{:S(2)}) collective-permute-start(f32[16,128]{1,0:T(8,128)S(1)} %broadcast_select_fusion), channel_id=1, source_target_pairs={{0,8},{8,0},{16,24},{24,16},{32,40},{40,32},{48,56},{56,48},{64,72... | collective-permute-start | bytes 24584 | tf_op jit(solution)/shard_map/ppermute | solution.py:704
  116.7 2.2 %collective-permute-done.3 = f32[16,128]{1,0:T(8,128)S(1)} collective-permute-done((f32[16,128]{1,0:T(8,128)S(1)}, f32[16,128]{1,0:T(8,128)S(1)}, u32[]{:S(2)}, u32[]{:S(2)}) %collective-permute-start.3) | collective-permute-done | bytes 8224 | tf_op jit(solution)/shard_map/ppermute | solution.py:704
  119.0 2.7 %collective-permute-start.4 = (f32[16,128]{1,0:T(8,128)S(1)}, f32[16,128]{1,0:T(8,128)S(1)}, u32[]{:S(2)}, u32[]{:S(2)}) collective-permute-start(f32[16,128]{1,0:T(8,128)S(1)} %fusion), channel_id=1, source_target_pairs={{0,24},{8,16},{16,8},{24,0},{32,56},{40,48},{48,40},{56,32},{64,88... | collective-permute-start | bytes 24584 | tf_op jit(solution)/shard_map/ppermute | solution.py:704
  121.7 2.2 %collective-permute-done.4 = f32[16,128]{1,0:T(8,128)S(1)} collective-permute-done((f32[16,128]{1,0:T(8,128)S(1)}, f32[16,128]{1,0:T(8,128)S(1)}, u32[]{:S(2)}, u32[]{:S(2)}) %collective-permute-start.4) | collective-permute-done | bytes 8224 | tf_op jit(solution)/shard_map/ppermute | solution.py:704
  123.9 1.6 %collective-permute-start.5 = (f32[16,128]{1,0:T(8,128)S(1)}, f32[16,128]{1,0:T(8,128)S(1)}, u32[]{:S(2)}, u32[]{:S(2)}) collective-permute-start(f32[16,128]{1,0:T(8,128)S(1)} %fusion.1), channel_id=1, source_target_pairs={{0,32},{8,40},{16,48},{24,56},{32,0},{40,8},{48,16},{56,24},{64,96... | collective-permute-start | bytes 24584 | tf_op jit(solution)/shard_map/ppermute | solution.py:704
  125.6 2.0 %collective-permute-done.5 = f32[16,128]{1,0:T(8,128)S(1)} collective-permute-done((f32[16,128]{1,0:T(8,128)S(1)}, f32[16,128]{1,0:T(8,128)S(1)}, u32[]{:S(2)}, u32[]{:S(2)}) %collective-permute-start.5) | collective-permute-done | bytes 8224 | tf_op jit(solution)/shard_map/ppermute | solution.py:704
  127.6 2.9 %collective-permute-start.6 = (f32[16,128]{1,0:T(8,128)S(1)}, f32[16,128]{1,0:T(8,128)S(1)}, u32[]{:S(2)}, u32[]{:S(2)}) collective-permute-start(f32[16,128]{1,0:T(8,128)S(1)} %add.26), channel_id=1, source_target_pairs={{0,96},{8,104},{16,112},{24,120},{32,64},{40,72},{48,80},{56,88},{... | collective-permute-start | bytes 24584 | tf_op jit(solution)/shard_map/ppermute | solution.py:704
  130.5 2.0 %collective-permute-done.6 = f32[16,128]{1,0:T(8,128)S(1)} collective-permute-done((f32[16,128]{1,0:T(8,128)S(1)}, f32[16,128]{1,0:T(8,128)S(1)}, u32[]{:S(2)}, u32[]{:S(2)}) %collective-permute-start.6) | collective-permute-done | bytes 8224 | tf_op jit(solution)/shard_map/ppermute | solution.py:704
  132.5 1.7 %finish.1 = (f32[128,512]{1,0:T(8,128)}, f32[1,16,512]{2,1,0:T(8,128)}, f32[128,512]{1,0:T(8,128)}, f32[32,512]{1,0:T(8,128)}) custom-call(f32[16,128]{1,0:T(8,128)S(1)} %add.27.sums, f32[16,160,128]{2,1,0:T(8,128)S(1)} %all-to-all-done.5.owned), custom_call_target="tpu_custom_call" | custom-call | tf_op jit(solution)/shard_map/finish/pallas_call | solution.py:762
  (12 shorter events, 0.4 us)
Async XLA Ops:
  43.2 13.9 %all-to-all-start.1 = ((f32[8,88,128]{2,1,0:T(8,128)}), f32[8,88,128]{2,1,0:T(8,128)S(1)}, u32[]{:S(2)}, u32[]{:S(2)}) async-start(f32[8,88,128]{2,1,0:T(8,128)} %bitcast.2), calls=%async_computation.1 | async-start | bytes 720896 | tf_op jit(solution)/shard_map/all_to_all | solution.py:644
  57.9 12.0 %all-to-all-start.2 = ((f32[8,88,128]{2,1,0:T(8,128)}), f32[8,88,128]{2,1,0:T(8,128)S(1)}, u32[]{:S(2)}, u32[]{:S(2)}) async-start(f32[8,88,128]{2,1,0:T(8,128)} %bitcast.6), calls=%async_computation.2 | async-start | bytes 720896 | tf_op jit(solution)/shard_map/all_to_all | solution.py:644
  74.6 12.0 %all-to-all-start.3 = ((f32[8,88,128]{2,1,0:T(8,128)}), f32[8,88,128]{2,1,0:T(8,128)S(1)}, u32[]{:S(2)}, u32[]{:S(2)}) async-start(f32[8,88,128]{2,1,0:T(8,128)} %bitcast.8), calls=%async_computation.3 | async-start | bytes 720896 | tf_op jit(solution)/shard_map/all_to_all | solution.py:644
  98.6 33.8 %all-to-all-start.5 = ((f32[16,160,128]{2,1,0:T(8,128)}), f32[16,160,128]{2,1,0:T(8,128)S(1)}, u32[]{:S(2)}, u32[]{:S(2)}) async-start(f32[16,160,128]{2,1,0:T(8,128)} %pack_owned.3), calls=%async_computation.5 | async-start | bytes 2621440 | tf_op jit(solution)/shard_map/all_to_all | solution.py:644
  105.5 1.2 collective-permute-start
  106.7 3.5 %collective-permute-start.1 = (f32[1,128]{1,0:T(1,128)S(1)}, f32[1,128]{1,0:T(1,128)S(1)}, u32[]{:S(2)}, u32[]{:S(2)}) collective-permute-start(f32[1,128]{1,0:T(1,128)S(1)} %add.21), channel_id=1, source_target_pairs={{0,2},{1,3},{2,0},{3,1},{4,6},{5,7},{6,4},{7,5},{8,10},{9,11},{10,... | collective-permute-start | bytes 1544 | tf_op jit(solution)/shard_map/ppermute | solution.py:704
  110.3 4.8 %collective-permute-start.2 = (f32[1,128]{1,0:T(1,128)S(1)}, f32[1,128]{1,0:T(1,128)S(1)}, u32[]{:S(2)}, u32[]{:S(2)}) collective-permute-start(f32[1,128]{1,0:T(1,128)S(1)} %add.22), channel_id=1, source_target_pairs={{0,6},{1,7},{2,4},{3,5},{4,2},{5,3},{6,0},{7,1},{8,14},{9,15},{10,... | collective-permute-start | bytes 1544 | tf_op jit(solution)/shard_map/ppermute | solution.py:704
  115.1 3.8 %collective-permute-start.3 = (f32[16,128]{1,0:T(8,128)S(1)}, f32[16,128]{1,0:T(8,128)S(1)}, u32[]{:S(2)}, u32[]{:S(2)}) collective-permute-start(f32[16,128]{1,0:T(8,128)S(1)} %broadcast_select_fusion), channel_id=1, source_target_pairs={{0,8},{8,0},{16,24},{24,16},{32,40},{40,32},{48,56},{56,48},{64,72... | collective-permute-start | bytes 24584 | tf_op jit(solution)/shard_map/ppermute | solution.py:704
  119.0 4.9 %collective-permute-start.4 = (f32[16,128]{1,0:T(8,128)S(1)}, f32[16,128]{1,0:T(8,128)S(1)}, u32[]{:S(2)}, u32[]{:S(2)}) collective-permute-start(f32[16,128]{1,0:T(8,128)S(1)} %fusion), channel_id=1, source_target_pairs={{0,24},{8,16},{16,8},{24,0},{32,56},{40,48},{48,40},{56,32},{64,88... | collective-permute-start | bytes 24584 | tf_op jit(solution)/shard_map/ppermute | solution.py:704
  123.9 3.7 %collective-permute-start.5 = (f32[16,128]{1,0:T(8,128)S(1)}, f32[16,128]{1,0:T(8,128)S(1)}, u32[]{:S(2)}, u32[]{:S(2)}) collective-permute-start(f32[16,128]{1,0:T(8,128)S(1)} %fusion.1), channel_id=1, source_target_pairs={{0,32},{8,40},{16,48},{24,56},{32,0},{40,8},{48,16},{56,24},{64,96... | collective-permute-start | bytes 24584 | tf_op jit(solution)/shard_map/ppermute | solution.py:704
  127.6 4.9 %collective-permute-start.6 = (f32[16,128]{1,0:T(8,128)S(1)}, f32[16,128]{1,0:T(8,128)S(1)}, u32[]{:S(2)}, u32[]{:S(2)}) collective-permute-start(f32[16,128]{1,0:T(8,128)S(1)} %add.26), channel_id=1, source_target_pairs={{0,96},{8,104},{16,112},{24,120},{32,64},{40,72},{48,80},{56,88},{... | collective-permute-start | bytes 24584 | tf_op jit(solution)/shard_map/ppermute | solution.py:704

commit v10 on v9

--- a/solution.py
+++ b/solution.py
@@ -280,13 +280,16 @@
 EXACT = 128
 
 
+ROW_EXACT = 16
+
+
 def kept_part(counts):
-    return (counts.astype(jnp.int32) & (EXACT - 1)).astype(F32).astype(BF16)
-
-
-def left_over(counts):
+    return (counts.astype(jnp.int32) & (ROW_EXACT - 1)).astype(F32).astype(FP8)
+
+
+def left_over(counts, exact):
     whole = counts.astype(jnp.int32)
-    return (whole - (whole & (EXACT - 1))).astype(F32).astype(BF16)
+    return (whole - (whole & (exact - 1))).astype(F32).astype(BF16)
 
 
 def peak(counts):
@@ -326,7 +329,7 @@
         to_rcv[...] += rcv_counts
         diag[...] += jnp.sum(rows, axis=0, keepdims=True)
         kept[place * SRC_G : (place + 1) * SRC_G] = kept_part(rows)
-        most[...] = jnp.maximum(most[...], peak(rows))
+        most[...] = jnp.maximum(most[...], peak(rows) * (EXACT / ROW_EXACT))
 
     fill_hot(index[even + 1], ids, hot_odd)
     add(hot_even, 0)
@@ -356,9 +359,9 @@
                 rows, cmp_counts, rcv_counts = block_counts(hot)
                 to_cmp[...] += cmp_counts
                 to_rcv[...] += rcv_counts
-                use_rows(block, left_over(rows))
-
-            use_both(left_over(to_cmp[...]), left_over(to_rcv[...]))
+                use_rows(block, left_over(rows, ROW_EXACT))
+
+            use_both(left_over(to_cmp[...], EXACT), left_over(to_rcv[...], EXACT))
 
 
 def fetch_counts(refs, held, held_cmp, held_rcv, sems):
@@ -405,10 +408,11 @@
     shared[top:] = jnp.where(lanes < LANES, 1.0, 0.0).astype(BF16)
     for chunk in range(CHUNKS):
         copies[chunk].wait()
+        rows = held[chunk].astype(BF16)
         span = slice(chunk * CHUNK_ROWS, (chunk + 1) * CHUNK_ROWS)
-        sums = jnp.dot(own[:, span], held[chunk], preferred_element_type=F32)
+        sums = jnp.dot(own[:, span], rows, preferred_element_type=F32)
         to_shared[...] = sums if chunk == 0 else to_shared[...] + sums
-        to_own[:, span] = nt_dot(shared[...], held[chunk])
+        to_own[:, span] = nt_dot(shared[...], rows)
 
     def others(to_cmp, to_rcv):
         cmp_sums = jnp.dot(shared[:top, :OR], to_cmp, preferred_element_type=F32)
@@ -474,8 +478,9 @@
     load_halves(tab_z, rcv_z, own, shared)
     for chunk in range(CHUNKS):
         copies[chunk].wait()
+        rows = held[chunk].astype(BF16)
         span = slice(chunk * CHUNK_ROWS, (chunk + 1) * CHUNK_ROWS)
-        sums = jnp.dot(own[:, span], held[chunk], preferred_element_type=F32)
+        sums = jnp.dot(own[:, span], rows, preferred_element_type=F32)
         to_shared[...] = sums if chunk == 0 else to_shared[...] + sums
 
     def whole(tabs, own):
@@ -560,7 +565,7 @@
         in_specs=[whole_spec(*INDEX)],
         out_specs=[rows] + small,
         out_shape=[
-            pltpu.HBM(COUNTS, BF16),
+            pltpu.HBM(COUNTS, FP8),
             pltpu.HBM(TO_CMP, jnp.int8),
             pltpu.HBM(TO_RCV, jnp.int8),
             jax.ShapeDtypeStruct((1, LANES), F32),
@@ -577,7 +582,7 @@
 def count_scratch(chunks):
     return (
         [
-            VMEM((chunks, CHUNK_ROWS, SHARED), BF16),
+            VMEM((chunks, CHUNK_ROWS, SHARED), FP8),
             VMEM((2,) + TO_CMP, jnp.int8),
             VMEM((2,) + TO_RCV, jnp.int8),
             pltpu.SemaphoreType.DMA((chunks + 4,)),

time: 135 us -> 135 us (level)
  no operation moved by 1% of the time
where the time goes in v10:
time: 135 us; the launch traced here: 134 us
  blocking collectives  41.4 us (31%)
  Pallas kernels  34.5 us (26%)
  waiting for transfers between devices  30.6 us (23%)
  starting transfers between devices  26.6 us (20%)
    all_to_all x2, blocking collectives, exchange(): return lax.all_to_all(array, axis, split_axis=0, concat_axis=0, tiled=True)  41.4 us
    ppermute x7, waiting for transfers between devices, swapped(): return lax.ppermute(value, axis, [(s, s ^ bit) for s in range(size)])  16.4 us
    all_to_all x4, starting transfers between devices, exchange(): return lax.all_to_all(array, axis, split_axis=0, concat_axis=0, tiled=True)  16.1 us
    all_to_all x4, waiting for transfers between devices, exchange(): return lax.all_to_all(array, axis, split_axis=0, concat_axis=0, tiled=True)  14.2 us
    ppermute x7, starting transfers between devices, swapped(): return lax.ppermute(value, axis, [(s, s ^ bit) for s in range(size)])  10.5 us
    pallas_call x2, Pallas kernels, count_call(): pl.pallas_call(functools.partial(count_kernel, first=first), grid=(COUNT_...  10.3 us
    pallas_call x1, Pallas kernels, adjoint_apply(): pl.pallas_call(adjoint_kernel, out_shape=table_shapes() + [jax.ShapeDtype...  7.46 us
    pallas_call x1, Pallas kernels, log_spectra(): pl.pallas_call(spectra_kernel, in_specs=[ANYWHERE] * (2 + len(small)), ou...  4.72 us
  transfers between devices with their start and end apart: 11, of which 10 were waited for; matrix products, arithmetic and copies ran while one was open for 0% of the time, Pallas kernels for 11%

profile of v10, /device:TPU:0, one launch (start us, length us, event | category | flops | bytes accessed | tf_op | source)
XLA Modules:
  0.0 134.1 jit_solution(13118759315871839820)
XLA Ops:
  0.6 4.7 %spectra.1 = f32[16,200,128]{2,1,0:T(8,128)S(1)} custom-call(bf16[640,1024]{1,0:T(8,128)(2,1)} %traces.1, bf16[1024,1024]{1,0:T(8,128)(2,1)} %constant.10.clone.waves, s32[16,80]{1,0:T(8,128)} %bitcast.19, s32[1,16]{1,0:T(1,128)} %refs_1_.1, s32[16,80]{1,0:T(8,128)} %bitcast.20, s32[640]{0:T(1024)} %refs_3_.1, s32[640]{0:T(1024)} %refs_4_.1, s32[640]{0:T(1024)} %refs_5_.1), custom_call_target="tpu_custom_call" | custom-call | flops 5000000000 | bytes 15000000 | tf_op jit(solution)/shard_map/spectra/pallas_call | solution.py:172
  5.4 30.4 %all_to_all.53.data = f32[16,200,128]{2,1,0:T(8,128)S(1)} all-to-all(f32[16,200,128]{2,1,0:T(8,128)S(1)} %spectra.1), channel_id=1, replica_groups=mesh['shot'=16,'rcv'=8] {'shot'}, dimensions={0} | all-to-all | bytes 3276800 | tf_op jit(solution)/shard_map/all_to_all | solution.py:649
  35.8 7.5 %adjoint_apply.1 = (f32[704,128]{1,0:T(8,128)}, f32[2,32,128]{2,1,0:T(8,128)S(1)}, s32[16,24,128]{2,1,0:T(8,128)S(1)}) custom-call(f32[16,200,128]{2,1,0:T(8,128)S(1)} %all_to_all.53.data), custom_call_target="tpu_custom_call" | custom-call | flops 8000000000 | bytes 24000000 | tf_op jit(solution)/shard_map/adjoint_apply/pallas_call | solution.py:543
  43.2 5.3 %all-to-all-start.1 = ((f32[8,88,128]{2,1,0:T(8,128)}), f32[8,88,128]{2,1,0:T(8,128)S(1)}, u32[]{:S(2)}, u32[]{:S(2)}) async-start(f32[8,88,128]{2,1,0:T(8,128)} %bitcast.2), calls=%async_computation.1 | async-start | bytes 720896 | tf_op jit(solution)/shard_map/all_to_all | solution.py:649
  48.6 5.2 %count_pairs.2 = (f8e4m3fn[1024,896]{1,0:T(32,128)(4,1)}, s8[384,512]{1,0:T(32,128)(4,1)}, s8[128,256]{1,0:T(32,128)(4,1)}, f32[1,128]{1,0:T(1,128)S(1)}, f32[1,896]{1,0:T(1,128)S(1)}) custom-call(s32[16,24,128]{2,1,0:T(8,128)S(1)} %get-tuple-element.43.index), custom_call_target="tpu_custom_call" | custom-call | flops 6000000000 | bytes 18000000 | tf_op jit(solution)/shard_map/count_pairs/pallas_call | solution.py:562
  53.7 3.4 %all-to-all-done.1 = f32[8,88,128]{2,1,0:T(8,128)S(1)} async-done(((f32[8,88,128]{2,1,0:T(8,128)}), f32[8,88,128]{2,1,0:T(8,128)S(1)}, u32[]{:S(2)}, u32[]{:S(2)}) %all-to-all-start.1) | async-done | bytes 360480 | tf_op jit(solution)/shard_map/all_to_all | solution.py:649
  57.1 0.8 sum_shares.2
  57.9 3.4 %all-to-all-start.2 = ((f32[8,88,128]{2,1,0:T(8,128)}), f32[8,88,128]{2,1,0:T(8,128)S(1)}, u32[]{:S(2)}, u32[]{:S(2)}) async-start(f32[8,88,128]{2,1,0:T(8,128)} %bitcast.6), calls=%async_computation.2 | async-start | bytes 720896 | tf_op jit(solution)/shard_map/all_to_all | solution.py:649
  61.4 5.2 %count_pairs.3 = (f8e4m3fn[1024,896]{1,0:T(32,128)(4,1)}, s8[384,512]{1,0:T(32,128)(4,1)}, s8[128,256]{1,0:T(32,128)(4,1)}, f32[1,128]{1,0:T(1,128)S(1)}, f32[1,896]{1,0:T(1,128)S(1)}) custom-call(s32[16,24,128]{2,1,0:T(8,128)S(1)} %get-tuple-element.43.index), custom_call_target="tpu_custom_call" | custom-call | flops 6000000000 | bytes 18000000 | tf_op jit(solution)/shard_map/count_pairs/pallas_call | solution.py:562
  66.5 3.3 %all-to-all-done.2 = f32[8,88,128]{2,1,0:T(8,128)S(1)} async-done(((f32[8,88,128]{2,1,0:T(8,128)}), f32[8,88,128]{2,1,0:T(8,128)S(1)}, u32[]{:S(2)}, u32[]{:S(2)}) %all-to-all-start.2) | async-done | bytes 360480 | tf_op jit(solution)/shard_map/all_to_all | solution.py:649
  69.9 4.6 %normal_apply.1 = (f32[704,128]{1,0:T(8,128)}, f32[2,32,128]{2,1,0:T(8,128)S(1)}, f32[16,128]{1,0:T(8,128)S(1)}) custom-call(f8e4m3fn[1024,896]{1,0:T(32,128)(4,1)} %get-tuple-element.40.first, f8e4m3fn[1024,896]{1,0:T(32,128)(4,1)} %get-tuple-element.44.last, s8[384,512]{1,0:T(32,128)(4,1)} %get-tuple-element.45.cmp_1, ...), custom_call_target="tpu_custom_call" | custom-call | flops 3000000000 | bytes 9000000 | tf_op jit(solution)/shard_map/normal_apply/pallas_call | solution.py:603
  74.5 3.5 %all-to-all-start.3 = ((f32[8,88,128]{2,1,0:T(8,128)}), f32[8,88,128]{2,1,0:T(8,128)S(1)}, u32[]{:S(2)}, u32[]{:S(2)}) async-start(f32[8,88,128]{2,1,0:T(8,128)} %bitcast.8), calls=%async_computation.3 | async-start | bytes 720896 | tf_op jit(solution)/shard_map/all_to_all | solution.py:649
  77.9 1.1 pack_owned.2.refs_0_
  79.0 7.4 %all-to-all-done.3 = f32[8,88,128]{2,1,0:T(8,128)S(1)} async-done(((f32[8,88,128]{2,1,0:T(8,128)}), f32[8,88,128]{2,1,0:T(8,128)S(1)}, u32[]{:S(2)}, u32[]{:S(2)}) %all-to-all-start.3) | async-done | bytes 360480 | tf_op jit(solution)/shard_map/all_to_all | solution.py:649
  86.5 11.0 %all_to_all.54 = f32[8,88,128]{2,1,0:T(8,128)S(1)} all-to-all(f32[8,88,128]{2,1,0:T(8,128)S(1)} %sum_shares.3), channel_id=1, replica_groups=mesh['shot'=16,'rcv'=8] {'rcv'}, dimensions={0} | all-to-all | bytes 720896 | tf_op jit(solution)/shard_map/all_to_all | solution.py:649
  97.4 1.1 pack_owned.3
  98.5 3.9 %all-to-all-start.5 = ((f32[16,160,128]{2,1,0:T(8,128)}), f32[16,160,128]{2,1,0:T(8,128)S(1)}, u32[]{:S(2)}, u32[]{:S(2)}) async-start(f32[16,160,128]{2,1,0:T(8,128)} %pack_owned.3), calls=%async_computation.5 | async-start | bytes 2621440 | tf_op jit(solution)/shard_map/all_to_all | solution.py:649
  102.4 2.7 %norm_sums.1 = f32[1,128]{1,0:T(1,128)S(1)} custom-call(f8e4m3fn[1024,896]{1,0:T(32,128)(4,1)} %get-tuple-element.40.first, f8e4m3fn[1024,896]{1,0:T(32,128)(4,1)} %get-tuple-element.44.last, s8[384,512]{1,0:T(32,128)(4,1)} %get-tuple-element.45.cmp_1, s8[384,512]{1,0:T(32,128)(4,1)} %get-tuple-element.46.cmp_2, s8[128,256]{1,0:T(32,128)(4,1)} %get-tuple-element.47.rcv_1, ...), custom_call_target="tpu_custom_call" | custom-call | flops 2000000000 | bytes 6000000 | tf_op jit(solution)/shard_map/norm_sums/pallas_call | solution.py:622
  105.2 1.1 collective-permute-done
  106.4 0.6 collective-permute-start.1
  106.9 3.0 %collective-permute-done.1 = f32[1,128]{1,0:T(1,128)S(1)} collective-permute-done((f32[1,128]{1,0:T(1,128)S(1)}, f32[1,128]{1,0:T(1,128)S(1)}, u32[]{:S(2)}, u32[]{:S(2)}) %collective-permute-start.1) | collective-permute-done | bytes 544 | tf_op jit(solution)/shard_map/ppermute | solution.py:709
  109.9 1.2 collective-permute-start.2
  111.1 3.6 %collective-permute-done.2 = f32[1,128]{1,0:T(1,128)S(1)} collective-permute-done((f32[1,128]{1,0:T(1,128)S(1)}, f32[1,128]{1,0:T(1,128)S(1)}, u32[]{:S(2)}, u32[]{:S(2)}) %collective-permute-start.2) | collective-permute-done | bytes 544 | tf_op jit(solution)/shard_map/ppermute | solution.py:709
  114.7 1.6 %collective-permute-start.3 = (f32[16,128]{1,0:T(8,128)S(1)}, f32[16,128]{1,0:T(8,128)S(1)}, u32[]{:S(2)}, u32[]{:S(2)}) collective-permute-start(f32[16,128]{1,0:T(8,128)S(1)} %broadcast_select_fusion), channel_id=1, source_target_pairs={{0,8},{8,0},{16,24},{24,16},{32,40},{40,32},{48,56},{56,48},{64,72... | collective-permute-start | bytes 24584 | tf_op jit(solution)/shard_map/ppermute | solution.py:709
  116.4 2.4 %collective-permute-done.3 = f32[16,128]{1,0:T(8,128)S(1)} collective-permute-done((f32[16,128]{1,0:T(8,128)S(1)}, f32[16,128]{1,0:T(8,128)S(1)}, u32[]{:S(2)}, u32[]{:S(2)}) %collective-permute-start.3) | collective-permute-done | bytes 8224 | tf_op jit(solution)/shard_map/ppermute | solution.py:709
  118.9 2.6 %collective-permute-start.4 = (f32[16,128]{1,0:T(8,128)S(1)}, f32[16,128]{1,0:T(8,128)S(1)}, u32[]{:S(2)}, u32[]{:S(2)}) collective-permute-start(f32[16,128]{1,0:T(8,128)S(1)} %fusion), channel_id=1, source_target_pairs={{0,24},{8,16},{16,8},{24,0},{32,56},{40,48},{48,40},{56,32},{64,88... | collective-permute-start | bytes 24584 | tf_op jit(solution)/shard_map/ppermute | solution.py:709
  121.4 2.3 %collective-permute-done.4 = f32[16,128]{1,0:T(8,128)S(1)} collective-permute-done((f32[16,128]{1,0:T(8,128)S(1)}, f32[16,128]{1,0:T(8,128)S(1)}, u32[]{:S(2)}, u32[]{:S(2)}) %collective-permute-start.4) | collective-permute-done | bytes 8224 | tf_op jit(solution)/shard_map/ppermute | solution.py:709
  123.8 1.6 %collective-permute-start.5 = (f32[16,128]{1,0:T(8,128)S(1)}, f32[16,128]{1,0:T(8,128)S(1)}, u32[]{:S(2)}, u32[]{:S(2)}) collective-permute-start(f32[16,128]{1,0:T(8,128)S(1)} %fusion.1), channel_id=1, source_target_pairs={{0,32},{8,40},{16,48},{24,56},{32,0},{40,8},{48,16},{56,24},{64,96... | collective-permute-start | bytes 24584 | tf_op jit(solution)/shard_map/ppermute | solution.py:709
  125.4 2.0 %collective-permute-done.5 = f32[16,128]{1,0:T(8,128)S(1)} collective-permute-done((f32[16,128]{1,0:T(8,128)S(1)}, f32[16,128]{1,0:T(8,128)S(1)}, u32[]{:S(2)}, u32[]{:S(2)}) %collective-permute-start.5) | collective-permute-done | bytes 8224 | tf_op jit(solution)/shard_map/ppermute | solution.py:709
  127.5 2.9 %collective-permute-start.6 = (f32[16,128]{1,0:T(8,128)S(1)}, f32[16,128]{1,0:T(8,128)S(1)}, u32[]{:S(2)}, u32[]{:S(2)}) collective-permute-start(f32[16,128]{1,0:T(8,128)S(1)} %add.26), channel_id=1, source_target_pairs={{0,96},{8,104},{16,112},{24,120},{32,64},{40,72},{48,80},{56,88},{... | collective-permute-start | bytes 24584 | tf_op jit(solution)/shard_map/ppermute | solution.py:709
  130.3 2.0 %collective-permute-done.6 = f32[16,128]{1,0:T(8,128)S(1)} collective-permute-done((f32[16,128]{1,0:T(8,128)S(1)}, f32[16,128]{1,0:T(8,128)S(1)}, u32[]{:S(2)}, u32[]{:S(2)}) %collective-permute-start.6) | collective-permute-done | bytes 8224 | tf_op jit(solution)/shard_map/ppermute | solution.py:709
  132.3 1.7 %finish.1 = (f32[128,512]{1,0:T(8,128)}, f32[1,16,512]{2,1,0:T(8,128)}, f32[128,512]{1,0:T(8,128)}, f32[32,512]{1,0:T(8,128)}) custom-call(f32[16,128]{1,0:T(8,128)S(1)} %add.27.sums, f32[16,160,128]{2,1,0:T(8,128)S(1)} %all-to-all-done.5.owned), custom_call_target="tpu_custom_call" | custom-call | tf_op jit(solution)/shard_map/finish/pallas_call | solution.py:767
  (12 shorter events, 0.4 us)
Async XLA Ops:
  43.2 13.9 %all-to-all-start.1 = ((f32[8,88,128]{2,1,0:T(8,128)}), f32[8,88,128]{2,1,0:T(8,128)S(1)}, u32[]{:S(2)}, u32[]{:S(2)}) async-start(f32[8,88,128]{2,1,0:T(8,128)} %bitcast.2), calls=%async_computation.1 | async-start | bytes 720896 | tf_op jit(solution)/shard_map/all_to_all | solution.py:649
  57.9 12.0 %all-to-all-start.2 = ((f32[8,88,128]{2,1,0:T(8,128)}), f32[8,88,128]{2,1,0:T(8,128)S(1)}, u32[]{:S(2)}, u32[]{:S(2)}) async-start(f32[8,88,128]{2,1,0:T(8,128)} %bitcast.6), calls=%async_computation.2 | async-start | bytes 720896 | tf_op jit(solution)/shard_map/all_to_all | solution.py:649
  74.5 12.0 %all-to-all-start.3 = ((f32[8,88,128]{2,1,0:T(8,128)}), f32[8,88,128]{2,1,0:T(8,128)S(1)}, u32[]{:S(2)}, u32[]{:S(2)}) async-start(f32[8,88,128]{2,1,0:T(8,128)} %bitcast.8), calls=%async_computation.3 | async-start | bytes 720896 | tf_op jit(solution)/shard_map/all_to_all | solution.py:649
  98.5 33.8 %all-to-all-start.5 = ((f32[16,160,128]{2,1,0:T(8,128)}), f32[16,160,128]{2,1,0:T(8,128)S(1)}, u32[]{:S(2)}, u32[]{:S(2)}) async-start(f32[16,160,128]{2,1,0:T(8,128)} %pack_owned.3), calls=%async_computation.5 | async-start | bytes 2621440 | tf_op jit(solution)/shard_map/all_to_all | solution.py:649
  105.2 1.2 collective-permute-start
  106.4 3.5 %collective-permute-start.1 = (f32[1,128]{1,0:T(1,128)S(1)}, f32[1,128]{1,0:T(1,128)S(1)}, u32[]{:S(2)}, u32[]{:S(2)}) collective-permute-start(f32[1,128]{1,0:T(1,128)S(1)} %add.21), channel_id=1, source_target_pairs={{0,2},{1,3},{2,0},{3,1},{4,6},{5,7},{6,4},{7,5},{8,10},{9,11},{10,... | collective-permute-start | bytes 1544 | tf_op jit(solution)/shard_map/ppermute | solution.py:709
  109.9 4.8 %collective-permute-start.2 = (f32[1,128]{1,0:T(1,128)S(1)}, f32[1,128]{1,0:T(1,128)S(1)}, u32[]{:S(2)}, u32[]{:S(2)}) collective-permute-start(f32[1,128]{1,0:T(1,128)S(1)} %add.22), channel_id=1, source_target_pairs={{0,6},{1,7},{2,4},{3,5},{4,2},{5,3},{6,0},{7,1},{8,14},{9,15},{10,... | collective-permute-start | bytes 1544 | tf_op jit(solution)/shard_map/ppermute | solution.py:709
  114.7 4.0 %collective-permute-start.3 = (f32[16,128]{1,0:T(8,128)S(1)}, f32[16,128]{1,0:T(8,128)S(1)}, u32[]{:S(2)}, u32[]{:S(2)}) collective-permute-start(f32[16,128]{1,0:T(8,128)S(1)} %broadcast_select_fusion), channel_id=1, source_target_pairs={{0,8},{8,0},{16,24},{24,16},{32,40},{40,32},{48,56},{56,48},{64,72... | collective-permute-start | bytes 24584 | tf_op jit(solution)/shard_map/ppermute | solution.py:709
  118.9 4.9 %collective-permute-start.4 = (f32[16,128]{1,0:T(8,128)S(1)}, f32[16,128]{1,0:T(8,128)S(1)}, u32[]{:S(2)}, u32[]{:S(2)}) collective-permute-start(f32[16,128]{1,0:T(8,128)S(1)} %fusion), channel_id=1, source_target_pairs={{0,24},{8,16},{16,8},{24,0},{32,56},{40,48},{48,40},{56,32},{64,88... | collective-permute-start | bytes 24584 | tf_op jit(solution)/shard_map/ppermute | solution.py:709
  123.8 3.7 %collective-permute-start.5 = (f32[16,128]{1,0:T(8,128)S(1)}, f32[16,128]{1,0:T(8,128)S(1)}, u32[]{:S(2)}, u32[]{:S(2)}) collective-permute-start(f32[16,128]{1,0:T(8,128)S(1)} %fusion.1), channel_id=1, source_target_pairs={{0,32},{8,40},{16,48},{24,56},{32,0},{40,8},{48,16},{56,24},{64,96... | collective-permute-start | bytes 24584 | tf_op jit(solution)/shard_map/ppermute | solution.py:709
  127.5 4.9 %collective-permute-start.6 = (f32[16,128]{1,0:T(8,128)S(1)}, f32[16,128]{1,0:T(8,128)S(1)}, u32[]{:S(2)}, u32[]{:S(2)}) collective-permute-start(f32[16,128]{1,0:T(8,128)S(1)} %add.26), channel_id=1, source_target_pairs={{0,96},{8,104},{16,112},{24,120},{32,64},{40,72},{48,80},{56,88},{... | collective-permute-start | bytes 24584 | tf_op jit(solution)/shard_map/ppermute | solution.py:709

commit v11 on v9

--- a/solution.py
+++ b/solution.py
@@ -268,7 +268,7 @@
     fill_ids(ids)
     prepare_block(data, index, ids, hot_even, 0)
 
-    @pl.loop(0, N_SHOT // 2)
+    @pl.loop(0, N_SHOT // 2, unroll=2)
     def _(pair):
         even = 2 * pair
         prepare_block(data, index, ids, hot_odd, even + 1)

time: 135 us -> 134 us (level)
  no operation moved by 1% of the time
where the time goes in v11:
time: 134 us
  blocking collectives  41.4 us (31%)
  Pallas kernels  34.4 us (26%)
  waiting for transfers between devices  30.1 us (22%)
  starting transfers between devices  26.8 us (20%)
    all_to_all x2, blocking collectives, exchange(): return lax.all_to_all(array, axis, split_axis=0, concat_axis=0, tiled=True)  41.4 us
    ppermute x7, waiting for transfers between devices, swapped(): return lax.ppermute(value, axis, [(s, s ^ bit) for s in range(size)])  16 us
    all_to_all x4, starting transfers between devices, exchange(): return lax.all_to_all(array, axis, split_axis=0, concat_axis=0, tiled=True)  15.9 us
    all_to_all x4, waiting for transfers between devices, exchange(): return lax.all_to_all(array, axis, split_axis=0, concat_axis=0, tiled=True)  14.1 us
    ppermute x7, starting transfers between devices, swapped(): return lax.ppermute(value, axis, [(s, s ^ bit) for s in range(size)])  10.8 us
    pallas_call x2, Pallas kernels, count_call(): pl.pallas_call(functools.partial(count_kernel, first=first), grid=(COUNT_...  10.5 us
    pallas_call x1, Pallas kernels, adjoint_apply(): pl.pallas_call(adjoint_kernel, out_shape=table_shapes() + [jax.ShapeDtype...  6.86 us
    pallas_call x1, Pallas kernels, normal_apply(): pl.pallas_call(normal_kernel, in_specs=[ANYWHERE] * 6 + [IN_VMEM] * 7, ou...  4.74 us
  transfers between devices with their start and end apart: 11, of which 10 were waited for; matrix products, arithmetic and copies ran while one was open for 0% of the time, Pallas kernels for 11%

profile of v11, /device:TPU:0, one launch (start us, length us, event | category | flops | bytes accessed | tf_op | source)
XLA Modules:
  0.0 133.6 jit_solution(3305217332704410937)
XLA Ops:
  0.6 4.7 %spectra.1 = f32[16,200,128]{2,1,0:T(8,128)S(1)} custom-call(bf16[640,1024]{1,0:T(8,128)(2,1)} %traces.1, bf16[1024,1024]{1,0:T(8,128)(2,1)} %constant.10.clone.waves, s32[16,80]{1,0:T(8,128)} %bitcast.19, s32[1,16]{1,0:T(1,128)} %refs_1_.1, s32[16,80]{1,0:T(8,128)} %bitcast.20, s32[640]{0:T(1024)} %refs_3_.1, s32[640]{0:T(1024)} %refs_4_.1, s32[640]{0:T(1024)} %refs_5_.1), custom_call_target="tpu_custom_call" | custom-call | flops 5000000000 | bytes 15000000 | tf_op jit(solution)/shard_map/spectra/pallas_call | solution.py:172
  5.4 30.4 %all_to_all.53.data = f32[16,200,128]{2,1,0:T(8,128)S(1)} all-to-all(f32[16,200,128]{2,1,0:T(8,128)S(1)} %spectra.1), channel_id=1, replica_groups=mesh['shot'=16,'rcv'=8] {'shot'}, dimensions={0} | all-to-all | bytes 3276800 | tf_op jit(solution)/shard_map/all_to_all | solution.py:644
  35.8 6.9 %adjoint_apply.1 = (f32[704,128]{1,0:T(8,128)}, f32[2,32,128]{2,1,0:T(8,128)S(1)}, s32[16,24,128]{2,1,0:T(8,128)S(1)}) custom-call(f32[16,200,128]{2,1,0:T(8,128)S(1)} %all_to_all.53.data), custom_call_target="tpu_custom_call" | custom-call | flops 8000000000 | bytes 24000000 | tf_op jit(solution)/shard_map/adjoint_apply/pallas_call | solution.py:538
  42.6 5.3 %all-to-all-start.1 = ((f32[8,88,128]{2,1,0:T(8,128)}), f32[8,88,128]{2,1,0:T(8,128)S(1)}, u32[]{:S(2)}, u32[]{:S(2)}) async-start(f32[8,88,128]{2,1,0:T(8,128)} %bitcast.2), calls=%async_computation.1 | async-start | bytes 720896 | tf_op jit(solution)/shard_map/all_to_all | solution.py:644
  48.0 5.2 %count_pairs.2 = (bf16[1024,896]{1,0:T(8,128)(2,1)}, s8[384,512]{1,0:T(32,128)(4,1)}, s8[128,256]{1,0:T(32,128)(4,1)}, f32[1,128]{1,0:T(1,128)S(1)}, f32[1,896]{1,0:T(1,128)S(1)}) custom-call(s32[16,24,128]{2,1,0:T(8,128)S(1)} %get-tuple-element.43.index), custom_call_target="tpu_custom_call" | custom-call | flops 6000000000 | bytes 18000000 | tf_op jit(solution)/shard_map/count_pairs/pallas_call | solution.py:557
  53.2 3.4 %all-to-all-done.1 = f32[8,88,128]{2,1,0:T(8,128)S(1)} async-done(((f32[8,88,128]{2,1,0:T(8,128)}), f32[8,88,128]{2,1,0:T(8,128)S(1)}, u32[]{:S(2)}, u32[]{:S(2)}) %all-to-all-start.1) | async-done | bytes 360480 | tf_op jit(solution)/shard_map/all_to_all | solution.py:644
  56.5 0.8 sum_shares.2
  57.3 3.4 %all-to-all-start.2 = ((f32[8,88,128]{2,1,0:T(8,128)}), f32[8,88,128]{2,1,0:T(8,128)S(1)}, u32[]{:S(2)}, u32[]{:S(2)}) async-start(f32[8,88,128]{2,1,0:T(8,128)} %bitcast.6), calls=%async_computation.2 | async-start | bytes 720896 | tf_op jit(solution)/shard_map/all_to_all | solution.py:644
  60.8 5.2 %count_pairs.3 = (bf16[1024,896]{1,0:T(8,128)(2,1)}, s8[384,512]{1,0:T(32,128)(4,1)}, s8[128,256]{1,0:T(32,128)(4,1)}, f32[1,128]{1,0:T(1,128)S(1)}, f32[1,896]{1,0:T(1,128)S(1)}) custom-call(s32[16,24,128]{2,1,0:T(8,128)S(1)} %get-tuple-element.43.index), custom_call_target="tpu_custom_call" | custom-call | flops 6000000000 | bytes 18000000 | tf_op jit(solution)/shard_map/count_pairs/pallas_call | solution.py:557
  66.0 3.3 %all-to-all-done.2 = f32[8,88,128]{2,1,0:T(8,128)S(1)} async-done(((f32[8,88,128]{2,1,0:T(8,128)}), f32[8,88,128]{2,1,0:T(8,128)S(1)}, u32[]{:S(2)}, u32[]{:S(2)}) %all-to-all-start.2) | async-done | bytes 360480 | tf_op jit(solution)/shard_map/all_to_all | solution.py:644
  69.3 4.7 %normal_apply.1 = (f32[704,128]{1,0:T(8,128)}, f32[2,32,128]{2,1,0:T(8,128)S(1)}, f32[16,128]{1,0:T(8,128)S(1)}) custom-call(bf16[1024,896]{1,0:T(8,128)(2,1)} %get-tuple-element.40.first, bf16[1024,896]{1,0:T(8,128)(2,1)} %get-tuple-element.44.last, s8[384,512]{1,0:T(32,128)(4,1)} %get-tuple-element.45.cmp_1, s8[384,512]{1,0:T(32,128)(4,1)} %get-tuple-element.46.cmp_2, ...), custom_call_target="tpu_custom_call" | custom-call | flops 3000000000 | bytes 9000000 | tf_op jit(solution)/shard_map/normal_apply/pallas_call | solution.py:598
  74.0 3.5 %all-to-all-start.3 = ((f32[8,88,128]{2,1,0:T(8,128)}), f32[8,88,128]{2,1,0:T(8,128)S(1)}, u32[]{:S(2)}, u32[]{:S(2)}) async-start(f32[8,88,128]{2,1,0:T(8,128)} %bitcast.8), calls=%async_computation.3 | async-start | bytes 720896 | tf_op jit(solution)/shard_map/all_to_all | solution.py:644
  77.5 1.1 pack_owned.2.refs_0_
  78.5 7.4 %all-to-all-done.3 = f32[8,88,128]{2,1,0:T(8,128)S(1)} async-done(((f32[8,88,128]{2,1,0:T(8,128)}), f32[8,88,128]{2,1,0:T(8,128)S(1)}, u32[]{:S(2)}, u32[]{:S(2)}) %all-to-all-start.3) | async-done | bytes 360480 | tf_op jit(solution)/shard_map/all_to_all | solution.py:644
  86.0 11.0 %all_to_all.54 = f32[8,88,128]{2,1,0:T(8,128)S(1)} all-to-all(f32[8,88,128]{2,1,0:T(8,128)S(1)} %sum_shares.3), channel_id=1, replica_groups=mesh['shot'=16,'rcv'=8] {'rcv'}, dimensions={0} | all-to-all | bytes 720896 | tf_op jit(solution)/shard_map/all_to_all | solution.py:644
  97.0 1.1 pack_owned.3
  98.1 3.7 %all-to-all-start.5 = ((f32[16,160,128]{2,1,0:T(8,128)}), f32[16,160,128]{2,1,0:T(8,128)S(1)}, u32[]{:S(2)}, u32[]{:S(2)}) async-start(f32[16,160,128]{2,1,0:T(8,128)} %pack_owned.3), calls=%async_computation.5 | async-start | bytes 2621440 | tf_op jit(solution)/shard_map/all_to_all | solution.py:644
  101.8 3.0 %norm_sums.1 = f32[1,128]{1,0:T(1,128)S(1)} custom-call(bf16[1024,896]{1,0:T(8,128)(2,1)} %get-tuple-element.40.first, bf16[1024,896]{1,0:T(8,128)(2,1)} %get-tuple-element.44.last, s8[384,512]{1,0:T(32,128)(4,1)} %get-tuple-element.45.cmp_1, s8[384,512]{1,0:T(32,128)(4,1)} %get-tuple-element.46.cmp_2, s8[128,256]{1,0:T(32,128)(4,1)} %get-tuple-element.47.rcv_1, ...), custom_call_target="tpu_custom_call" | custom-call | flops 2000000000 | bytes 6000000 | tf_op jit(solution)/shard_map/norm_sums/pallas_call | solution.py:617
  104.8 1.1 collective-permute-done
  105.9 0.6 collective-permute-start.1
  106.5 3.0 %collective-permute-done.1 = f32[1,128]{1,0:T(1,128)S(1)} collective-permute-done((f32[1,128]{1,0:T(1,128)S(1)}, f32[1,128]{1,0:T(1,128)S(1)}, u32[]{:S(2)}, u32[]{:S(2)}) %collective-permute-start.1) | collective-permute-done | bytes 544 | tf_op jit(solution)/shard_map/ppermute | solution.py:704
  109.5 1.2 collective-permute-start.2
  110.7 3.6 %collective-permute-done.2 = f32[1,128]{1,0:T(1,128)S(1)} collective-permute-done((f32[1,128]{1,0:T(1,128)S(1)}, f32[1,128]{1,0:T(1,128)S(1)}, u32[]{:S(2)}, u32[]{:S(2)}) %collective-permute-start.2) | collective-permute-done | bytes 544 | tf_op jit(solution)/shard_map/ppermute | solution.py:704
  114.3 1.8 %collective-permute-start.3 = (f32[16,128]{1,0:T(8,128)S(1)}, f32[16,128]{1,0:T(8,128)S(1)}, u32[]{:S(2)}, u32[]{:S(2)}) collective-permute-start(f32[16,128]{1,0:T(8,128)S(1)} %broadcast_select_fusion), channel_id=1, source_target_pairs={{0,8},{8,0},{16,24},{24,16},{32,40},{40,32},{48,56},{56,48},{64,72... | collective-permute-start | bytes 24584 | tf_op jit(solution)/shard_map/ppermute | solution.py:704
  116.1 2.2 %collective-permute-done.3 = f32[16,128]{1,0:T(8,128)S(1)} collective-permute-done((f32[16,128]{1,0:T(8,128)S(1)}, f32[16,128]{1,0:T(8,128)S(1)}, u32[]{:S(2)}, u32[]{:S(2)}) %collective-permute-start.3) | collective-permute-done | bytes 8224 | tf_op jit(solution)/shard_map/ppermute | solution.py:704
  118.4 2.7 %collective-permute-start.4 = (f32[16,128]{1,0:T(8,128)S(1)}, f32[16,128]{1,0:T(8,128)S(1)}, u32[]{:S(2)}, u32[]{:S(2)}) collective-permute-start(f32[16,128]{1,0:T(8,128)S(1)} %fusion), channel_id=1, source_target_pairs={{0,24},{8,16},{16,8},{24,0},{32,56},{40,48},{48,40},{56,32},{64,88... | collective-permute-start | bytes 24584 | tf_op jit(solution)/shard_map/ppermute | solution.py:704
  121.1 2.2 %collective-permute-done.4 = f32[16,128]{1,0:T(8,128)S(1)} collective-permute-done((f32[16,128]{1,0:T(8,128)S(1)}, f32[16,128]{1,0:T(8,128)S(1)}, u32[]{:S(2)}, u32[]{:S(2)}) %collective-permute-start.4) | collective-permute-done | bytes 8224 | tf_op jit(solution)/shard_map/ppermute | solution.py:704
  123.3 1.6 %collective-permute-start.5 = (f32[16,128]{1,0:T(8,128)S(1)}, f32[16,128]{1,0:T(8,128)S(1)}, u32[]{:S(2)}, u32[]{:S(2)}) collective-permute-start(f32[16,128]{1,0:T(8,128)S(1)} %fusion.1), channel_id=1, source_target_pairs={{0,32},{8,40},{16,48},{24,56},{32,0},{40,8},{48,16},{56,24},{64,96... | collective-permute-start | bytes 24584 | tf_op jit(solution)/shard_map/ppermute | solution.py:704
  125.0 2.0 %collective-permute-done.5 = f32[16,128]{1,0:T(8,128)S(1)} collective-permute-done((f32[16,128]{1,0:T(8,128)S(1)}, f32[16,128]{1,0:T(8,128)S(1)}, u32[]{:S(2)}, u32[]{:S(2)}) %collective-permute-start.5) | collective-permute-done | bytes 8224 | tf_op jit(solution)/shard_map/ppermute | solution.py:704
  127.0 2.9 %collective-permute-start.6 = (f32[16,128]{1,0:T(8,128)S(1)}, f32[16,128]{1,0:T(8,128)S(1)}, u32[]{:S(2)}, u32[]{:S(2)}) collective-permute-start(f32[16,128]{1,0:T(8,128)S(1)} %add.26), channel_id=1, source_target_pairs={{0,96},{8,104},{16,112},{24,120},{32,64},{40,72},{48,80},{56,88},{... | collective-permute-start | bytes 24584 | tf_op jit(solution)/shard_map/ppermute | solution.py:704
  129.9 2.0 %collective-permute-done.6 = f32[16,128]{1,0:T(8,128)S(1)} collective-permute-done((f32[16,128]{1,0:T(8,128)S(1)}, f32[16,128]{1,0:T(8,128)S(1)}, u32[]{:S(2)}, u32[]{:S(2)}) %collective-permute-start.6) | collective-permute-done | bytes 8224 | tf_op jit(solution)/shard_map/ppermute | solution.py:704
  131.9 1.7 %finish.1 = (f32[128,512]{1,0:T(8,128)}, f32[1,16,512]{2,1,0:T(8,128)}, f32[128,512]{1,0:T(8,128)}, f32[32,512]{1,0:T(8,128)}) custom-call(f32[16,128]{1,0:T(8,128)S(1)} %add.27.sums, f32[16,160,128]{2,1,0:T(8,128)S(1)} %all-to-all-done.5.owned), custom_call_target="tpu_custom_call" | custom-call | tf_op jit(solution)/shard_map/finish/pallas_call | solution.py:762
  (12 shorter events, 0.4 us)
Async XLA Ops:
  42.6 13.9 %all-to-all-start.1 = ((f32[8,88,128]{2,1,0:T(8,128)}), f32[8,88,128]{2,1,0:T(8,128)S(1)}, u32[]{:S(2)}, u32[]{:S(2)}) async-start(f32[8,88,128]{2,1,0:T(8,128)} %bitcast.2), calls=%async_computation.1 | async-start | bytes 720896 | tf_op jit(solution)/shard_map/all_to_all | solution.py:644
  57.3 12.0 %all-to-all-start.2 = ((f32[8,88,128]{2,1,0:T(8,128)}), f32[8,88,128]{2,1,0:T(8,128)S(1)}, u32[]{:S(2)}, u32[]{:S(2)}) async-start(f32[8,88,128]{2,1,0:T(8,128)} %bitcast.6), calls=%async_computation.2 | async-start | bytes 720896 | tf_op jit(solution)/shard_map/all_to_all | solution.py:644
  74.0 12.0 %all-to-all-start.3 = ((f32[8,88,128]{2,1,0:T(8,128)}), f32[8,88,128]{2,1,0:T(8,128)S(1)}, u32[]{:S(2)}, u32[]{:S(2)}) async-start(f32[8,88,128]{2,1,0:T(8,128)} %bitcast.8), calls=%async_computation.3 | async-start | bytes 720896 | tf_op jit(solution)/shard_map/all_to_all | solution.py:644
  98.1 33.8 %all-to-all-start.5 = ((f32[16,160,128]{2,1,0:T(8,128)}), f32[16,160,128]{2,1,0:T(8,128)S(1)}, u32[]{:S(2)}, u32[]{:S(2)}) async-start(f32[16,160,128]{2,1,0:T(8,128)} %pack_owned.3), calls=%async_computation.5 | async-start | bytes 2621440 | tf_op jit(solution)/shard_map/all_to_all | solution.py:644
  104.7 1.2 collective-permute-start
  105.9 3.5 %collective-permute-start.1 = (f32[1,128]{1,0:T(1,128)S(1)}, f32[1,128]{1,0:T(1,128)S(1)}, u32[]{:S(2)}, u32[]{:S(2)}) collective-permute-start(f32[1,128]{1,0:T(1,128)S(1)} %add.21), channel_id=1, source_target_pairs={{0,2},{1,3},{2,0},{3,1},{4,6},{5,7},{6,4},{7,5},{8,10},{9,11},{10,... | collective-permute-start | bytes 1544 | tf_op jit(solution)/shard_map/ppermute | solution.py:704
  109.5 4.8 %collective-permute-start.2 = (f32[1,128]{1,0:T(1,128)S(1)}, f32[1,128]{1,0:T(1,128)S(1)}, u32[]{:S(2)}, u32[]{:S(2)}) collective-permute-start(f32[1,128]{1,0:T(1,128)S(1)} %add.22), channel_id=1, source_target_pairs={{0,6},{1,7},{2,4},{3,5},{4,2},{5,3},{6,0},{7,1},{8,14},{9,15},{10,... | collective-permute-start | bytes 1544 | tf_op jit(solution)/shard_map/ppermute | solution.py:704
  114.3 4.0 %collective-permute-start.3 = (f32[16,128]{1,0:T(8,128)S(1)}, f32[16,128]{1,0:T(8,128)S(1)}, u32[]{:S(2)}, u32[]{:S(2)}) collective-permute-start(f32[16,128]{1,0:T(8,128)S(1)} %broadcast_select_fusion), channel_id=1, source_target_pairs={{0,8},{8,0},{16,24},{24,16},{32,40},{40,32},{48,56},{56,48},{64,72... | collective-permute-start | bytes 24584 | tf_op jit(solution)/shard_map/ppermute | solution.py:704
  118.4 4.9 %collective-permute-start.4 = (f32[16,128]{1,0:T(8,128)S(1)}, f32[16,128]{1,0:T(8,128)S(1)}, u32[]{:S(2)}, u32[]{:S(2)}) collective-permute-start(f32[16,128]{1,0:T(8,128)S(1)} %fusion), channel_id=1, source_target_pairs={{0,24},{8,16},{16,8},{24,0},{32,56},{40,48},{48,40},{56,32},{64,88... | collective-permute-start | bytes 24584 | tf_op jit(solution)/shard_map/ppermute | solution.py:704
  123.3 3.7 %collective-permute-start.5 = (f32[16,128]{1,0:T(8,128)S(1)}, f32[16,128]{1,0:T(8,128)S(1)}, u32[]{:S(2)}, u32[]{:S(2)}) collective-permute-start(f32[16,128]{1,0:T(8,128)S(1)} %fusion.1), channel_id=1, source_target_pairs={{0,32},{8,40},{16,48},{24,56},{32,0},{40,8},{48,16},{56,24},{64,96... | collective-permute-start | bytes 24584 | tf_op jit(solution)/shard_map/ppermute | solution.py:704
  127.0 4.9 %collective-permute-start.6 = (f32[16,128]{1,0:T(8,128)S(1)}, f32[16,128]{1,0:T(8,128)S(1)}, u32[]{:S(2)}, u32[]{:S(2)}) collective-permute-start(f32[16,128]{1,0:T(8,128)S(1)} %add.26), channel_id=1, source_target_pairs={{0,96},{8,104},{16,112},{24,120},{32,64},{40,72},{48,80},{56,88},{... | collective-permute-start | bytes 24584 | tf_op jit(solution)/shard_map/ppermute | solution.py:704
